TPU v7x, 256 devices: a whole 4x4x8 slice. The times are simulated.
256 devices in a mesh: px: 8 (over y, core), py: 32 (over z, x).
Axes of the slice: x: 4, y: 4, z: 8, core: 2. Of those that a mesh axis runs over, the one named last changes fastest.
Arguments:
- white_noise: float32 [512, 512, 512], P(('px', 'py')), may hold values from -6 to 6
- mode_amplitude: bfloat16 [512, 512, 512], P(('px', 'py')), may hold values from 0.099609375 to 0.59765625
- kick_noise: bfloat16 [512, 512, 512], P(('px', 'py')), may hold values from -6 to 6
- shell_owner: int32 [8, 32, 4096], P('px', 'py'), may hold values from 0 to 31, as said below
- galaxy_counts: int32 [8, 32, 32, 256, 128], P('px', 'py'), may hold values from 0 to 7
- shell_bias: float32 [8, 32], replicated, may hold values from 1 to 2
- shell_density: float32 [8, 32], replicated, may hold values from 2 to 4
- accepted: int32 [64], replicated, may hold values from 0 to 1
Outputs:
- log_gradient: float32 [512, 512, 512], P(('px', 'py'))
- next_state: float32 [512, 512, 512], P(('px', 'py'))
Inputs may be any that keep to these rules, and one draw needn't show every extreme that they name: `shell_owner`: in every row a, one owner receives exactly 256 blocks from every device (a, b); each device's other blocks are spread over the other 31 owners of its row with loads that differ by at most one; so no device assigns more than 256 blocks to one owner.
All inputs are finite; a program needn't handle non-finite values.
Results may differ from a plain program's by a relative error of at most 0.0003.
Values sent between devices are 32-bit elements; how exact they have to be, the bound alone decides.
No kernel may reach another device: no remote copies, remote signals or barrier semaphores. Data moves between devices by JAX's collectives and lax.ppermute only.
A program may use at most 128 MiB of HBM per device.

v0:
```python
import math

import jax
import jax.numpy as jnp
from jax import lax
from jax.sharding import PartitionSpec as P

BLOCK = 128


HIGHEST = lax.Precision.HIGHEST


def hartley_table(rows_in, cols_in, order):
    angle_index = rows_in[:, None] * cols_in[None, :] % order
    angle = angle_index.astype(jnp.float32) * (2.0 * math.pi / order)
    return jnp.cos(angle) + jnp.sin(angle)


def adapted_step(accepted):
    powers = jnp.power(
        jnp.float32(0.9), jnp.arange(accepted.shape[0], dtype=jnp.int32).astype(jnp.float32)
    )
    accept_rate = jnp.float32(0.1) * jnp.sum(accepted.astype(jnp.float32) * powers)
    return jnp.float32(0.02) * jnp.exp(jnp.float32(2.0) * (accept_rate - jnp.float32(0.574)))


def body(
    white_noise,
    mode_amplitude,
    kick_noise,
    shell_owner,
    galaxy_counts,
    shell_bias,
    shell_density,
    accepted,
):
    depth_local, size_x, size_y = white_noise.shape
    rows_px = lax.axis_size("px")
    rows_py = lax.axis_size("py")
    size_z = depth_local * rows_px * rows_py
    row_index = lax.axis_index("px")
    col_index = lax.axis_index("py")
    span_x = jnp.arange(size_x, dtype=jnp.int32)
    span_y = jnp.arange(size_y, dtype=jnp.int32)
    span_z = jnp.arange(size_z, dtype=jnp.int32)
    table_x = hartley_table(span_x, span_x, size_x)
    table_y = hartley_table(span_y, span_y, size_y)
    table_z = hartley_table(span_z, span_z, size_z)
    scale_x = 1.0 / math.sqrt(size_x)
    scale_y = 1.0 / math.sqrt(size_y)
    scale_z = 1.0 / math.sqrt(size_z)
    freq_here = (row_index * rows_py + col_index) * depth_local + jnp.arange(
        depth_local, dtype=jnp.int32
    )
    anchor = (
        (freq_here[:, None, None] == 0)
        & (span_x[None, :, None] == 0)
        & (span_y[None, None, :] == 0)
    )
    amplitude_live = jnp.where(anchor, jnp.float32(0.0), mode_amplitude.astype(jnp.float32))
    weighted = amplitude_live * white_noise
    first_pass = jnp.einsum("zxk,ky->zxy", weighted, table_y, precision=HIGHEST) * scale_y
    second_pass = jnp.einsum("zky,kx->zxy", first_pass, table_x, precision=HIGHEST) * scale_x
    cell_layout = lax.all_to_all(
        lax.all_to_all(second_pass, "px", split_axis=1, concat_axis=0, tiled=True),
        "py",
        split_axis=2,
        concat_axis=0,
        tiled=True,
    )
    outer_part = span_z // (rows_px * depth_local)
    inner_part = span_z % (rows_px * depth_local)
    freq_order = (
        inner_part // depth_local * (rows_py * depth_local)
        + outer_part * depth_local
        + inner_part % depth_local
    )
    table_mixed = hartley_table(freq_order, span_z, size_z)
    contrast = jnp.einsum("qxy,qz->xyz", cell_layout, table_mixed, precision=HIGHEST) * scale_z
    blocks = contrast.reshape(-1, BLOCK)
    owner_list = shell_owner.reshape(-1)
    peers = jnp.arange(rows_py, dtype=jnp.int32)
    onehot = (owner_list[:, None] == peers[None, :]).astype(jnp.int32)
    rank_index = jnp.sum(jnp.cumsum(onehot, axis=0) * onehot, axis=1) - 1
    capacity = galaxy_counts.shape[3]
    slot_index = owner_list * capacity + rank_index
    outgoing = jnp.zeros((rows_py * capacity, BLOCK), jnp.float32).at[slot_index].set(blocks)
    outgoing = outgoing.reshape(rows_py, capacity, BLOCK)
    arrived = lax.all_to_all(outgoing, "py", split_axis=0, concat_axis=0, tiled=True)
    own_bias = shell_bias[row_index, col_index]
    own_density = shell_density[row_index, col_index]
    galaxy = galaxy_counts[0, 0].astype(jnp.float32)
    owner_grad = own_bias * (galaxy - own_density * jnp.exp(own_bias * arrived))
    returned = lax.all_to_all(owner_grad, "py", split_axis=0, concat_axis=0, tiled=True)
    like_grad = returned.reshape(-1, BLOCK)[slot_index]
    like_grid = like_grad.reshape(contrast.shape)
    back_z = jnp.einsum("xyz,zk->kxy", like_grid, table_z, precision=HIGHEST) * scale_z
    mode_layout = lax.all_to_all(
        lax.all_to_all(back_z, "px", split_axis=0, concat_axis=1, tiled=True),
        "py",
        split_axis=0,
        concat_axis=2,
        tiled=True,
    )
    back_x = jnp.einsum("kxy,xq->kqy", mode_layout, table_x, precision=HIGHEST) * scale_x
    back_y = jnp.einsum("kqy,yp->kqp", back_x, table_y, precision=HIGHEST) * scale_y
    log_gradient = amplitude_live * back_y - white_noise
    step_size = adapted_step(accepted)
    next_state = (
        white_noise
        + step_size * log_gradient
        + jnp.sqrt(2.0 * step_size) * kick_noise.astype(jnp.float32)
    )
    return (log_gradient, next_state)


def solution(mesh):
    return jax.shard_map(
        body,
        mesh=mesh,
        in_specs=(
            P(("px", "py"), None, None),
            P(("px", "py"), None, None),
            P(("px", "py"), None, None),
            P("px", "py", None),
            P("px", "py", None, None, None),
            P(),
            P(),
            P(),
        ),
        out_specs=(P(("px", "py"), None, None), P(("px", "py"), None, None)),
        check_vma=False,
    )
```

profile of v0, /device:TPU:1, one launch (start us, length us, event | category | flops | bytes accessed | tf_op | source)
XLA Modules:
  0.0 539.8 jit_solution(12392985362593773181)
XLA Ops:
  0.7 9.8 %fusion.8 = f32[2,512,512]{2,1,0:T(8,128)S(1)} fusion(f32[2,512,512]{2,1,0:T(8,128)} %param.8, bf16[2,512,512]{2,1,0:T(8,128)(2,1)} %param.9, pred[512]{0:T(512)(128)(4,1)S(1)} %iota_compare_fusion.2, pred[2,512]{1,0:T(4,128)(4,1)S(1)} %broadcast_and_fusion), kind=kOutput, calls=%fused_computation.15 | convolution fusion | flops 3227254784 | bytes 5244416 | tf_op jit(solution)/shard_map/zxk,ky->zxy/dot_general | solution.py:63
  10.6 8.1 %multiply_bitcast_fusion = f32[2,512,512]{2,1,0:T(8,128)S(1)} fusion(f32[2,512,512]{2,1,0:T(8,128)S(1)} %fusion.8), kind=kOutput, calls=%fused_computation.12 | convolution fusion | flops 3226206208 | bytes 4194304 | tf_op jit(solution)/shard_map/zky,kx->zxy/dot_general | solution.py:64
  20.3 32.2 %all_to_all.82 = f32[2,512,512]{2,0,1:T(2,128)S(1)} all-to-all(f32[2,512,512]{2,0,1:T(2,128)S(1)} %copy.33), channel_id=1, replica_groups=mesh['px'=8,'py'=32] {'px'}, dimensions={1} | all-to-all | bytes 4194304 | tf_op jit(solution)/shard_map/all_to_all | solution.py:66
  62.4 11.3 %all-to-all-start.1 = ((f32[32,1,16384]{2,1,0:T(1,128)}), f32[32,1,16384]{2,1,0:T(1,128)S(1)}, u32[]{:S(2)}, u32[]{:S(2)}) async-start(f32[32,1,16384]{2,1,0:T(1,128)} %reshape.194), calls=%async_computation.1 | async-start | bytes 4194304 | tf_op jit(solution)/shard_map/all_to_all | solution.py:65
  73.8 9.2 %reduce-window.6 = s32[32,32,128]{2,1,0:T(8,128)S(1)} reduce-window(s32[32,32,128]{2,1,0:T(8,128)S(1)} %fusion.57, s32[]{:T(128)} %constant.106.clone.1), window={size=1x1x128 pad=0_0x0_0x127_0}, to_apply=%region_0.1 | reduce-window | flops 16646144 | bytes 1048580 | tf_op jit(solution)/shard_map/reduce-window
  84.7 37.2 %all-to-all-done.1 = f32[32,1,16384]{2,1,0:T(1,128)S(1)} async-done(((f32[32,1,16384]{2,1,0:T(1,128)}), f32[32,1,16384]{2,1,0:T(1,128)S(1)}, u32[]{:S(2)}, u32[]{:S(2)}) %all-to-all-start.1) | async-done | bytes 2097184 | tf_op jit(solution)/shard_map/all_to_all | solution.py:65
  123.7 7.4 %reduce.2 = f32[32,16384]{1,0:T(8,128)S(1)} reduce(f32[32,1,16384]{2,1,0:T(1,128)} %copy-done, f32[]{:T(128)} %broadcast.312), dimensions={1}, to_apply=%all_to_all.62.reduce_sub_computation | reduce | bytes 4194308 | tf_op jit(solution)/shard_map/all_to_all | solution.py:65
  144.0 9.0 %convolution_multiply_fusion = f32[64,16,512]{2,1,0:T(8,128)} fusion(f32[512,64,16]{0,2,1:T(8,128)S(1)} %copy.39, s32[512]{0:T(512)S(1)} %fusion.64), kind=kOutput, calls=%fused_computation.22 | convolution fusion | flops 3225681920 | bytes 4196352 | tf_op jit(solution)/shard_map/qxy,qz->xyz/dot_general | solution.py:80
  154.6 12.8 %scatter_custom_fusion = f32[8192,128]{1,0:T(8,128)} fusion(s32[4096]{0:T(1024)S(1)} %bitcast.98, f32[4096,128]{1,0:T(8,128)S(1)} %reshape.183, f32[]{:T(128)} %constant.107.clone.1), kind=kCustom, calls=%fused_computation.17 | custom fusion | bytes 4194308 | tf_op jit(solution)/shard_map/scatter | solution.py:88
  167.4 6.6 %all-to-all-start.2 = ((f32[32,256,128]{2,1,0:T(8,128)}), f32[32,256,128]{2,1,0:T(8,128)}, u32[]{:S(2)}, u32[]{:S(2)}) async-start(f32[32,256,128]{2,1,0:T(8,128)} %bitcast.85), calls=%async_computation.2 | async-start | bytes 8388608 | tf_op jit(solution)/shard_map/all_to_all | solution.py:90
  176.5 90.2 %all-to-all-done.2 = f32[32,256,128]{2,1,0:T(8,128)} async-done(((f32[32,256,128]{2,1,0:T(8,128)}), f32[32,256,128]{2,1,0:T(8,128)}, u32[]{:S(2)}, u32[]{:S(2)}) %all-to-all-start.2) | async-done | bytes 4194336 | tf_op jit(solution)/shard_map/all_to_all | solution.py:90
  266.7 7.8 %fusion = f32[32,256,128]{2,1,0:T(8,128)} fusion(f32[32,256,128]{2,1,0:T(8,128)} %all-to-all-done.2, s32[1,1,32,256,128]{4,3,2,1,0:T(8,128)} %param.12, f32[]{:T(128)} %bitcast.4, f32[]{:T(128)} %bitcast.2), kind=kLoop, calls=%fused_computation.3 | loop fusion | flops 5242880 | bytes 12582920 | tf_op jit(solution)/shard_map/mul | solution.py:94
  274.5 7.0 %all-to-all-start.3 = ((f32[32,256,128]{2,1,0:T(8,128)}), f32[32,256,128]{2,1,0:T(8,128)}, u32[]{:S(2)}, u32[]{:S(2)}) async-start(f32[32,256,128]{2,1,0:T(8,128)} %fusion), calls=%async_computation.3 | async-start | bytes 8388608 | tf_op jit(solution)/shard_map/all_to_all | solution.py:95
  281.6 92.3 %all-to-all-done.3 = f32[32,256,128]{2,1,0:T(8,128)} async-done(((f32[32,256,128]{2,1,0:T(8,128)}), f32[32,256,128]{2,1,0:T(8,128)}, u32[]{:S(2)}, u32[]{:S(2)}) %all-to-all-start.3) | async-done | bytes 4194336 | tf_op jit(solution)/shard_map/all_to_all | solution.py:95
  373.9 13.0 %gather_fusion = f32[4096,128]{1,0:T(8,128)S(1)} fusion(f32[8192,128]{1,0:T(8,128)} %bitcast.22, s32[4096]{0:T(1024)S(1)} %broadcast_clamp_fusion), kind=kCustom, calls=%fused_computation | custom fusion | bytes 4210688 | tf_op jit(solution)/shard_map/gather | solution.py:96
  388.3 9.8 %fusion.15 = f32[512,64,16]{0,1,2:T(8,128)S(1)} fusion(f32[64,16,512]{2,1,0:T(8,128)} %reshape.170), kind=kOutput, calls=%fused_computation.21 | convolution fusion | flops 3225681920 | bytes 4194304 | tf_op jit(solution)/shard_map/xyz,zk->kxy/dot_general | solution.py:98
  401.9 5.9 %reshape.196 = f32[8,1,65536]{2,1,0:T(1,128)S(1)} reshape(f32[512,16,64]{2,1,0:T(8,128)} %bitcast.84) | data formatting | bytes 4194304
  407.9 32.9 %all_to_all.83 = f32[8,1,65536]{2,1,0:T(1,128)} all-to-all(f32[8,1,65536]{2,1,0:T(1,128)S(1)} %reshape.196), channel_id=1, replica_groups=mesh['px'=8,'py'=32] {'px'}, dimensions={0} | all-to-all | bytes 4194304 | tf_op jit(solution)/shard_map/all_to_all | solution.py:100
  440.8 7.2 %reduce.3 = f32[8,65536]{1,0:T(8,128)S(1)} reduce(f32[8,1,65536]{2,1,0:T(1,128)} %all_to_all.83, f32[]{:T(128)} %broadcast.312), dimensions={1}, to_apply=%all_to_all.68.reduce_sub_computation | reduce | bytes 4194308 | tf_op jit(solution)/shard_map/all_to_all | solution.py:100
  451.6 6.6 %copy.59 = f32[8,64,64,16]{2,0,3,1:T(8,128)} copy(f32[8,64,64,16]{2,3,1,0:T(8,128)} %bitcast.88) | data formatting | bytes 4194304 | tf_op jit(solution)/shard_map/all_to_all | solution.py:100
  463.0 6.9 %all-to-all-start.5 = ((f32[64,512,16]{1,2,0:T(8,128)}), f32[64,512,16]{1,2,0:T(8,128)S(1)}, u32[]{:S(2)}, u32[]{:S(2)}) async-start(f32[64,512,16]{1,2,0:T(8,128)} %all_to_all.71), calls=%async_computation.5 | async-start | bytes 4194304 | tf_op jit(solution)/shard_map/all_to_all | solution.py:99
  471.2 46.6 %all-to-all-done.5 = f32[64,512,16]{1,2,0:T(8,128)S(1)} async-done(((f32[64,512,16]{1,2,0:T(8,128)}), f32[64,512,16]{1,2,0:T(8,128)S(1)}, u32[]{:S(2)}, u32[]{:S(2)}) %all-to-all-start.5) | async-done | bytes 2097184 | tf_op jit(solution)/shard_map/all_to_all | solution.py:99
  518.0 10.8 %fusion.31 = f32[512,2,512]{2,0,1:T(8,128)S(1)} fusion(f32[2,512,512]{1,2,0:T(8,128)S(1)} %bitcast.93), kind=kOutput, calls=%fused_computation.40 | convolution fusion | flops 3225157632 | bytes 4194304 | tf_op jit(solution)/shard_map/kxy,xq->kqy/dot_general | solution.py:106
  528.8 10.6 %multiply_add_fusion = (f32[2,512,512]{2,1,0:T(8,128)}, f32[2,512,512]{2,1,0:T(8,128)}) fusion(bf16[2,512,512]{2,1,0:T(8,128)(2,1)S(1)} %copy-done.3, f32[2,512,512]{2,1,0:T(8,128)S(1)} %copy-done.2, f32[]{:T(128)S(6)} %sqrt.3, f32[]{:T(128)S(6)} %mul_shard_map.7, f32[512,2,512]{2,0,1:T(8,128)S(1)} %fusion.31, bf16[2,512,512]{2,1,0:T(8,128)(2,1)S(1)} %copy-done.4, ...), kind=kOutput, calls=%fused_computation.9 | convolution fusion | flops 3231449088 | bytes 10487304 | tf_op jit(solution)/shard_map/kqy,yp->kqp/dot_general | solution.py:107
  (42 shorter events, 46.4 us)
Async XLA Ops:
  62.4 11.3 %copy-start.1 = (s32[1,1,4096]{2,1,0:T(1,128)S(1)}, s32[1,1,4096]{2,1,0:T(1,128)}, u32[]{:S(2)}) copy-start(s32[1,1,4096]{2,1,0:T(1,128)} %param.11) | copy-start | bytes 49156
  62.4 59.5 %all-to-all-start.1 = ((f32[32,1,16384]{2,1,0:T(1,128)}), f32[32,1,16384]{2,1,0:T(1,128)S(1)}, u32[]{:S(2)}, u32[]{:S(2)}) async-start(f32[32,1,16384]{2,1,0:T(1,128)} %reshape.194), calls=%async_computation.1 | async-start | bytes 4194304 | tf_op jit(solution)/shard_map/all_to_all | solution.py:65
  121.9 1.3 copy-start
  167.4 99.3 %all-to-all-start.2 = ((f32[32,256,128]{2,1,0:T(8,128)}), f32[32,256,128]{2,1,0:T(8,128)}, u32[]{:S(2)}, u32[]{:S(2)}) async-start(f32[32,256,128]{2,1,0:T(8,128)} %bitcast.85), calls=%async_computation.2 | async-start | bytes 8388608 | tf_op jit(solution)/shard_map/all_to_all | solution.py:90
  274.5 99.3 %all-to-all-start.3 = ((f32[32,256,128]{2,1,0:T(8,128)}), f32[32,256,128]{2,1,0:T(8,128)}, u32[]{:S(2)}, u32[]{:S(2)}) async-start(f32[32,256,128]{2,1,0:T(8,128)} %fusion), calls=%async_computation.3 | async-start | bytes 8388608 | tf_op jit(solution)/shard_map/all_to_all | solution.py:95
  463.0 6.9 %copy-start.5 = (s32[64]{0:T(128)S(1)}, s32[64]{0:T(128)}, u32[]{:S(2)}) copy-start(s32[64]{0:T(128)} %param.15) | copy-start | bytes 772
  463.0 54.8 %all-to-all-start.5 = ((f32[64,512,16]{1,2,0:T(8,128)}), f32[64,512,16]{1,2,0:T(8,128)S(1)}, u32[]{:S(2)}, u32[]{:S(2)}) async-start(f32[64,512,16]{1,2,0:T(8,128)} %all_to_all.71), calls=%async_computation.5 | async-start | bytes 4194304 | tf_op jit(solution)/shard_map/all_to_all | solution.py:99
  518.0 10.8 %copy-start.2 = (f32[2,512,512]{2,1,0:T(8,128)S(1)}, f32[2,512,512]{2,1,0:T(8,128)}, u32[]{:S(2)}) copy-start(f32[2,512,512]{2,1,0:T(8,128)} %param.8) | copy-start | bytes 6291460
  518.0 10.8 %copy-start.3 = (bf16[2,512,512]{2,1,0:T(8,128)(2,1)S(1)}, bf16[2,512,512]{2,1,0:T(8,128)(2,1)}, u32[]{:S(2)}) copy-start(bf16[2,512,512]{2,1,0:T(8,128)(2,1)} %param.10) | copy-start | bytes 3145732
  518.0 10.8 %copy-start.4 = (bf16[2,512,512]{2,1,0:T(8,128)(2,1)S(1)}, bf16[2,512,512]{2,1,0:T(8,128)(2,1)}, u32[]{:S(2)}) copy-start(bf16[2,512,512]{2,1,0:T(8,128)(2,1)} %param.9) | copy-start | bytes 3145732
where the time goes:
time: 551 us; the launch traced here: 540 us
  waiting for transfers between devices  266 us (48%)
  local copies, waits for them, and re-layouts  83.1 us (15%)
  blocking collectives  65.1 us (12%)
  matrix products  58.2 us (11%)
  other arithmetic  33.2 us (6%)
  starting transfers between devices  31.8 us (6%)
    all_to_all x1, waiting for transfers between devices, body(): lax.all_to_all(owner_grad, 'py', split_axis=0, concat_axis=0, tiled=True)  92.3 us
    all_to_all x1, waiting for transfers between devices, body(): lax.all_to_all(outgoing, 'py', split_axis=0, concat_axis=0, tiled=True)  90.2 us
    all_to_all x1, waiting for transfers between devices, body(): lax.all_to_all(lax.all_to_all(back_z, 'px', split_axis=0, concat_axis=1,...  46.6 us
    all_to_all x1, waiting for transfers between devices, body(): lax.all_to_all(lax.all_to_all(second_pass, 'px', split_axis=1, concat_axi...  37.2 us
    all_to_all x1, blocking collectives, body(): lax.all_to_all(back_z, 'px', split_axis=0, concat_axis=1, tiled=True)  32.9 us
    all_to_all x1, blocking collectives, body(): lax.all_to_all(second_pass, 'px', split_axis=1, concat_axis=0, tiled=True)  32.2 us
    unnamed x16, local copies, waits for them, and re-layouts  19.3 us
    gather x1, local copies, waits for them, and re-layouts, body(): like_grad = returned.reshape(-1, BLOCK)[slot_index]  13 us
  transfers between devices with their start and end apart: 4, of which 4 were waited for; matrix products, arithmetic and copies ran while one was open for 3% of the time, Pallas kernels for 0%

commit v1 on v0

v1 whole, which is shorter than its diff:
```python
import math

import jax
import jax.numpy as jnp
import numpy as np
from jax import lax
from jax.experimental import pallas as pl
from jax.experimental.pallas import tpu as pltpu
from jax.sharding import PartitionSpec as P

BLOCK = 128
HALF = BLOCK // 2
VMEM_BYTES = 56 * 1024 * 1024


def scaled_table(rows, cols, order):
    angle = (rows[:, None] * cols[None, :] % order).astype(np.float64) * (2.0 * math.pi / order)
    table = ((np.cos(angle) + np.sin(angle)) / math.sqrt(order)).astype(np.float32)
    high = table.astype(jnp.bfloat16)
    low = (table - high.astype(np.float32)).astype(jnp.bfloat16)
    return high, low


def split(value):
    high = value.astype(jnp.bfloat16)
    low = (value - high.astype(jnp.float32)).astype(jnp.bfloat16)
    return high, low


def product(left, right, contract=((1,), (0,))):
    left_high, left_low = left
    right_high, right_low = right
    dot = lambda a, b: lax.dot_general(a, b, (contract, ((), ())), preferred_element_type=jnp.float32)
    return dot(left_high, right_high) + (dot(left_high, right_low) + dot(left_low, right_high))


def first_half(shape):
    return lax.broadcasted_iota(jnp.int32, shape, len(shape) - 1) % BLOCK < HALF


def live_amplitude(first_ref, amplitude_ref):
    amplitude = amplitude_ref[0].astype(jnp.float32)
    rows = lax.broadcasted_iota(jnp.int32, amplitude.shape, 0)
    cols = lax.broadcasted_iota(jnp.int32, amplitude.shape, 1)
    anchor = (rows + cols + first_ref[0] + pl.program_id(0)) == 0
    return jnp.where(anchor, 0.0, amplitude)


def synthesis_kernel(
    first_ref, white_ref, amplitude_ref, y_high, y_low, even_high, even_low, odd_high, odd_low, out_ref
):
    weighted = split(live_amplitude(first_ref, amplitude_ref) * white_ref[0])
    passed = product((y_high[...], y_low[...]), weighted, ((1,), (1,)))
    rows = passed.shape[0] // 2
    lower = product(split(passed[:rows]), (even_high[...], even_low[...]))
    upper = product(split(passed[rows:]), (odd_high[...], odd_low[...]))
    groups = out_ref.shape[1]
    for pair in range(out_ref.shape[0] // 2):
        left = lower[:, pair * BLOCK : (pair + 1) * BLOCK]
        right = upper[:, pair * BLOCK : (pair + 1) * BLOCK]
        mask = first_half(left.shape)
        out_ref[2 * pair, :, 0] = jnp.where(mask, left, right).reshape(groups, -1, BLOCK)
        out_ref[2 * pair + 1, :, 0] = jnp.where(mask, right, left).reshape(groups, -1, BLOCK)


def shell_kernel(field_ref, galaxy_ref, bias_ref, density_ref, z_high, z_low, out_ref):
    table = (z_high[...], z_low[...])
    size_z = z_high.shape[0]
    rows_y = field_ref.shape[0] // size_z
    for step in range(rows_y // 2):
        field = jnp.concatenate(
            [field_ref[pl.ds(2 * step + k, size_z, stride=rows_y), :] for k in range(2)], axis=1
        )
        contrast = product(table, split(field))
        span = slice(2 * step * BLOCK, 2 * (step + 1) * BLOCK)
        grads = []
        for quarter in range(size_z // BLOCK):
            depth = slice(quarter * BLOCK, (quarter + 1) * BLOCK)
            bias = bias_ref[quarter : quarter + 1, span]
            density = density_ref[quarter : quarter + 1, span]
            grads.append(bias * (galaxy_ref[depth, span] - density * jnp.exp(bias * contrast[depth])))
        back = product(table, split(jnp.concatenate(grads, axis=0)))
        for k in range(2):
            out_ref[pl.ds(2 * step + k, size_z, stride=rows_y), :] = back[:, k * BLOCK : (k + 1) * BLOCK]


def analysis_kernel(
    first_ref, step_ref, field_ref, white_ref, amplitude_ref, kick_ref,
    y_high, y_low, even_high, even_low, odd_high, odd_low, grad_ref, next_ref,
):
    lower, upper = [], []
    for pair in range(field_ref.shape[0] // 2):
        left = field_ref[2 * pair, :, 0].reshape(-1, BLOCK)
        right = field_ref[2 * pair + 1, :, 0].reshape(-1, BLOCK)
        mask = first_half(left.shape)
        lower.append(jnp.where(mask, left, right))
        upper.append(jnp.where(mask, right, left))
    contract = ((1,), (1,))
    lower = product(split(jnp.concatenate(lower, axis=1)), (even_high[...], even_low[...]), contract)
    upper = product(split(jnp.concatenate(upper, axis=1)), (odd_high[...], odd_low[...]), contract)
    passed = split(jnp.concatenate([lower, upper], axis=0))
    back = product(passed, (y_high[...], y_low[...]), ((0,), (0,)))
    white = white_ref[0]
    gradient = live_amplitude(first_ref, amplitude_ref) * back - white
    grad_ref[0] = gradient
    next_ref[0] = white + step_ref[0] * gradient + step_ref[1] * kick_ref[0].astype(jnp.float32)


def adapted_step(accepted):
    powers = jnp.power(
        jnp.float32(0.9), jnp.arange(accepted.shape[0], dtype=jnp.int32).astype(jnp.float32)
    )
    accept_rate = jnp.float32(0.1) * jnp.sum(accepted.astype(jnp.float32) * powers)
    return jnp.float32(0.02) * jnp.exp(jnp.float32(2.0) * (accept_rate - jnp.float32(0.574)))


def solution(mesh):
    rows_px, rows_py = mesh.shape["px"], mesh.shape["py"]
    devices = rows_px * rows_py

    def body(
        white_noise, mode_amplitude, kick_noise, shell_owner, galaxy_counts, shell_bias, shell_density, accepted
    ):
        depth, size_x, size_y = white_noise.shape
        size_z = depth * devices
        span_x, span_y = size_x // rows_px, size_y // rows_py
        rows_y = span_y // 2
        quarters = size_z // BLOCK
        row_index = lax.axis_index("px")
        col_index = lax.axis_index("py")
        first = ((row_index * rows_py + col_index) * depth).reshape(1)

        plain_x, plain_y, plain_z = np.arange(size_x), np.arange(size_y), np.arange(size_z)
        y_order = plain_y.reshape(rows_py, 2, rows_y).transpose(1, 0, 2).reshape(-1)
        x_order = plain_x.reshape(-1, 2, HALF)[:, ::-1].reshape(-1)
        y_table = scaled_table(y_order, plain_y, size_y)
        even_table = scaled_table(plain_x, plain_x, size_x)
        odd_table = scaled_table(plain_x, x_order, size_x)
        z_table = scaled_table(plain_z, plain_z, size_z)
        tables = [jnp.asarray(part) for part in (*y_table, *even_table, *odd_table)]

        capacity = galaxy_counts.shape[3]
        counts = lax.all_to_all(galaxy_counts[0, 0], "py", split_axis=0, concat_axis=0, tiled=True)

        owner_list = shell_owner.reshape(-1)
        peers = jnp.arange(rows_py, dtype=jnp.int32)
        onehot = owner_list[:, None] == peers[None, :]
        onehot_int = onehot.astype(jnp.int32)
        rank_index = jnp.sum(jnp.cumsum(onehot_int, axis=0) * onehot_int, axis=1) - 1
        slot_index = owner_list * capacity + rank_index
        bias_row = lax.dynamic_index_in_dim(shell_bias, row_index, 0, keepdims=False)
        density_row = lax.dynamic_index_in_dim(shell_density, row_index, 0, keepdims=False)

        def by_column(blocks):
            grid = blocks.reshape(span_x, 2, rows_y, quarters)
            grid = jnp.where(row_index % 2 == 0, grid, grid[:, ::-1])
            return grid.transpose(3, 2, 1, 0).reshape(quarters, -1)

        slot_grid = by_column(slot_index)
        owner_grid = by_column(owner_list)
        hit = owner_grid[:, :, None] == peers
        bias_grid = jnp.sum(jnp.where(hit, bias_row, 0.0), axis=-1)
        density_grid = jnp.sum(jnp.where(hit, density_row, 0.0), axis=-1)

        whole = lambda array: pl.BlockSpec(array.shape, lambda i: (0,) * array.ndim)
        plane = pl.BlockSpec((1, size_x, size_y), lambda i: (i, 0, 0))
        scalar = pl.BlockSpec(memory_space=pltpu.SMEM)
        packed_shape = (rows_px, rows_py, depth, rows_y, BLOCK)
        packed = pl.BlockSpec((rows_px, rows_py, 1, rows_y, BLOCK), lambda i: (0, 0, i, 0, 0))
        params = pltpu.CompilerParams(vmem_limit_bytes=VMEM_BYTES)

        flops = 2 * 3 * 2 * depth * size_x * size_y * size_x
        sent = pl.pallas_call(
            synthesis_kernel,
            grid=(depth,),
            in_specs=[scalar, plane, plane] + [whole(table) for table in tables],
            out_specs=packed,
            out_shape=jax.ShapeDtypeStruct(packed_shape, jnp.float32),
            compiler_params=params,
            cost_estimate=pl.CostEstimate(flops=flops, bytes_accessed=8 * 2**20, transcendentals=0),
            name="synthesis",
        )(first, white_noise, mode_amplitude, *tables)

        chunk = depth * rows_y
        field = lax.all_to_all(
            sent.reshape(devices, chunk, BLOCK), ("px", "py"), split_axis=0, concat_axis=0, tiled=True
        )

        picked = counts.reshape(-1, BLOCK).at[slot_grid.reshape(-1)].get(mode="promise_in_bounds")
        galaxy = picked.reshape(quarters, -1, BLOCK).transpose(0, 2, 1).reshape(size_z, -1).astype(jnp.float32)

        back = pl.pallas_call(
            shell_kernel,
            out_shape=jax.ShapeDtypeStruct((size_z * rows_y, BLOCK), jnp.float32),
            compiler_params=params,
            cost_estimate=pl.CostEstimate(flops=flops, bytes_accessed=8 * 2**20, transcendentals=size_z * 1024),
            name="shell_gradient",
        )(field.reshape(-1, BLOCK), galaxy, bias_grid, density_grid, *[jnp.asarray(part) for part in z_table])

        returned = lax.all_to_all(
            back.reshape(devices, chunk, BLOCK), ("px", "py"), split_axis=0, concat_axis=0, tiled=True
        )
        step_size = adapted_step(accepted)
        steps = jnp.stack([step_size, jnp.sqrt(2.0 * step_size)])
        out_plane = jax.ShapeDtypeStruct(white_noise.shape, jnp.float32)
        return pl.pallas_call(
            analysis_kernel,
            grid=(depth,),
            in_specs=[scalar, scalar, packed, plane, plane, plane] + [whole(table) for table in tables],
            out_specs=(plane, plane),
            out_shape=(out_plane, out_plane),
            compiler_params=params,
            cost_estimate=pl.CostEstimate(flops=flops, bytes_accessed=12 * 2**20, transcendentals=0),
            name="analysis",
        )(first, steps, returned.reshape(packed_shape), white_noise, mode_amplitude, kick_noise, *tables)

    modes = P(("px", "py"), None, None)
    return jax.shard_map(
        body,
        mesh=mesh,
        in_specs=(modes, modes, modes, P("px", "py", None), P("px", "py", None, None, None), P(), P(), P()),
        out_specs=(modes, modes),
        check_vma=False,
    )
```

time: 551 us -> 250 us (0.45); the launches traced: 540 us -> 249 us
  waiting for transfers between devices: 266 us -> 155 us
  blocking collectives: 65.1 us -> 0 us
  local copies, waits for them, and re-layouts: 83.1 us -> 23.4 us
  matrix products: 58.2 us -> 0 us
  Pallas kernels: 0 us -> 24.3 us
  other arithmetic: 33.2 us -> 14.6 us
    all_to_all x4 -> x3, waiting for transfers between devices: 266 us -> 155 us  [the longest x1 85.8 us: body(): lax.all_to_all(galaxy_counts[0, 0], 'py', split_axis=0, concat_axis=0, ti...]
    all_to_all x2 -> x0, blocking collectives: 65.1 us -> none  [the longest x1 32.9 us: body(): lax.all_to_all(back_z, 'px', split_axis=0, concat_axis=1, tiled=True)]
    dot_general x6 -> x0, matrix products: 58.2 us -> none  [the longest x1 10.8 us: body(): jnp.einsum('kxy,xq->kqy', mode_layout, table_x, precision=HIGHEST) * scale_x]
    all_to_all x9 -> x0, local copies, waits for them, and re-layouts: 26.2 us -> none  [the longest x2 11.4 us: body(): lax.all_to_all(back_z, 'px', split_axis=0, concat_axis=1, tiled=True)]
    pallas_call x0 -> x3, Pallas kernels: none -> 24.3 us  [the longest x1 8.79 us: body(): pl.pallas_call(analysis_kernel, grid=(depth,), in_specs=[scalar, scalar,...]
    unnamed x16 -> x7, local copies, waits for them, and re-layouts: 19.3 us -> 1.87 us
    all_to_all x2 -> x0, other arithmetic: 14.6 us -> none  [the longest x1 7.39 us: body(): lax.all_to_all(lax.all_to_all(second_pass, 'px', split_axis=1, concat_axi...]
    scatter x1 -> x0, local copies, waits for them, and re-layouts: 12.8 us -> none  [body(): jnp.zeros((rows_py * capacity, BLOCK), jnp.float32).at[slot_index]]
  transfers between devices with their start and end apart: 4 -> 3, of which waited for: 4 -> 3; matrix products, arithmetic and copies ran while one was open for 3% -> 15% of each run, Pallas kernels for 0% -> 3%
where the time goes in v1:
time: 250 us; the launch traced here: 249 us
  waiting for transfers between devices  155 us (62%)
  starting transfers between devices  30.8 us (12%)
  Pallas kernels  24.3 us (10%)
  local copies, waits for them, and re-layouts  23.4 us (9%)
  other arithmetic  14.6 us (6%)
    all_to_all x1, waiting for transfers between devices, body(): lax.all_to_all(galaxy_counts[0, 0], 'py', split_axis=0, concat_axis=0, ti...  85.8 us
    all_to_all x1, waiting for transfers between devices, body(): lax.all_to_all(back.reshape(devices, chunk, BLOCK), ('px', 'py'), split_a...  51.7 us
    all_to_all x1, waiting for transfers between devices, body(): lax.all_to_all(sent.reshape(devices, chunk, BLOCK), ('px', 'py'), split_a...  17.2 us
    gather x1, local copies, waits for them, and re-layouts, body(): counts.reshape(-1, BLOCK).at[slot_grid.reshape(-1)]  16.4 us
    all_to_all x1, starting transfers between devices, body(): lax.all_to_all(sent.reshape(devices, chunk, BLOCK), ('px', 'py'), split_a...  12.9 us
    all_to_all x1, starting transfers between devices, body(): lax.all_to_all(galaxy_counts[0, 0], 'py', split_axis=0, concat_axis=0, ti...  12 us
    another operation x3, other arithmetic  9.62 us
    pallas_call x1, Pallas kernels, body(): pl.pallas_call(analysis_kernel, grid=(depth,), in_specs=[scalar, scalar,...  8.79 us
  transfers between devices with their start and end apart: 3, of which 3 were waited for; matrix products, arithmetic and copies ran while one was open for 15% of the time, Pallas kernels for 3%

profile of v1, /device:TPU:1, one launch (start us, length us, event | category | flops | bytes accessed | tf_op | source)
XLA Modules:
  0.0 249.2 jit_solution(2071997190695286511)
XLA Ops:
  0.6 12.0 %all-to-all-start.1 = ((s32[32,256,128]{2,1,0:T(8,128)}), s32[32,256,128]{2,1,0:T(8,128)}, u32[]{:S(2)}, u32[]{:S(2)}) async-start(s32[32,256,128]{2,1,0:T(8,128)} %bitcast.39), calls=%async_computation.1 | async-start | bytes 8388608 | tf_op jit(solution)/shard_map/all_to_all | solution.py:143
  12.6 7.2 %synthesis.1 = f32[8,32,2,8,128]{4,3,2,1,0:T(8,128)} custom-call(s32[1]{0:T(128)} %bitcast.first_ref, f32[2,512,512]{2,1,0:T(8,128)} %white_ref.3, bf16[2,512,512]{2,1,0:T(8,128)(2,1)} %amplitude_ref.3, bf16[512,512]{1,0:T(8,128)(2,1)} %constant.73.clone.y_high, bf16[512,512]{1,0:T(8,128)(2,1)} %constant.74.clone.y_low, ...), custom_call_target="tpu_custom_call" | custom-call | flops 3221225472 | bytes 8388608 | tf_op jit(solution)/shard_map/synthesis/pallas_call | solution.py:173
  19.9 85.8 %all-to-all-done.1 = s32[32,256,128]{2,1,0:T(8,128)} async-done(((s32[32,256,128]{2,1,0:T(8,128)}), s32[32,256,128]{2,1,0:T(8,128)}, u32[]{:S(2)}, u32[]{:S(2)}) %all-to-all-start.1) | async-done | bytes 4194336 | tf_op jit(solution)/shard_map/all_to_all | solution.py:143
  105.7 12.9 %all-to-all-start = ((f32[256,16,128]{2,1,0:T(8,128)}), f32[256,16,128]{2,1,0:T(8,128)}, u32[]{:S(2)}, u32[]{:S(2)}) async-start(f32[256,16,128]{2,1,0:T(8,128)} %bitcast.40), calls=%async_computation | async-start | bytes 4194304 | tf_op jit(solution)/shard_map/all_to_all | solution.py:185
  118.6 0.5 broadcast.50
  119.1 0.7 reduce.5
  119.8 0.5 reshape.84
  120.4 9.2 %reduce-window.6 = s32[32,32,128]{2,1,0:T(8,128)S(1)} reduce-window(s32[32,32,128]{2,1,0:T(8,128)S(1)} %fusion.4, s32[]{:T(128)} %constant.67.clone.1), window={size=1x1x128 pad=0_0x0_0x127_0}, to_apply=%region_1.2 | reduce-window | flops 16646144 | bytes 1048580 | tf_op jit(solution)/shard_map/reduce-window
  129.6 0.8 slice_reduce_fusion
  130.8 0.3 fusion.3
  131.2 0.5 sub.11
  132.6 0.7 dynamic-slice_bitcast_fusion
  133.3 0.8 select_reduce_fusion
  134.2 16.4 %gather_fusion = s32[4096,128]{1,0:T(8,128)} fusion(s32[8192,128]{1,0:T(8,128)} %bitcast.6, s32[4096]{0:T(1024)S(1)} %broadcast_clamp_fusion), kind=kCustom, calls=%fused_computation | custom fusion | bytes 4210688 | tf_op jit(solution)/shard_map/gather | solution.py:189
  150.5 1.7 convert_element_type.23
  152.3 1.8 copy.23
  154.1 17.2 %all-to-all-done = f32[256,16,128]{2,1,0:T(8,128)} async-done(((f32[256,16,128]{2,1,0:T(8,128)}), f32[256,16,128]{2,1,0:T(8,128)}, u32[]{:S(2)}, u32[]{:S(2)}) %all-to-all-start) | async-done | bytes 2097184 | tf_op jit(solution)/shard_map/all_to_all | solution.py:185
  171.3 8.2 %shell_gradient.1 = f32[4096,128]{1,0:T(8,128)} custom-call(f32[4096,128]{1,0:T(8,128)} %bitcast.4.field_ref, f32[512,1024]{1,0:T(8,128)} %bitcast.43, f32[4,1024]{1,0:T(4,128)} %get-tuple-element.3.bias_ref, f32[4,1024]{1,0:T(4,128)} %get-tuple-element.2.density_ref, bf16[512,512]{1,0:T(8,128)(2,1)} %constant.75.clone.even_high.z_high, ...), custom_call_target="tpu_custom_call" | custom-call | flops 3221225472 | bytes 8388608 | tf_op jit(solution)/shard_map/shell_gradient/pallas_call | solution.py:192
  179.6 5.9 %all-to-all-start.2 = ((f32[256,16,128]{2,1,0:T(8,128)}), f32[256,16,128]{2,1,0:T(8,128)S(1)}, u32[]{:S(2)}, u32[]{:S(2)}) async-start(f32[256,16,128]{2,1,0:T(8,128)} %bitcast.42), calls=%async_computation.2 | async-start | bytes 4194304 | tf_op jit(solution)/shard_map/all_to_all | solution.py:200
  185.5 0.6 multiply_reduce_fusion
  186.8 0.6 pad_maximum_fusion.step_ref
  187.4 51.7 %all-to-all-done.2 = f32[256,16,128]{2,1,0:T(8,128)S(1)} async-done(((f32[256,16,128]{2,1,0:T(8,128)}), f32[256,16,128]{2,1,0:T(8,128)S(1)}, u32[]{:S(2)}, u32[]{:S(2)}) %all-to-all-start.2) | async-done | bytes 2097184 | tf_op jit(solution)/shard_map/all_to_all | solution.py:200
  239.1 1.3 copy-done
  240.5 8.8 %analysis.1 = (f32[2,512,512]{2,1,0:T(8,128)}, f32[2,512,512]{2,1,0:T(8,128)}) custom-call(s32[1]{0:T(128)} %bitcast.first_ref, f32[2]{0:T(128)} %pad_maximum_fusion.step_ref, f32[8,32,2,8,128]{4,3,2,1,0:T(8,128)} %bitcast.41, f32[2,512,512]{2,1,0:T(8,128)} %white_ref.3, bf16[2,512,512]{2,1,0:T(8,128)(2,1)} %amplitude_ref.3, bf16[2,512,512]{2,1,0:T(8,128)(2,1)} %kick_ref.1, ...), custom_call_target="tpu_custom_call" | custom-call | flops 3221225472 | bytes 12582912 | tf_op jit(solution)/shard_map/analysis/pallas_call | solution.py:206
  (17 shorter events, 1.4 us)
Async XLA Ops:
  0.6 105.0 %all-to-all-start.1 = ((s32[32,256,128]{2,1,0:T(8,128)}), s32[32,256,128]{2,1,0:T(8,128)}, u32[]{:S(2)}, u32[]{:S(2)}) async-start(s32[32,256,128]{2,1,0:T(8,128)} %bitcast.39), calls=%async_computation.1 | async-start | bytes 8388608 | tf_op jit(solution)/shard_map/all_to_all | solution.py:143
  105.7 13.4 %copy-start.1 = (s32[1,1,4096]{2,1,0:T(1,128)S(1)}, s32[1,1,4096]{2,1,0:T(1,128)}, u32[]{:S(2)}) copy-start(s32[1,1,4096]{2,1,0:T(1,128)} %param.19) | copy-start | bytes 49156
  105.7 65.6 %all-to-all-start = ((f32[256,16,128]{2,1,0:T(8,128)}), f32[256,16,128]{2,1,0:T(8,128)}, u32[]{:S(2)}, u32[]{:S(2)}) async-start(f32[256,16,128]{2,1,0:T(8,128)} %bitcast.40), calls=%async_computation | async-start | bytes 4194304 | tf_op jit(solution)/shard_map/all_to_all | solution.py:185
  179.6 5.9 %copy-start.2 = (s32[64]{0:T(128)S(1)}, s32[64]{0:T(128)}, u32[]{:S(2)}) copy-start(s32[64]{0:T(128)} %param.23) | copy-start | bytes 772
  179.6 59.5 %all-to-all-start.2 = ((f32[256,16,128]{2,1,0:T(8,128)}), f32[256,16,128]{2,1,0:T(8,128)S(1)}, u32[]{:S(2)}, u32[]{:S(2)}) async-start(f32[256,16,128]{2,1,0:T(8,128)} %bitcast.42), calls=%async_computation.2 | async-start | bytes 4194304 | tf_op jit(solution)/shard_map/all_to_all | solution.py:200
  239.1 1.4 copy-start

commit v2 on v1

--- a/solution.py
+++ b/solution.py
@@ -10,6 +10,7 @@
 
 BLOCK = 128
 HALF = BLOCK // 2
+WIDTH = 4
 VMEM_BYTES = 56 * 1024 * 1024
 
 
@@ -114,6 +115,36 @@
     return jnp.float32(0.02) * jnp.exp(jnp.float32(2.0) * (accept_rate - jnp.float32(0.574)))
 
 
+def heavy_ranks(counts, keep, heavy, col_index):
+    size, capacity, block = counts.shape
+    height = size // WIDTH
+    parts = counts.reshape(height, WIDTH, capacity, block)
+    at_z, at_x = col_index // WIDTH, col_index % WIDTH
+    heavy_z, heavy_x = heavy // WIDTH, heavy % WIDTH
+
+    def pick(array, axis, index):
+        return lax.dynamic_index_in_dim(array, index, axis, keepdims=False)
+
+    def column(index):
+        part = lax.dynamic_slice(parts, (0, index, keep, 0), (height, 1, capacity - keep, block))
+        return part.reshape(height, capacity - keep, block)
+
+    mine = column(at_x)
+    for shift in range(1, WIDTH):
+        pairs = [(i, i // WIDTH * WIDTH + (i + shift) % WIDTH) for i in range(size)]
+        arrived = lax.ppermute(column((at_x + shift) % WIDTH), "py", pairs)
+        mine = jnp.where((at_x - heavy_x) % WIDTH == shift, arrived, mine)
+    bit = 1
+    while bit < height:
+        mine = mine.reshape(height // (2 * bit), 2, *mine.shape[1:])
+        here = at_z // bit % 2
+        pairs = [(i, i ^ (bit * WIDTH)) for i in range(size)]
+        arrived = lax.ppermute(pick(mine, 1, 1 - here), "py", pairs)
+        mine = jnp.where(here == heavy_z // bit % 2, pick(mine, 1, here), arrived)
+        bit *= 2
+    return mine.reshape(capacity - keep, block)
+
+
 def solution(mesh):
     rows_px, rows_py = mesh.shape["px"], mesh.shape["py"]
     devices = rows_px * rows_py
@@ -139,15 +170,20 @@
         z_table = scaled_table(plain_z, plain_z, size_z)
         tables = [jnp.asarray(part) for part in (*y_table, *even_table, *odd_table)]
 
-        capacity = galaxy_counts.shape[3]
-        counts = lax.all_to_all(galaxy_counts[0, 0], "py", split_axis=0, concat_axis=0, tiled=True)
-
+        galaxy_in = galaxy_counts[0, 0]
+        blocks, capacity = shell_owner.shape[-1], galaxy_counts.shape[3]
+        keep = -(-(-(-(blocks - capacity) // (rows_py - 1))) // 8) * 8
         owner_list = shell_owner.reshape(-1)
         peers = jnp.arange(rows_py, dtype=jnp.int32)
         onehot = owner_list[:, None] == peers[None, :]
         onehot_int = onehot.astype(jnp.int32)
         rank_index = jnp.sum(jnp.cumsum(onehot_int, axis=0) * onehot_int, axis=1) - 1
-        slot_index = owner_list * capacity + rank_index
+        heavy = jnp.argmax(jnp.sum(onehot_int, axis=0)).astype(jnp.int32)
+        slot_index = jnp.where(
+            rank_index < keep, owner_list * keep + rank_index, rows_py * keep + rank_index - keep
+        )
+        counts = lax.all_to_all(galaxy_in[:, :keep], "py", split_axis=0, concat_axis=0, tiled=True)
+        extra = heavy_ranks(galaxy_in, keep, heavy, col_index)
         bias_row = lax.dynamic_index_in_dim(shell_bias, row_index, 0, keepdims=False)
         density_row = lax.dynamic_index_in_dim(shell_density, row_index, 0, keepdims=False)
 
@@ -182,11 +218,13 @@
         )(first, white_noise, mode_amplitude, *tables)
 
         chunk = depth * rows_y
+        sent, extra = lax.optimization_barrier((sent, extra))
         field = lax.all_to_all(
             sent.reshape(devices, chunk, BLOCK), ("px", "py"), split_axis=0, concat_axis=0, tiled=True
         )
 
-        picked = counts.reshape(-1, BLOCK).at[slot_grid.reshape(-1)].get(mode="promise_in_bounds")
+        held = jnp.concatenate([counts.reshape(-1, BLOCK), extra], axis=0)
+        picked = held.at[slot_grid.reshape(-1)].get(mode="promise_in_bounds")
         galaxy = picked.reshape(quarters, -1, BLOCK).transpose(0, 2, 1).reshape(size_z, -1).astype(jnp.float32)
 
         back = pl.pallas_call(

time: 250 us -> 236 us (0.944)
  waiting for transfers between devices: 155 us -> 116 us
  starting transfers between devices: 30.8 us -> 44.3 us
  local copies, waits for them, and re-layouts: 23.4 us -> 28.8 us
  other arithmetic: 14.6 us -> 18.5 us
  between operations: 1.52 us -> 4.23 us
    all_to_all x1, waiting for transfers between devices: 85.8 us -> 0.01 us  [body(): lax.all_to_all(galaxy_in[:, :keep], 'py', split_axis=0, concat_axis=0, ti...]
    ppermute x0 -> x6, waiting for transfers between devices: none -> 36.1 us  [the longest x3 27.9 us: heavy_ranks(): arrived = lax.ppermute(column((at_x + shift) % WIDTH), 'py', pairs)]
    ppermute x0 -> x6, starting transfers between devices: none -> 16.5 us  [the longest x3 11.7 us: heavy_ranks(): arrived = lax.ppermute(pick(mine, 1, 1 - here), 'py', pairs)]
    all_to_all x1, waiting for transfers between devices: 17.2 us -> 27.9 us  [body(): lax.all_to_all(sent.reshape(devices, chunk, BLOCK), ('px', 'py'), split_a...]
    slice x1 -> x2, local copies, waits for them, and re-layouts: 0.79 us -> 3.93 us  [the longest x1 3.14 us: body(): galaxy_in[:, :keep]]
    all_to_all x1, starting transfers between devices: 12.9 us -> 10 us  [body(): lax.all_to_all(sent.reshape(devices, chunk, BLOCK), ('px', 'py'), split_a...]
    reshape x0 -> x1, local copies, waits for them, and re-layouts: none -> 2.57 us  [column(): return part.reshape(height, capacity - keep, block)]
    another operation x3 -> x4, other arithmetic: 9.62 us -> 10.3 us
  transfers between devices with their start and end apart: 3 -> 9, of which waited for: 3 -> 6; matrix products, arithmetic and copies ran while one was open for 15% -> 18% of each run, Pallas kernels for 3% -> 3%
where the time goes in v2:
time: 236 us
  waiting for transfers between devices  116 us (49%)
  starting transfers between devices  44.3 us (19%)
  local copies, waits for them, and re-layouts  28.8 us (12%)
  Pallas kernels  24.2 us (10%)
  other arithmetic  18.5 us (8%)
  between operations  4.23 us (2%)
    all_to_all x1, waiting for transfers between devices, body(): lax.all_to_all(back.reshape(devices, chunk, BLOCK), ('px', 'py'), split_a...  51.7 us
    all_to_all x1, waiting for transfers between devices, body(): lax.all_to_all(sent.reshape(devices, chunk, BLOCK), ('px', 'py'), split_a...  27.9 us
    ppermute x3, waiting for transfers between devices, heavy_ranks(): arrived = lax.ppermute(column((at_x + shift) % WIDTH), 'py', pairs)  27.9 us
    gather x1, local copies, waits for them, and re-layouts, body(): picked = held.at[slot_grid.reshape(-1)].get(mode='promise_in_bounds')  14.2 us
    all_to_all x1, starting transfers between devices, body(): lax.all_to_all(galaxy_in[:, :keep], 'py', split_axis=0, concat_axis=0, ti...  11.9 us
    ppermute x3, starting transfers between devices, heavy_ranks(): arrived = lax.ppermute(pick(mine, 1, 1 - here), 'py', pairs)  11.7 us
    all_to_all x1, starting transfers between devices, body(): lax.all_to_all(sent.reshape(devices, chunk, BLOCK), ('px', 'py'), split_a...  10 us
    another operation x3, other arithmetic  9.62 us
  transfers between devices with their start and end apart: 9, of which 6 were waited for; matrix products, arithmetic and copies ran while one was open for 18% of the time, Pallas kernels for 3%

profile of v2, /device:TPU:1, one launch (start us, length us, event | category | flops | bytes accessed | tf_op | source)
XLA Modules:
  0.0 235.8 jit_solution(4726708959931523314)
XLA Ops:
  0.6 3.1 %slice.14 = s32[32,128,128]{2,1,0:T(8,128)} slice(s32[32,256,128]{2,1,0:T(8,128)} %bitcast.73), slice={[0:32], [0:128], [0:128]} | slice | bytes 4194304 | tf_op jit(solution)/shard_map/slice | solution.py:185
  3.8 11.9 %all-to-all-start.1 = ((s32[32,128,128]{2,1,0:T(8,128)}), s32[32,128,128]{2,1,0:T(8,128)S(1)}, u32[]{:S(2)}, u32[]{:S(2)}) async-start(s32[32,128,128]{2,1,0:T(8,128)} %slice.14), calls=%async_computation.1 | async-start | bytes 4194304 | tf_op jit(solution)/shard_map/all_to_all | solution.py:185
  15.7 2.6 %dynamic-slice_bitcast_fusion = (s32[8,128,128]{2,1,0:T(8,128)}, s32[8,128,128]{2,1,0:T(8,128)}, s32[8,128,128]{2,1,0:T(8,128)}) fusion(s32[8,4,256,128]{3,2,1,0:T(8,128)} %bitcast.74, s32[]{:T(128)S(6)} %select_n.228, s32[]{:T(128)S(6)} %select_n.225, s32[]{:T(128)S(6)} %select_n.222), kind=kLoop, calls=%fused_computation.18 | loop fusion | bytes 3145740 | tf_op jit(solution)/shard_map/reshape | solution.py:130
  19.5 2.4 %collective-permute-start.1 = (s32[8,128,128]{2,1,0:T(8,128)}, s32[8,128,128]{2,1,0:T(8,128)}, u32[]{:S(2)}, u32[]{:S(2)}) collective-permute-start(s32[8,128,128]{2,1,0:T(8,128)} %get-tuple-element.13), channel_id=1, source_target_pairs={{0,2},{1,3},{2,0},{3,1},{4,6},{5,7},{6,4},{7,5},{8,10},{9,11},{10,... | collective-permute-start | bytes 1572872 | tf_op jit(solution)/shard_map/ppermute | solution.py:135
  23.2 9.2 %reduce-window.6 = s32[32,32,128]{2,1,0:T(8,128)S(1)} reduce-window(s32[32,32,128]{2,1,0:T(8,128)S(1)} %fusion.6, s32[]{:T(128)} %constant.217.clone.1), window={size=1x1x128 pad=0_0x0_0x127_0}, to_apply=%region_3.4 | reduce-window | flops 16646144 | bytes 1048580 | tf_op jit(solution)/shard_map/reduce-window
  36.6 9.9 %collective-permute-done.2 = s32[8,128,128]{2,1,0:T(8,128)} collective-permute-done((s32[8,128,128]{2,1,0:T(8,128)}, s32[8,128,128]{2,1,0:T(8,128)}, u32[]{:S(2)}, u32[]{:S(2)}) %collective-permute-start.2) | collective-permute-done | bytes 524320 | tf_op jit(solution)/shard_map/ppermute | solution.py:135
  46.5 17.9 %collective-permute-done.1 = s32[8,128,128]{2,1,0:T(8,128)} collective-permute-done((s32[8,128,128]{2,1,0:T(8,128)}, s32[8,128,128]{2,1,0:T(8,128)}, u32[]{:S(2)}, u32[]{:S(2)}) %collective-permute-start.1) | collective-permute-done | bytes 524320 | tf_op jit(solution)/shard_map/ppermute | solution.py:135
  65.8 1.4 collective-permute-start.3
  67.9 4.2 %collective-permute-done.3 = s32[4,128,128]{2,1,0:T(8,128)S(1)} collective-permute-done((s32[4,128,128]{2,1,0:T(8,128)S(1)}, s32[4,128,128]{2,1,0:T(8,128)S(1)}, u32[]{:S(2)}, u32[]{:S(2)}) %collective-permute-start.3) | collective-permute-done | bytes 262176 | tf_op jit(solution)/shard_map/ppermute | solution.py:142
  72.2 2.2 collective-permute-start.4
  74.4 4.0 %collective-permute-done.4 = s32[2,128,128]{2,1,0:T(8,128)S(1)} collective-permute-done((s32[2,128,128]{2,1,0:T(8,128)S(1)}, s32[2,128,128]{2,1,0:T(8,128)S(1)}, u32[]{:S(2)}, u32[]{:S(2)}) %collective-permute-start.4) | collective-permute-done | bytes 131104 | tf_op jit(solution)/shard_map/ppermute | solution.py:142
  78.5 8.0 %collective-permute-start.5 = (s32[1,128,128]{2,1,0:T(8,128)S(1)}, s32[1,128,128]{2,1,0:T(8,128)S(1)}, u32[]{:S(2)}, u32[]{:S(2)}) collective-permute-start(s32[1,128,128]{2,1,0:T(8,128)S(1)} %constant_dynamic-slice_fusion.2), channel_id=1, source_target_pairs={{0,16},{1,17},{2,18},{3,19},{4,20},{5,21},{6,22},{7,23},{8,24},{9,... | collective-permute-start | bytes 196616 | tf_op jit(solution)/shard_map/ppermute | solution.py:142
  86.5 7.2 %synthesis.1 = f32[8,32,2,8,128]{4,3,2,1,0:T(8,128)} custom-call(s32[1]{0:T(128)} %bitcast.first_ref, f32[2,512,512]{2,1,0:T(8,128)} %white_ref.3, bf16[2,512,512]{2,1,0:T(8,128)(2,1)} %amplitude_ref.3, bf16[512,512]{1,0:T(8,128)(2,1)} %constant.226.clone.y_high, bf16[512,512]{1,0:T(8,128)(2,1)} %constant.227.clone.y_low, ...), custom_call_target="tpu_custom_call" | custom-call | flops 3221225472 | bytes 8388608 | tf_op jit(solution)/shard_map/synthesis/pallas_call | solution.py:209
  95.1 10.0 %all-to-all-start = ((f32[256,16,128]{2,1,0:T(8,128)}), f32[256,16,128]{2,1,0:T(8,128)}, u32[]{:S(2)}, u32[]{:S(2)}) async-start(f32[256,16,128]{2,1,0:T(8,128)} %bitcast.77), calls=%async_computation | async-start | bytes 4194304 | tf_op jit(solution)/shard_map/all_to_all | solution.py:222
  110.4 1.7 pad_add_fusion
  112.1 14.2 %gather_fusion = s32[4096,128]{1,0:T(8,128)} fusion(s32[4224,128]{1,0:T(8,128)S(1)} %pad_add_fusion, s32[4096]{0:T(1024)S(1)} %broadcast_clamp_fusion), kind=kCustom, calls=%fused_computation | custom fusion | bytes 4210688 | tf_op jit(solution)/shard_map/gather | solution.py:227
  126.3 1.7 convert_element_type.26
  128.1 1.8 copy.34
  129.9 27.9 %all-to-all-done = f32[256,16,128]{2,1,0:T(8,128)} async-done(((f32[256,16,128]{2,1,0:T(8,128)}), f32[256,16,128]{2,1,0:T(8,128)}, u32[]{:S(2)}, u32[]{:S(2)}) %all-to-all-start) | async-done | bytes 2097184 | tf_op jit(solution)/shard_map/all_to_all | solution.py:222
  157.8 8.2 %shell_gradient.1 = f32[4096,128]{1,0:T(8,128)} custom-call(f32[4096,128]{1,0:T(8,128)} %bitcast.17.field_ref, f32[512,1024]{1,0:T(8,128)} %bitcast.80, f32[4,1024]{1,0:T(4,128)} %get-tuple-element.9.bias_ref, f32[4,1024]{1,0:T(4,128)} %get-tuple-element.8.density_ref, bf16[512,512]{1,0:T(8,128)(2,1)} %constant.228.clone.even_high.z_high, ...), custom_call_target="tpu_custom_call" | custom-call | flops 3221225472 | bytes 8388608 | tf_op jit(solution)/shard_map/shell_gradient/pallas_call | solution.py:230
  166.1 5.9 %all-to-all-start.2 = ((f32[256,16,128]{2,1,0:T(8,128)}), f32[256,16,128]{2,1,0:T(8,128)S(1)}, u32[]{:S(2)}, u32[]{:S(2)}) async-start(f32[256,16,128]{2,1,0:T(8,128)} %bitcast.79), calls=%async_computation.2 | async-start | bytes 4194304 | tf_op jit(solution)/shard_map/all_to_all | solution.py:238
  173.9 51.7 %all-to-all-done.2 = f32[256,16,128]{2,1,0:T(8,128)S(1)} async-done(((f32[256,16,128]{2,1,0:T(8,128)}), f32[256,16,128]{2,1,0:T(8,128)S(1)}, u32[]{:S(2)}, u32[]{:S(2)}) %all-to-all-start.2) | async-done | bytes 2097184 | tf_op jit(solution)/shard_map/all_to_all | solution.py:238
  225.6 1.3 copy-done.1
  227.0 8.8 %analysis.1 = (f32[2,512,512]{2,1,0:T(8,128)}, f32[2,512,512]{2,1,0:T(8,128)}) custom-call(s32[1]{0:T(128)} %bitcast.first_ref, f32[2]{0:T(128)} %pad_maximum_fusion.step_ref, f32[8,32,2,8,128]{4,3,2,1,0:T(8,128)} %bitcast.78, f32[2,512,512]{2,1,0:T(8,128)} %white_ref.3, bf16[2,512,512]{2,1,0:T(8,128)(2,1)} %amplitude_ref.3, bf16[2,512,512]{2,1,0:T(8,128)(2,1)} %kick_ref.1, ...), custom_call_target="tpu_custom_call" | custom-call | flops 3221225472 | bytes 12582912 | tf_op jit(solution)/shard_map/analysis/pallas_call | solution.py:244
  (43 shorter events, 14.0 us)
Async XLA Ops:
  3.8 90.0 %all-to-all-start.1 = ((s32[32,128,128]{2,1,0:T(8,128)}), s32[32,128,128]{2,1,0:T(8,128)S(1)}, u32[]{:S(2)}, u32[]{:S(2)}) async-start(s32[32,128,128]{2,1,0:T(8,128)} %slice.14), calls=%async_computation.1 | async-start | bytes 4194304 | tf_op jit(solution)/shard_map/all_to_all | solution.py:185
  15.6 7.5 %copy-start.2 = (s32[1,1,4096]{2,1,0:T(1,128)S(1)}, s32[1,1,4096]{2,1,0:T(1,128)}, u32[]{:S(2)}) copy-start(s32[1,1,4096]{2,1,0:T(1,128)} %param.19) | copy-start | bytes 49156
  18.3 28.3 %collective-permute-start.2 = (s32[8,128,128]{2,1,0:T(8,128)}, s32[8,128,128]{2,1,0:T(8,128)}, u32[]{:S(2)}, u32[]{:S(2)}) collective-permute-start(s32[8,128,128]{2,1,0:T(8,128)} %get-tuple-element.12), channel_id=1, source_target_pairs={{0,1},{1,2},{2,3},{3,0},{4,5},{5,6},{6,7},{7,4},{8,9},{9,10},{10,1... | collective-permute-start | bytes 1572872 | tf_op jit(solution)/shard_map/ppermute | solution.py:135
  19.5 45.0 %collective-permute-start.1 = (s32[8,128,128]{2,1,0:T(8,128)}, s32[8,128,128]{2,1,0:T(8,128)}, u32[]{:S(2)}, u32[]{:S(2)}) collective-permute-start(s32[8,128,128]{2,1,0:T(8,128)} %get-tuple-element.13), channel_id=1, source_target_pairs={{0,2},{1,3},{2,0},{3,1},{4,6},{5,7},{6,4},{7,5},{8,10},{9,11},{10,... | collective-permute-start | bytes 1572872 | tf_op jit(solution)/shard_map/ppermute | solution.py:135
  21.9 42.6 %collective-permute-start = (s32[8,128,128]{2,1,0:T(8,128)}, s32[8,128,128]{2,1,0:T(8,128)}, u32[]{:S(2)}, u32[]{:S(2)}) collective-permute-start(s32[8,128,128]{2,1,0:T(8,128)} %get-tuple-element.14), channel_id=1, source_target_pairs={{0,3},{1,0},{2,1},{3,2},{4,7},{5,4},{6,5},{7,6},{8,11},{9,8},{10,9... | collective-permute-start | bytes 1572872 | tf_op jit(solution)/shard_map/ppermute | solution.py:135
  65.8 6.3 %collective-permute-start.3 = (s32[4,128,128]{2,1,0:T(8,128)S(1)}, s32[4,128,128]{2,1,0:T(8,128)S(1)}, u32[]{:S(2)}, u32[]{:S(2)}) collective-permute-start(s32[4,128,128]{2,1,0:T(8,128)S(1)} %dynamic-slice_bitcast_fusion.3), channel_id=1, source_target_pairs={{0,4},{1,5},{2,6},{3,7},{4,0},{5,1},{6,2},{7,3},{8,12},{9,13},{10,... | collective-permute-start | bytes 786440 | tf_op jit(solution)/shard_map/ppermute | solution.py:142
  72.2 6.2 %collective-permute-start.4 = (s32[2,128,128]{2,1,0:T(8,128)S(1)}, s32[2,128,128]{2,1,0:T(8,128)S(1)}, u32[]{:S(2)}, u32[]{:S(2)}) collective-permute-start(s32[2,128,128]{2,1,0:T(8,128)S(1)} %dynamic-slice_bitcast_fusion.4), channel_id=1, source_target_pairs={{0,8},{1,9},{2,10},{3,11},{4,12},{5,13},{6,14},{7,15},{8,0},{9,1},... | collective-permute-start | bytes 393224 | tf_op jit(solution)/shard_map/ppermute | solution.py:142
  78.5 15.3 %collective-permute-start.5 = (s32[1,128,128]{2,1,0:T(8,128)S(1)}, s32[1,128,128]{2,1,0:T(8,128)S(1)}, u32[]{:S(2)}, u32[]{:S(2)}) collective-permute-start(s32[1,128,128]{2,1,0:T(8,128)S(1)} %constant_dynamic-slice_fusion.2), channel_id=1, source_target_pairs={{0,16},{1,17},{2,18},{3,19},{4,20},{5,21},{6,22},{7,23},{8,24},{9,... | collective-permute-start | bytes 196616 | tf_op jit(solution)/shard_map/ppermute | solution.py:142
  93.7 1.3 copy-start
  95.1 62.8 %all-to-all-start = ((f32[256,16,128]{2,1,0:T(8,128)}), f32[256,16,128]{2,1,0:T(8,128)}, u32[]{:S(2)}, u32[]{:S(2)}) async-start(f32[256,16,128]{2,1,0:T(8,128)} %bitcast.77), calls=%async_computation | async-start | bytes 4194304 | tf_op jit(solution)/shard_map/all_to_all | solution.py:222
  166.1 5.9 %copy-start.3 = (s32[64]{0:T(128)S(1)}, s32[64]{0:T(128)}, u32[]{:S(2)}) copy-start(s32[64]{0:T(128)} %param.23) | copy-start | bytes 772
  166.1 59.5 %all-to-all-start.2 = ((f32[256,16,128]{2,1,0:T(8,128)}), f32[256,16,128]{2,1,0:T(8,128)S(1)}, u32[]{:S(2)}, u32[]{:S(2)}) async-start(f32[256,16,128]{2,1,0:T(8,128)} %bitcast.79), calls=%async_computation.2 | async-start | bytes 4194304 | tf_op jit(solution)/shard_map/all_to_all | solution.py:238
  225.6 1.4 copy-start.1

commit v3 on v2

--- a/solution.py
+++ b/solution.py
@@ -14,8 +14,9 @@
 VMEM_BYTES = 56 * 1024 * 1024
 
 
-def scaled_table(rows, cols, order):
-    angle = (rows[:, None] * cols[None, :] % order).astype(np.float64) * (2.0 * math.pi / order)
+def scaled_table(order):
+    place = np.arange(order)
+    angle = (place[:, None] * place[None, :] % order).astype(np.float64) * (2.0 * math.pi / order)
     table = ((np.cos(angle) + np.sin(angle)) / math.sqrt(order)).astype(np.float32)
     high = table.astype(jnp.bfloat16)
     low = (table - high.astype(np.float32)).astype(jnp.bfloat16)
@@ -39,72 +40,136 @@
     return lax.broadcasted_iota(jnp.int32, shape, len(shape) - 1) % BLOCK < HALF
 
 
-def live_amplitude(first_ref, amplitude_ref):
-    amplitude = amplitude_ref[0].astype(jnp.float32)
+def swap_halves(value):
+    return pltpu.roll(value, HALF, axis=1)
+
+
+def live_amplitude(first, amplitude):
     rows = lax.broadcasted_iota(jnp.int32, amplitude.shape, 0)
     cols = lax.broadcasted_iota(jnp.int32, amplitude.shape, 1)
-    anchor = (rows + cols + first_ref[0] + pl.program_id(0)) == 0
-    return jnp.where(anchor, 0.0, amplitude)
-
-
-def synthesis_kernel(
-    first_ref, white_ref, amplitude_ref, y_high, y_low, even_high, even_low, odd_high, odd_low, out_ref
-):
-    weighted = split(live_amplitude(first_ref, amplitude_ref) * white_ref[0])
-    passed = product((y_high[...], y_low[...]), weighted, ((1,), (1,)))
-    rows = passed.shape[0] // 2
-    lower = product(split(passed[:rows]), (even_high[...], even_low[...]))
-    upper = product(split(passed[rows:]), (odd_high[...], odd_low[...]))
-    groups = out_ref.shape[1]
+    return jnp.where(rows + cols + first == 0, 0.0, amplitude.astype(jnp.float32))
+
+
+def synthesis_kernel(first_ref, white_ref, amplitude_ref, high_ref, low_ref, out_ref):
+    table = (high_ref[...], low_ref[...])
+    weighted = live_amplitude(first_ref[0] + pl.program_id(0), amplitude_ref[0]) * white_ref[0]
+    passed = product(table, split(weighted), ((1,), (1,)))
+    groups, rows_y = out_ref.shape[1], out_ref.shape[3]
+    passed = passed.reshape(groups, 2, rows_y, -1)
+    lower, upper = (product(split(passed[:, k].reshape(groups * rows_y, -1)), table) for k in range(2))
     for pair in range(out_ref.shape[0] // 2):
         left = lower[:, pair * BLOCK : (pair + 1) * BLOCK]
-        right = upper[:, pair * BLOCK : (pair + 1) * BLOCK]
+        right = swap_halves(upper[:, pair * BLOCK : (pair + 1) * BLOCK])
         mask = first_half(left.shape)
         out_ref[2 * pair, :, 0] = jnp.where(mask, left, right).reshape(groups, -1, BLOCK)
         out_ref[2 * pair + 1, :, 0] = jnp.where(mask, right, left).reshape(groups, -1, BLOCK)
 
 
-def shell_kernel(field_ref, galaxy_ref, bias_ref, density_ref, z_high, z_low, out_ref):
-    table = (z_high[...], z_low[...])
-    size_z = z_high.shape[0]
+def shell_kernel(
+    field_any, galaxy_any, bias_ref, density_ref, high_any, low_any, out_any,
+    field_ref, galaxy_ref, high_ref, low_ref, grad_high, grad_low, out_ref, in_sems, galaxy_sems, out_sems,
+):
+    size_z = high_ref.shape[0]
     rows_y = field_ref.shape[0] // size_z
-    for step in range(rows_y // 2):
+    pairs, quarters = rows_y // 2, size_z // BLOCK
+    loads = [
+        pltpu.make_async_copy(source, target, in_sems.at[k])
+        for k, (source, target) in enumerate(
+            [(high_any, high_ref), (field_any, field_ref), (low_any, low_ref)]
+        )
+    ]
+    spans = [slice(2 * step * BLOCK, 2 * (step + 1) * BLOCK) for step in range(pairs)]
+    counts = [
+        pltpu.make_async_copy(galaxy_any.at[:, span], galaxy_ref.at[:, span], galaxy_sems.at[step])
+        for step, span in enumerate(spans)
+    ]
+    for copy in loads + counts:
+        copy.start()
+    for copy in loads:
+        copy.wait()
+    table = (high_ref[...], low_ref[...])
+    for step, span in enumerate(spans):
         field = jnp.concatenate(
             [field_ref[pl.ds(2 * step + k, size_z, stride=rows_y), :] for k in range(2)], axis=1
         )
         contrast = product(table, split(field))
-        span = slice(2 * step * BLOCK, 2 * (step + 1) * BLOCK)
-        grads = []
-        for quarter in range(size_z // BLOCK):
+        counts[step].wait()
+        for quarter in range(quarters):
             depth = slice(quarter * BLOCK, (quarter + 1) * BLOCK)
             bias = bias_ref[quarter : quarter + 1, span]
             density = density_ref[quarter : quarter + 1, span]
-            grads.append(bias * (galaxy_ref[depth, span] - density * jnp.exp(bias * contrast[depth])))
-        back = product(table, split(jnp.concatenate(grads, axis=0)))
-        for k in range(2):
-            out_ref[pl.ds(2 * step + k, size_z, stride=rows_y), :] = back[:, k * BLOCK : (k + 1) * BLOCK]
+            grad = bias * (galaxy_ref[depth, span] - density * jnp.exp(bias * contrast[depth]))
+            grad_high[depth, span], grad_low[depth, span] = split(grad)
+    grads = (grad_high[...], grad_low[...])
+    stores = []
+    for quarter in range(quarters):
+        depth = slice(quarter * BLOCK, (quarter + 1) * BLOCK)
+        back = product((high_ref[depth, :], low_ref[depth, :]), grads)
+        start = quarter * BLOCK * rows_y
+        for row in range(rows_y):
+            out_ref[pl.ds(start + row, BLOCK, stride=rows_y), :] = back[:, row * BLOCK : (row + 1) * BLOCK]
+        part = slice(start, start + BLOCK * rows_y)
+        stores.append(pltpu.make_async_copy(out_ref.at[part], out_any.at[part], out_sems.at[quarter]))
+        stores[-1].start()
+    for copy in stores:
+        copy.wait()
 
 
 def analysis_kernel(
-    first_ref, step_ref, field_ref, white_ref, amplitude_ref, kick_ref,
-    y_high, y_low, even_high, even_low, odd_high, odd_low, grad_ref, next_ref,
+    first_ref, step_ref, field_any, white_any, amplitude_any, kick_any, high_any, low_any, grad_any, next_any,
+    field_ref, white_ref, amplitude_ref, kick_ref, high_ref, low_ref, grad_ref, next_ref,
+    table_sems, field_sems, mode_sems, out_sems,
 ):
-    lower, upper = [], []
-    for pair in range(field_ref.shape[0] // 2):
-        left = field_ref[2 * pair, :, 0].reshape(-1, BLOCK)
-        right = field_ref[2 * pair + 1, :, 0].reshape(-1, BLOCK)
-        mask = first_half(left.shape)
-        lower.append(jnp.where(mask, left, right))
-        upper.append(jnp.where(mask, right, left))
-    contract = ((1,), (1,))
-    lower = product(split(jnp.concatenate(lower, axis=1)), (even_high[...], even_low[...]), contract)
-    upper = product(split(jnp.concatenate(upper, axis=1)), (odd_high[...], odd_low[...]), contract)
-    passed = split(jnp.concatenate([lower, upper], axis=0))
-    back = product(passed, (y_high[...], y_low[...]), ((0,), (0,)))
-    white = white_ref[0]
-    gradient = live_amplitude(first_ref, amplitude_ref) * back - white
-    grad_ref[0] = gradient
-    next_ref[0] = white + step_ref[0] * gradient + step_ref[1] * kick_ref[0].astype(jnp.float32)
+    depth = white_ref.shape[0]
+    tables = [
+        pltpu.make_async_copy(high_any, high_ref, table_sems.at[0]),
+        pltpu.make_async_copy(low_any, low_ref, table_sems.at[1]),
+    ]
+    fields = [
+        pltpu.make_async_copy(field_any.at[:, :, k], field_ref.at[k], field_sems.at[k]) for k in range(depth)
+    ]
+    modes = [
+        [
+            pltpu.make_async_copy(source.at[k], target.at[k], mode_sems.at[k, n])
+            for n, (source, target) in enumerate(
+                [(white_any, white_ref), (amplitude_any, amplitude_ref), (kick_any, kick_ref)]
+            )
+        ]
+        for k in range(depth)
+    ]
+    for copy in [fields[0], *tables, *fields[1:]] + sum(modes, []):
+        copy.start()
+    for copy in tables:
+        copy.wait()
+    table = (high_ref[...], low_ref[...])
+    stores = []
+    for k in range(depth):
+        fields[k].wait()
+        lower, upper = [], []
+        for pair in range(field_ref.shape[1] // 2):
+            left = field_ref[k, 2 * pair].reshape(-1, BLOCK)
+            right = field_ref[k, 2 * pair + 1].reshape(-1, BLOCK)
+            mask = first_half(left.shape)
+            lower.append(jnp.where(mask, left, right))
+            upper.append(swap_halves(jnp.where(mask, right, left)))
+        groups, rows_y = field_ref.shape[2:4]
+        halves = [
+            product(split(jnp.concatenate(half, axis=1)), table).reshape(groups, rows_y, -1)
+            for half in (lower, upper)
+        ]
+        passed = jnp.stack(halves, axis=1).reshape(2 * groups * rows_y, -1)
+        back = product(split(passed), table, ((0,), (0,)))
+        for copy in modes[k]:
+            copy.wait()
+        white = white_ref[k]
+        gradient = live_amplitude(first_ref[0] + k, amplitude_ref[k]) * back - white
+        grad_ref[k] = gradient
+        next_ref[k] = white + step_ref[0] * gradient + step_ref[1] * kick_ref[k].astype(jnp.float32)
+        for n, (source, target) in enumerate([(grad_ref, grad_any), (next_ref, next_any)]):
+            stores.append(pltpu.make_async_copy(source.at[k], target.at[k], out_sems.at[k, n]))
+            stores[-1].start()
+    for copy in stores:
+        copy.wait()
 
 
 def adapted_step(accepted):
@@ -161,14 +226,7 @@
         col_index = lax.axis_index("py")
         first = ((row_index * rows_py + col_index) * depth).reshape(1)
 
-        plain_x, plain_y, plain_z = np.arange(size_x), np.arange(size_y), np.arange(size_z)
-        y_order = plain_y.reshape(rows_py, 2, rows_y).transpose(1, 0, 2).reshape(-1)
-        x_order = plain_x.reshape(-1, 2, HALF)[:, ::-1].reshape(-1)
-        y_table = scaled_table(y_order, plain_y, size_y)
-        even_table = scaled_table(plain_x, plain_x, size_x)
-        odd_table = scaled_table(plain_x, x_order, size_x)
-        z_table = scaled_table(plain_z, plain_z, size_z)
-        tables = [jnp.asarray(part) for part in (*y_table, *even_table, *odd_table)]
+        tables = [jnp.asarray(part) for part in scaled_table(size_x)]
 
         galaxy_in = galaxy_counts[0, 0]
         blocks, capacity = shell_owner.shape[-1], galaxy_counts.shape[3]
@@ -218,7 +276,6 @@
         )(first, white_noise, mode_amplitude, *tables)
 
         chunk = depth * rows_y
-        sent, extra = lax.optimization_barrier((sent, extra))
         field = lax.all_to_all(
             sent.reshape(devices, chunk, BLOCK), ("px", "py"), split_axis=0, concat_axis=0, tiled=True
         )
@@ -227,13 +284,30 @@
         picked = held.at[slot_grid.reshape(-1)].get(mode="promise_in_bounds")
         galaxy = picked.reshape(quarters, -1, BLOCK).transpose(0, 2, 1).reshape(size_z, -1).astype(jnp.float32)
 
+        anywhere = pl.BlockSpec(memory_space=pl.ANY)
+        inside = pl.BlockSpec(memory_space=pltpu.VMEM)
+        table_shapes = [pltpu.VMEM(table.shape, jnp.bfloat16) for table in tables]
+        cells = (size_z * rows_y, BLOCK)
         back = pl.pallas_call(
             shell_kernel,
-            out_shape=jax.ShapeDtypeStruct((size_z * rows_y, BLOCK), jnp.float32),
+            in_specs=[anywhere, anywhere, inside, inside, anywhere, anywhere],
+            out_specs=anywhere,
+            out_shape=jax.ShapeDtypeStruct(cells, jnp.float32),
+            scratch_shapes=[
+                pltpu.VMEM(cells, jnp.float32),
+                pltpu.VMEM(galaxy.shape, jnp.float32),
+                *table_shapes,
+                pltpu.VMEM(galaxy.shape, jnp.bfloat16),
+                pltpu.VMEM(galaxy.shape, jnp.bfloat16),
+                pltpu.VMEM(cells, jnp.float32),
+                pltpu.SemaphoreType.DMA((3,)),
+                pltpu.SemaphoreType.DMA((rows_y // 2,)),
+                pltpu.SemaphoreType.DMA((quarters,)),
+            ],
             compiler_params=params,
             cost_estimate=pl.CostEstimate(flops=flops, bytes_accessed=8 * 2**20, transcendentals=size_z * 1024),
             name="shell_gradient",
-        )(field.reshape(-1, BLOCK), galaxy, bias_grid, density_grid, *[jnp.asarray(part) for part in z_table])
+        )(field.reshape(cells), galaxy, bias_grid, density_grid, *tables)
 
         returned = lax.all_to_all(
             back.reshape(devices, chunk, BLOCK), ("px", "py"), split_axis=0, concat_axis=0, tiled=True
@@ -243,10 +317,22 @@
         out_plane = jax.ShapeDtypeStruct(white_noise.shape, jnp.float32)
         return pl.pallas_call(
             analysis_kernel,
-            grid=(depth,),
-            in_specs=[scalar, scalar, packed, plane, plane, plane] + [whole(table) for table in tables],
-            out_specs=(plane, plane),
+            in_specs=[scalar, scalar] + [anywhere] * 6,
+            out_specs=(anywhere, anywhere),
             out_shape=(out_plane, out_plane),
+            scratch_shapes=[
+                pltpu.VMEM((depth, rows_px, rows_py, rows_y, BLOCK), jnp.float32),
+                pltpu.VMEM(white_noise.shape, jnp.float32),
+                pltpu.VMEM(white_noise.shape, jnp.bfloat16),
+                pltpu.VMEM(white_noise.shape, jnp.bfloat16),
+                *table_shapes,
+                pltpu.VMEM(white_noise.shape, jnp.float32),
+                pltpu.VMEM(white_noise.shape, jnp.float32),
+                pltpu.SemaphoreType.DMA((2,)),
+                pltpu.SemaphoreType.DMA((depth,)),
+                pltpu.SemaphoreType.DMA((depth, 3)),
+                pltpu.SemaphoreType.DMA((depth, 2)),
+            ],
             compiler_params=params,
             cost_estimate=pl.CostEstimate(flops=flops, bytes_accessed=12 * 2**20, transcendentals=0),
             name="analysis",

time: 236 us -> 253 us (1.072)
  waiting for transfers between devices: 116 us -> 123 us
  starting transfers between devices: 44.3 us -> 50.8 us
    ppermute x3, waiting for transfers between devices: 8.21 us -> 46.9 us  [heavy_ranks(): arrived = lax.ppermute(pick(mine, 1, 1 - here), 'py', pairs)]
    all_to_all x1, waiting for transfers between devices: 27.9 us -> 0.01 us  [body(): lax.all_to_all(sent.reshape(devices, chunk, BLOCK), ('px', 'py'), split_a...]
    ppermute x3, waiting for transfers between devices: 27.9 us -> 0.01 us  [heavy_ranks(): arrived = lax.ppermute(column((at_x + shift) % WIDTH), 'py', pairs)]
    all_to_all x1, waiting for transfers between devices: 0.01 us -> 24.4 us  [body(): lax.all_to_all(galaxy_in[:, :keep], 'py', split_axis=0, concat_axis=0, ti...]
    all_to_all x1, starting transfers between devices: 5.89 us -> 14.1 us  [body(): lax.all_to_all(back.reshape(devices, chunk, BLOCK), ('px', 'py'), split_a...]
    pallas_call x2, Pallas kernels: 17 us -> 19.7 us  [the longest x1 10.2 us: body(): pl.pallas_call(shell_kernel, in_specs=[anywhere, anywhere, inside, inside...]
  transfers between devices with their start and end apart: 9 -> 9, of which waited for: 6 -> 5; matrix products, arithmetic and copies ran while one was open for 18% -> 16% of each run, Pallas kernels for 3% -> 3%
where the time goes in v3:
time: 253 us; the launch traced here: 252 us
  waiting for transfers between devices  123 us (49%)
  starting transfers between devices  50.8 us (20%)
  local copies, waits for them, and re-layouts  28.9 us (11%)
  Pallas kernels  26.6 us (11%)
  other arithmetic  18.6 us (7%)
  between operations  4.57 us (2%)
    all_to_all x1, waiting for transfers between devices, body(): lax.all_to_all(back.reshape(devices, chunk, BLOCK), ('px', 'py'), split_a...  51.7 us
    ppermute x3, waiting for transfers between devices, heavy_ranks(): arrived = lax.ppermute(pick(mine, 1, 1 - here), 'py', pairs)  46.9 us
    all_to_all x1, waiting for transfers between devices, body(): lax.all_to_all(galaxy_in[:, :keep], 'py', split_axis=0, concat_axis=0, ti...  24.4 us
    gather x1, local copies, waits for them, and re-layouts, body(): picked = held.at[slot_grid.reshape(-1)].get(mode='promise_in_bounds')  14.2 us
    all_to_all x1, starting transfers between devices, body(): lax.all_to_all(back.reshape(devices, chunk, BLOCK), ('px', 'py'), split_a...  14.1 us
    all_to_all x1, starting transfers between devices, body(): lax.all_to_all(galaxy_in[:, :keep], 'py', split_axis=0, concat_axis=0, ti...  11.9 us
    all_to_all x1, starting transfers between devices, body(): lax.all_to_all(sent.reshape(devices, chunk, BLOCK), ('px', 'py'), split_a...  11.8 us
    pallas_call x1, Pallas kernels, body(): pl.pallas_call(shell_kernel, in_specs=[anywhere, anywhere, inside, inside...  10.2 us
  transfers between devices with their start and end apart: 9, of which 5 were waited for; matrix products, arithmetic and copies ran while one was open for 16% of the time, Pallas kernels for 3%

profile of v3, /device:TPU:1, one launch (start us, length us, event | category | flops | bytes accessed | tf_op | source)
XLA Modules:
  0.0 252.5 jit_solution(6762908243223833983)
XLA Ops:
  0.6 3.1 %slice.14 = s32[32,128,128]{2,1,0:T(8,128)} slice(s32[32,256,128]{2,1,0:T(8,128)} %bitcast.73), slice={[0:32], [0:128], [0:128]} | slice | bytes 4194304 | tf_op jit(solution)/shard_map/slice | solution.py:243
  3.8 11.9 %all-to-all-start.1 = ((s32[32,128,128]{2,1,0:T(8,128)}), s32[32,128,128]{2,1,0:T(8,128)S(1)}, u32[]{:S(2)}, u32[]{:S(2)}) async-start(s32[32,128,128]{2,1,0:T(8,128)} %slice.14), calls=%async_computation.1 | async-start | bytes 4194304 | tf_op jit(solution)/shard_map/all_to_all | solution.py:243
  15.7 2.5 %dynamic-slice_bitcast_fusion = (s32[8,128,128]{2,1,0:T(8,128)}, s32[8,128,128]{2,1,0:T(8,128)}, s32[8,128,128]{2,1,0:T(8,128)}) fusion(s32[8,4,256,128]{3,2,1,0:T(8,128)} %bitcast.74, s32[]{:T(128)S(6)} %select_n.228, s32[]{:T(128)S(6)} %select_n.225, s32[]{:T(128)S(6)} %select_n.222), kind=kLoop, calls=%fused_computation.18 | loop fusion | bytes 3145740 | tf_op jit(solution)/shard_map/reshape | solution.py:195
  18.3 2.4 collective-permute-start
  21.9 9.2 %reduce-window.6 = s32[32,32,128]{2,1,0:T(8,128)S(1)} reduce-window(s32[32,32,128]{2,1,0:T(8,128)S(1)} %fusion.6, s32[]{:T(128)} %constant.209.clone.1), window={size=1x1x128 pad=0_0x0_0x127_0}, to_apply=%region_3.4 | reduce-window | flops 16646144 | bytes 1048580 | tf_op jit(solution)/shard_map/reduce-window
  32.8 6.9 %synthesis.1 = f32[8,32,2,8,128]{4,3,2,1,0:T(8,128)} custom-call(s32[1]{0:T(128)} %bitcast.first_ref, f32[2,512,512]{2,1,0:T(8,128)} %white_any.1, bf16[2,512,512]{2,1,0:T(8,128)(2,1)} %amplitude_any.1, bf16[512,512]{1,0:T(8,128)(2,1)} %constant.218.clone.high_ref.high_any, bf16[512,512]{1,0:T(8,128)(2,1)} %constant.219.clone.low_ref.low_any), custom_call_target="tpu_custom_call" | custom-call | flops 3221225472 | bytes 8388608 | tf_op jit(solution)/shard_map/synthesis/pallas_call | solution.py:267
  39.7 24.4 %all-to-all-done.1 = s32[32,128,128]{2,1,0:T(8,128)S(1)} async-done(((s32[32,128,128]{2,1,0:T(8,128)}), s32[32,128,128]{2,1,0:T(8,128)S(1)}, u32[]{:S(2)}, u32[]{:S(2)}) %all-to-all-start.1) | async-done | bytes 2097184 | tf_op jit(solution)/shard_map/all_to_all | solution.py:243
  65.4 11.8 %all-to-all-start = ((f32[256,16,128]{2,1,0:T(8,128)}), f32[256,16,128]{2,1,0:T(8,128)}, u32[]{:S(2)}, u32[]{:S(2)}) async-start(f32[256,16,128]{2,1,0:T(8,128)} %bitcast.77), calls=%async_computation | async-start | bytes 4194304 | tf_op jit(solution)/shard_map/all_to_all | solution.py:279
  83.6 1.3 fusion.5
  84.9 1.6 collective-permute-start.3
  87.3 40.3 %collective-permute-done.3 = s32[4,128,128]{2,1,0:T(8,128)S(1)} collective-permute-done((s32[4,128,128]{2,1,0:T(8,128)S(1)}, s32[4,128,128]{2,1,0:T(8,128)S(1)}, u32[]{:S(2)}, u32[]{:S(2)}) %collective-permute-start.3) | collective-permute-done | bytes 262176 | tf_op jit(solution)/shard_map/ppermute | solution.py:207
  127.6 2.7 %collective-permute-start.4 = (s32[2,128,128]{2,1,0:T(8,128)S(1)}, s32[2,128,128]{2,1,0:T(8,128)S(1)}, u32[]{:S(2)}, u32[]{:S(2)}) collective-permute-start(s32[2,128,128]{2,1,0:T(8,128)S(1)} %dynamic-slice_bitcast_fusion.4), channel_id=1, source_target_pairs={{0,8},{1,9},{2,10},{3,11},{4,12},{5,13},{6,14},{7,15},{8,0},{9,1},... | collective-permute-start | bytes 393224 | tf_op jit(solution)/shard_map/ppermute | solution.py:207
  131.4 5.2 %collective-permute-done.4 = s32[2,128,128]{2,1,0:T(8,128)S(1)} collective-permute-done((s32[2,128,128]{2,1,0:T(8,128)S(1)}, s32[2,128,128]{2,1,0:T(8,128)S(1)}, u32[]{:S(2)}, u32[]{:S(2)}) %collective-permute-start.4) | collective-permute-done | bytes 131104 | tf_op jit(solution)/shard_map/ppermute | solution.py:207
  136.7 5.1 %collective-permute-start.5 = (s32[1,128,128]{2,1,0:T(8,128)S(1)}, s32[1,128,128]{2,1,0:T(8,128)S(1)}, u32[]{:S(2)}, u32[]{:S(2)}) collective-permute-start(s32[1,128,128]{2,1,0:T(8,128)S(1)} %constant_dynamic-slice_fusion.2), channel_id=1, source_target_pairs={{0,16},{1,17},{2,18},{3,19},{4,20},{5,21},{6,22},{7,23},{8,24},{9,... | collective-permute-start | bytes 196616 | tf_op jit(solution)/shard_map/ppermute | solution.py:207
  142.6 1.4 collective-permute-done.5
  144.0 1.7 pad_add_fusion
  145.7 14.2 %gather_fusion = s32[4096,128]{1,0:T(8,128)} fusion(s32[4224,128]{1,0:T(8,128)S(1)} %pad_add_fusion, s32[4096]{0:T(1024)S(1)} %broadcast_clamp_fusion), kind=kCustom, calls=%fused_computation | custom fusion | bytes 4210688 | tf_op jit(solution)/shard_map/gather | solution.py:284
  159.9 1.7 convert_element_type.26
  161.7 1.8 copy.28
  163.5 10.2 %shell_gradient.1 = f32[4096,128]{1,0:T(8,128)} custom-call(f32[4096,128]{1,0:T(8,128)} %bitcast.4.field_any, f32[512,1024]{1,0:T(8,128)} %bitcast.80, f32[4,1024]{1,0:T(4,128)} %get-tuple-element.5.bias_ref, f32[4,1024]{1,0:T(4,128)} %get-tuple-element.4.density_ref, bf16[512,512]{1,0:T(8,128)(2,1)} %constant.218.clone.high_ref.high_any, ...), custom_call_target="tpu_custom_call" | custom-call | flops 3221225472 | bytes 8388608 | tf_op jit(solution)/shard_map/shell_gradient/pallas_call | solution.py:291
  173.7 14.1 %all-to-all-start.2 = ((f32[256,16,128]{2,1,0:T(8,128)}), f32[256,16,128]{2,1,0:T(8,128)S(1)}, u32[]{:S(2)}, u32[]{:S(2)}) async-start(f32[256,16,128]{2,1,0:T(8,128)} %bitcast.79), calls=%async_computation.2 | async-start | bytes 4194304 | tf_op jit(solution)/shard_map/all_to_all | solution.py:312
  189.8 51.7 %all-to-all-done.2 = f32[256,16,128]{2,1,0:T(8,128)S(1)} async-done(((f32[256,16,128]{2,1,0:T(8,128)}), f32[256,16,128]{2,1,0:T(8,128)S(1)}, u32[]{:S(2)}, u32[]{:S(2)}) %all-to-all-start.2) | async-done | bytes 2097184 | tf_op jit(solution)/shard_map/all_to_all | solution.py:312
  241.5 1.3 copy-done.1
  242.9 9.4 %analysis.1 = (f32[2,512,512]{2,1,0:T(8,128)}, f32[2,512,512]{2,1,0:T(8,128)}) custom-call(s32[1]{0:T(128)} %bitcast.first_ref, f32[2]{0:T(128)} %pad_maximum_fusion.step_ref, f32[8,32,2,8,128]{4,3,2,1,0:T(8,128)} %bitcast.78, f32[2,512,512]{2,1,0:T(8,128)} %white_any.1, bf16[2,512,512]{2,1,0:T(8,128)(2,1)} %amplitude_any.1, bf16[2,512,512]{2,1,0:T(8,128)(2,1)} %kick_any.1, ...), custom_call_target="tpu_custom_call" | custom-call | flops 3221225472 | bytes 12582912 | tf_op jit(solution)/shard_map/analysis/pallas_call | solution.py:318
  (43 shorter events, 11.5 us)
Async XLA Ops:
  3.8 60.4 %all-to-all-start.1 = ((s32[32,128,128]{2,1,0:T(8,128)}), s32[32,128,128]{2,1,0:T(8,128)S(1)}, u32[]{:S(2)}, u32[]{:S(2)}) async-start(s32[32,128,128]{2,1,0:T(8,128)} %slice.14), calls=%async_computation.1 | async-start | bytes 4194304 | tf_op jit(solution)/shard_map/all_to_all | solution.py:243
  15.6 6.2 %copy-start.2 = (s32[1,1,4096]{2,1,0:T(1,128)S(1)}, s32[1,1,4096]{2,1,0:T(1,128)}, u32[]{:S(2)}) copy-start(s32[1,1,4096]{2,1,0:T(1,128)} %param.13) | copy-start | bytes 49156
  18.3 65.2 %collective-permute-start = (s32[8,128,128]{2,1,0:T(8,128)}, s32[8,128,128]{2,1,0:T(8,128)}, u32[]{:S(2)}, u32[]{:S(2)}) collective-permute-start(s32[8,128,128]{2,1,0:T(8,128)} %get-tuple-element.10), channel_id=1, source_target_pairs={{0,3},{1,0},{2,1},{3,2},{4,7},{5,4},{6,5},{7,6},{8,11},{9,8},{10,9... | collective-permute-start | bytes 1572872 | tf_op jit(solution)/shard_map/ppermute | solution.py:200
  20.7 62.8 %collective-permute-start.1 = (s32[8,128,128]{2,1,0:T(8,128)}, s32[8,128,128]{2,1,0:T(8,128)}, u32[]{:S(2)}, u32[]{:S(2)}) collective-permute-start(s32[8,128,128]{2,1,0:T(8,128)} %get-tuple-element.9), channel_id=1, source_target_pairs={{0,2},{1,3},{2,0},{3,1},{4,6},{5,7},{6,4},{7,5},{8,10},{9,11},{10,... | collective-permute-start | bytes 1572872 | tf_op jit(solution)/shard_map/ppermute | solution.py:200
  21.3 62.3 %collective-permute-start.2 = (s32[8,128,128]{2,1,0:T(8,128)}, s32[8,128,128]{2,1,0:T(8,128)}, u32[]{:S(2)}, u32[]{:S(2)}) collective-permute-start(s32[8,128,128]{2,1,0:T(8,128)} %get-tuple-element.8), channel_id=1, source_target_pairs={{0,1},{1,2},{2,3},{3,0},{4,5},{5,6},{6,7},{7,4},{8,9},{9,10},{10,1... | collective-permute-start | bytes 1572872 | tf_op jit(solution)/shard_map/ppermute | solution.py:200
  64.1 1.3 copy-start
  65.4 98.0 %all-to-all-start = ((f32[256,16,128]{2,1,0:T(8,128)}), f32[256,16,128]{2,1,0:T(8,128)}, u32[]{:S(2)}, u32[]{:S(2)}) async-start(f32[256,16,128]{2,1,0:T(8,128)} %bitcast.77), calls=%async_computation | async-start | bytes 4194304 | tf_op jit(solution)/shard_map/all_to_all | solution.py:279
  84.9 42.6 %collective-permute-start.3 = (s32[4,128,128]{2,1,0:T(8,128)S(1)}, s32[4,128,128]{2,1,0:T(8,128)S(1)}, u32[]{:S(2)}, u32[]{:S(2)}) collective-permute-start(s32[4,128,128]{2,1,0:T(8,128)S(1)} %dynamic-slice_bitcast_fusion.3), channel_id=1, source_target_pairs={{0,4},{1,5},{2,6},{3,7},{4,0},{5,1},{6,2},{7,3},{8,12},{9,13},{10,... | collective-permute-start | bytes 786440 | tf_op jit(solution)/shard_map/ppermute | solution.py:207
  127.6 9.0 %collective-permute-start.4 = (s32[2,128,128]{2,1,0:T(8,128)S(1)}, s32[2,128,128]{2,1,0:T(8,128)S(1)}, u32[]{:S(2)}, u32[]{:S(2)}) collective-permute-start(s32[2,128,128]{2,1,0:T(8,128)S(1)} %dynamic-slice_bitcast_fusion.4), channel_id=1, source_target_pairs={{0,8},{1,9},{2,10},{3,11},{4,12},{5,13},{6,14},{7,15},{8,0},{9,1},... | collective-permute-start | bytes 393224 | tf_op jit(solution)/shard_map/ppermute | solution.py:207
  136.7 7.3 %collective-permute-start.5 = (s32[1,128,128]{2,1,0:T(8,128)S(1)}, s32[1,128,128]{2,1,0:T(8,128)S(1)}, u32[]{:S(2)}, u32[]{:S(2)}) collective-permute-start(s32[1,128,128]{2,1,0:T(8,128)S(1)} %constant_dynamic-slice_fusion.2), channel_id=1, source_target_pairs={{0,16},{1,17},{2,18},{3,19},{4,20},{5,21},{6,22},{7,23},{8,24},{9,... | collective-permute-start | bytes 196616 | tf_op jit(solution)/shard_map/ppermute | solution.py:207
  173.7 14.2 %copy-start.3 = (s32[64]{0:T(128)S(1)}, s32[64]{0:T(128)}, u32[]{:S(2)}) copy-start(s32[64]{0:T(128)} %param.17) | copy-start | bytes 772
  173.7 67.8 %all-to-all-start.2 = ((f32[256,16,128]{2,1,0:T(8,128)}), f32[256,16,128]{2,1,0:T(8,128)S(1)}, u32[]{:S(2)}, u32[]{:S(2)}) async-start(f32[256,16,128]{2,1,0:T(8,128)} %bitcast.79), calls=%async_computation.2 | async-start | bytes 4194304 | tf_op jit(solution)/shard_map/all_to_all | solution.py:312
  241.5 1.4 copy-start.1

commit v4 on v2

v4 whole, which is shorter than its diff:
```python
import math

import jax
import jax.numpy as jnp
import numpy as np
from jax import lax
from jax.experimental import pallas as pl
from jax.experimental.pallas import tpu as pltpu
from jax.sharding import PartitionSpec as P

BLOCK = 128
HALF = BLOCK // 2
WIDTH = 4
VMEM_BYTES = 56 * 1024 * 1024


def half_tables(order):
    place = np.arange(order // 2)
    parts = []
    for rows in (2 * place, 2 * place + 1):
        angle = (rows[:, None] * place[None, :] % order).astype(np.float64) * (2.0 * math.pi / order)
        parts.append(((np.cos(angle) + np.sin(angle)) / math.sqrt(order)).astype(np.float32))
    parts.append(parts[1].T)
    pairs = []
    for part in parts:
        high = part.astype(jnp.bfloat16)
        pairs += [high, (part - high.astype(np.float32)).astype(jnp.bfloat16)]
    return np.stack(pairs)


def split(value):
    high = value.astype(jnp.bfloat16)
    low = (value - high.astype(jnp.float32)).astype(jnp.bfloat16)
    return high, low


def product(left, right, contract=((1,), (0,))):
    left_high, left_low = left
    right_high, right_low = right
    dot = lambda a, b: lax.dot_general(a, b, (contract, ((), ())), preferred_element_type=jnp.float32)
    return dot(left_high, right_high) + (dot(left_high, right_low) + dot(left_low, right_high))


def first_half(shape):
    return lax.broadcasted_iota(jnp.int32, shape, len(shape) - 1) % BLOCK < HALF


def swap_halves(value):
    return pltpu.roll(value, HALF, axis=1)


def live_amplitude(first, amplitude):
    rows = lax.broadcasted_iota(jnp.int32, amplitude.shape, 0)
    cols = lax.broadcasted_iota(jnp.int32, amplitude.shape, 1)
    return jnp.where(rows + cols + first == 0, 0.0, amplitude.astype(jnp.float32))


def table_pairs(tables_ref):
    return [(tables_ref[2 * n], tables_ref[2 * n + 1]) for n in range(3)]


def fold(value, axis):
    left, right = jnp.split(value, 2, axis=axis)
    return left + right, left - right


def unfold(even, odd, axis):
    return jnp.concatenate([even + odd, even - odd], axis=axis)


def synthesis_kernel(first_ref, white_ref, amplitude_ref, tables_ref, out_ref, weighted_ref):
    even_table, odd_table, _ = table_pairs(tables_ref)
    tiles, size, _ = weighted_ref.shape
    weighted = live_amplitude(first_ref[0] + pl.program_id(0), amplitude_ref[0]) * white_ref[0]
    for tile in range(tiles):
        weighted_ref[tile] = weighted[:, tile * BLOCK : (tile + 1) * BLOCK]
    transposed = ((1,), (1,))
    passed = []
    for parity in range(2):
        rows = [weighted_ref[tile, pl.ds(parity, size // 2, stride=2), :] for tile in range(tiles)]
        total, change = fold(jnp.concatenate(rows, axis=1), 1)
        passed.append(
            (product(even_table, split(total), transposed), product(odd_table, split(change), transposed))
        )
    lower, upper = (
        unfold(product(split(passed[0][k]), even_table), product(split(passed[1][k]), odd_table), 1)
        for k in range(2)
    )
    groups = out_ref.shape[1]
    for pair in range(out_ref.shape[0] // 2):
        left = lower[:, pair * BLOCK : (pair + 1) * BLOCK]
        right = swap_halves(upper[:, pair * BLOCK : (pair + 1) * BLOCK])
        mask = first_half(left.shape)
        out_ref[2 * pair, :, 0] = jnp.where(mask, left, right).reshape(groups, -1, BLOCK)
        out_ref[2 * pair + 1, :, 0] = jnp.where(mask, right, left).reshape(groups, -1, BLOCK)


def shell_kernel(field_ref, galaxy_ref, bias_ref, density_ref, tables_ref, out_ref):
    even_table, odd_table, odd_transposed = table_pairs(tables_ref)
    half_z = tables_ref.shape[1]
    rows_y = field_ref.shape[0] // (2 * half_z)
    for step in range(rows_y // 2):
        fields = [
            jnp.concatenate(
                [
                    field_ref[pl.ds(parity * rows_y + 2 * step + k, half_z, stride=2 * rows_y), :]
                    for k in range(2)
                ],
                axis=1,
            )
            for parity in range(2)
        ]
        contrast = unfold(product(even_table, split(fields[0])), product(odd_transposed, split(fields[1])), 0)
        span = slice(2 * step * BLOCK, 2 * (step + 1) * BLOCK)
        grads = []
        for quarter in range(2 * half_z // BLOCK):
            depth = slice(quarter * BLOCK, (quarter + 1) * BLOCK)
            bias = bias_ref[quarter : quarter + 1, span]
            density = density_ref[quarter : quarter + 1, span]
            grads.append(bias * (galaxy_ref[depth, span] - density * jnp.exp(bias * contrast[depth])))
        total, change = fold(jnp.concatenate(grads, axis=0), 0)
        for parity, back in enumerate([product(even_table, split(total)), product(odd_table, split(change))]):
            for k in range(2):
                row = pl.ds(parity * rows_y + 2 * step + k, half_z, stride=2 * rows_y)
                out_ref[row, :] = back[:, k * BLOCK : (k + 1) * BLOCK]


def analysis_kernel(
    first_ref, step_ref, field_ref, white_ref, amplitude_ref, kick_ref, tables_ref, grad_ref, next_ref, back_ref
):
    even_table, odd_table, _ = table_pairs(tables_ref)
    tiles, size, _ = back_ref.shape
    lower, upper = [], []
    for pair in range(field_ref.shape[0] // 2):
        left = field_ref[2 * pair, :, 0].reshape(-1, BLOCK)
        right = field_ref[2 * pair + 1, :, 0].reshape(-1, BLOCK)
        mask = first_half(left.shape)
        lower.append(jnp.where(mask, left, right))
        upper.append(swap_halves(jnp.where(mask, right, left)))
    transposed = ((1,), (1,))
    folded = [fold(jnp.concatenate(part, axis=1), 1) for part in (lower, upper)]
    for parity, table in enumerate([even_table, odd_table]):
        passed = [split(product(table, split(part[parity]), transposed)) for part in folded]
        back = unfold(product(passed[0], even_table), product(passed[1], odd_table), 1)
        for tile in range(tiles):
            rows = pl.ds(parity, size // 2, stride=2)
            back_ref[tile, rows, :] = back[:, tile * BLOCK : (tile + 1) * BLOCK]
    back = jnp.concatenate([back_ref[tile] for tile in range(tiles)], axis=1)
    white = white_ref[0]
    gradient = live_amplitude(first_ref[0] + pl.program_id(0), amplitude_ref[0]) * back - white
    grad_ref[0] = gradient
    next_ref[0] = white + step_ref[0] * gradient + step_ref[1] * kick_ref[0].astype(jnp.float32)


def adapted_step(accepted):
    powers = jnp.power(
        jnp.float32(0.9), jnp.arange(accepted.shape[0], dtype=jnp.int32).astype(jnp.float32)
    )
    accept_rate = jnp.float32(0.1) * jnp.sum(accepted.astype(jnp.float32) * powers)
    return jnp.float32(0.02) * jnp.exp(jnp.float32(2.0) * (accept_rate - jnp.float32(0.574)))


def heavy_ranks(counts, keep, heavy, col_index, sent):
    size, capacity, block = counts.shape
    height = size // WIDTH
    parts = counts.reshape(height, WIDTH, capacity, block)
    at_z, at_x = col_index // WIDTH, col_index % WIDTH
    heavy_z, heavy_x = heavy // WIDTH, heavy % WIDTH

    def pick(array, axis, index):
        return lax.dynamic_index_in_dim(array, index, axis, keepdims=False)

    def column(index):
        part = lax.dynamic_slice(parts, (0, index, keep, 0), (height, 1, capacity - keep, block))
        return part.reshape(height, capacity - keep, block)

    mine = column(at_x)
    for shift in range(1, WIDTH):
        pairs = [(i, i // WIDTH * WIDTH + (i + shift) % WIDTH) for i in range(size)]
        arrived = lax.ppermute(column((at_x + shift) % WIDTH), "py", pairs)
        mine = jnp.where((at_x - heavy_x) % WIDTH == shift, arrived, mine)
    mine, sent = lax.optimization_barrier((mine, sent))
    low = 4
    mine = mine.reshape(height // low, low, capacity - keep, block)
    here = at_z % low
    away = here ^ (heavy_z % low)
    best = pick(mine, 1, here)
    for flip in range(1, low):
        pairs = [(i, i ^ (flip * WIDTH)) for i in range(size)]
        arrived = lax.ppermute(pick(mine, 1, here ^ flip), "py", pairs)
        best = jnp.where(away == flip, arrived, best)
    here = at_z // low
    away = (here - heavy_z // low) % (height // low)
    mine = pick(best, 0, here)
    for shift in range(1, height // low):
        pairs = [(i, (i + shift * low * WIDTH) % size) for i in range(size)]
        arrived = lax.ppermute(pick(best, 0, (here + shift) % (height // low)), "py", pairs)
        mine = jnp.where(away == shift, arrived, mine)
    return lax.optimization_barrier((mine, sent))


def solution(mesh):
    rows_px, rows_py = mesh.shape["px"], mesh.shape["py"]
    devices = rows_px * rows_py

    def body(
        white_noise, mode_amplitude, kick_noise, shell_owner, galaxy_counts, shell_bias, shell_density, accepted
    ):
        depth, size_x, size_y = white_noise.shape
        size_z = depth * devices
        span_x, span_y = size_x // rows_px, size_y // rows_py
        rows_y = span_y // 2
        quarters = size_z // BLOCK
        row_index = lax.axis_index("px")
        col_index = lax.axis_index("py")
        first = ((row_index * rows_py + col_index) * depth).reshape(1)

        tables = jnp.asarray(half_tables(size_x))

        galaxy_in = galaxy_counts[0, 0]
        blocks, capacity = shell_owner.shape[-1], galaxy_counts.shape[3]
        keep = -(-(-(-(blocks - capacity) // (rows_py - 1))) // 8) * 8
        owner_list = shell_owner.reshape(-1)
        peers = jnp.arange(rows_py, dtype=jnp.int32)
        onehot = owner_list[:, None] == peers[None, :]
        onehot_int = onehot.astype(jnp.int32)
        rank_index = jnp.sum(jnp.cumsum(onehot_int, axis=0) * onehot_int, axis=1) - 1
        heavy = jnp.argmax(jnp.sum(onehot_int, axis=0)).astype(jnp.int32)
        slot_index = jnp.where(
            rank_index < keep, owner_list * keep + rank_index, rows_py * keep + rank_index - keep
        )
        counts = lax.all_to_all(galaxy_in[:, :keep], "py", split_axis=0, concat_axis=0, tiled=True)
        bias_row = lax.dynamic_index_in_dim(shell_bias, row_index, 0, keepdims=False)
        density_row = lax.dynamic_index_in_dim(shell_density, row_index, 0, keepdims=False)

        def by_column(blocks):
            grid = blocks.reshape(span_x, rows_y, 2, quarters)
            grid = jnp.where(row_index % 2 == 0, grid, grid[:, :, ::-1])
            return grid.transpose(3, 1, 2, 0).reshape(quarters, -1)

        slot_grid = by_column(slot_index)
        owner_grid = by_column(owner_list)
        hit = owner_grid[:, :, None] == peers
        bias_grid = jnp.sum(jnp.where(hit, bias_row, 0.0), axis=-1)
        density_grid = jnp.sum(jnp.where(hit, density_row, 0.0), axis=-1)

        whole = lambda array: pl.BlockSpec(array.shape, lambda i: (0,) * array.ndim)
        plane = pl.BlockSpec((1, size_x, size_y), lambda i: (i, 0, 0))
        scalar = pl.BlockSpec(memory_space=pltpu.SMEM)
        packed_shape = (rows_px, rows_py, depth, rows_y, BLOCK)
        packed = pl.BlockSpec((rows_px, rows_py, 1, rows_y, BLOCK), lambda i: (0, 0, i, 0, 0))
        tiled = pltpu.VMEM((size_y // BLOCK, size_x, BLOCK), jnp.float32)
        params = pltpu.CompilerParams(vmem_limit_bytes=VMEM_BYTES)

        flops = 3 * 2 * depth * size_x * size_y * size_x
        sent = pl.pallas_call(
            synthesis_kernel,
            grid=(depth,),
            in_specs=[scalar, plane, plane, whole(tables)],
            out_specs=packed,
            scratch_shapes=[tiled],
            out_shape=jax.ShapeDtypeStruct(packed_shape, jnp.float32),
            compiler_params=params,
            cost_estimate=pl.CostEstimate(flops=flops, bytes_accessed=8 * 2**20, transcendentals=0),
            name="synthesis",
        )(first, white_noise, mode_amplitude, tables)

        chunk = depth * rows_y
        extra, sent = heavy_ranks(galaxy_in, keep, heavy, col_index, sent)
        field = lax.all_to_all(
            sent.reshape(devices, chunk, BLOCK), ("px", "py"), split_axis=0, concat_axis=0, tiled=True
        )

        held = jnp.concatenate([counts.reshape(-1, BLOCK), extra], axis=0)
        picked = held.at[slot_grid.reshape(-1)].get(mode="promise_in_bounds")
        galaxy = picked.reshape(quarters, -1, BLOCK).transpose(0, 2, 1).reshape(size_z, -1).astype(jnp.float32)

        cells = (size_z * rows_y, BLOCK)
        back = pl.pallas_call(
            shell_kernel,
            out_shape=jax.ShapeDtypeStruct(cells, jnp.float32),
            compiler_params=params,
            cost_estimate=pl.CostEstimate(flops=flops, bytes_accessed=8 * 2**20, transcendentals=size_z * 1024),
            name="shell_gradient",
        )(field.reshape(cells), galaxy, bias_grid, density_grid, tables)

        returned = lax.all_to_all(
            back.reshape(devices, chunk, BLOCK), ("px", "py"), split_axis=0, concat_axis=0, tiled=True
        )
        step_size = adapted_step(accepted)
        steps = jnp.stack([step_size, jnp.sqrt(2.0 * step_size)])
        out_plane = jax.ShapeDtypeStruct(white_noise.shape, jnp.float32)
        return pl.pallas_call(
            analysis_kernel,
            grid=(depth,),
            in_specs=[scalar, scalar, packed, plane, plane, plane, whole(tables)],
            out_specs=(plane, plane),
            out_shape=(out_plane, out_plane),
            scratch_shapes=[tiled],
            compiler_params=params,
            cost_estimate=pl.CostEstimate(flops=flops, bytes_accessed=12 * 2**20, transcendentals=0),
            name="analysis",
        )(first, steps, returned.reshape(packed_shape), white_noise, mode_amplitude, kick_noise, tables)

    modes = P(("px", "py"), None, None)
    return jax.shard_map(
        body,
        mesh=mesh,
        in_specs=(modes, modes, modes, P("px", "py", None), P("px", "py", None, None, None), P(), P(), P()),
        out_specs=(modes, modes),
        check_vma=False,
    )
```

time: 236 us -> 232 us (0.983)
  waiting for transfers between devices: 116 us -> 106 us
  starting transfers between devices: 44.3 us -> 48.8 us
  Pallas kernels: 24.2 us -> 20.4 us
  local copies, waits for them, and re-layouts: 28.8 us -> 32.6 us
    all_to_all x1, starting transfers between devices: 10 us -> 17.7 us  [body(): lax.all_to_all(sent.reshape(devices, chunk, BLOCK), ('px', 'py'), split_a...]
    ppermute x3, waiting for transfers between devices: 27.9 us -> 22.2 us  [heavy_ranks(): arrived = lax.ppermute(column((at_x + shift) % WIDTH), 'py', pairs)]
    all_to_all x1, waiting for transfers between devices: 27.9 us -> 23.3 us  [body(): lax.all_to_all(sent.reshape(devices, chunk, BLOCK), ('px', 'py'), split_a...]
    ppermute x3 -> x4, starting transfers between devices: 11.7 us -> 8.58 us  [the longest x1 4.94 us: heavy_ranks(): lax.ppermute(pick(best, 0, (here + shift) % (height // low)), 'py', pairs)]
    rev x0 -> x2, local copies, waits for them, and re-layouts: none -> 2.62 us  [by_column(): grid = jnp.where(row_index % 2 == 0, grid, grid[:, :, ::-1])]
    ppermute x3 -> x4, waiting for transfers between devices: 8.21 us -> 8.65 us  [the longest x3 6.38 us: heavy_ranks(): arrived = lax.ppermute(pick(mine, 1, here ^ flip), 'py', pairs)]
  transfers between devices with their start and end apart: 9 -> 10, of which waited for: 6 -> 7; matrix products, arithmetic and copies ran while one was open for 18% -> 20% of each run, Pallas kernels for 3% -> 2%
where the time goes in v4:
time: 232 us; the launch traced here: 231 us
  waiting for transfers between devices  106 us (46%)
  starting transfers between devices  48.8 us (21%)
  local copies, waits for them, and re-layouts  32.6 us (14%)
  Pallas kernels  20.4 us (9%)
  other arithmetic  19.3 us (8%)
  between operations  4.33 us (2%)
    all_to_all x1, waiting for transfers between devices, body(): lax.all_to_all(back.reshape(devices, chunk, BLOCK), ('px', 'py'), split_a...  51.7 us
    all_to_all x1, waiting for transfers between devices, body(): lax.all_to_all(sent.reshape(devices, chunk, BLOCK), ('px', 'py'), split_a...  23.3 us
    ppermute x3, waiting for transfers between devices, heavy_ranks(): arrived = lax.ppermute(column((at_x + shift) % WIDTH), 'py', pairs)  22.2 us
    all_to_all x1, starting transfers between devices, body(): lax.all_to_all(sent.reshape(devices, chunk, BLOCK), ('px', 'py'), split_a...  17.7 us
    gather x1, local copies, waits for them, and re-layouts, body(): picked = held.at[slot_grid.reshape(-1)].get(mode='promise_in_bounds')  14.2 us
    all_to_all x1, starting transfers between devices, body(): lax.all_to_all(galaxy_in[:, :keep], 'py', split_axis=0, concat_axis=0, ti...  11.9 us
    another operation x3, other arithmetic  9.62 us
    pallas_call x1, Pallas kernels, body(): pl.pallas_call(analysis_kernel, grid=(depth,), in_specs=[scalar, scalar,...  7.58 us
  transfers between devices with their start and end apart: 10, of which 7 were waited for; matrix products, arithmetic and copies ran while one was open for 20% of the time, Pallas kernels for 2%

profile of v4, /device:TPU:1, one launch (start us, length us, event | category | flops | bytes accessed | tf_op | source)
XLA Modules:
  0.0 231.2 jit_solution(70510841987180473)
XLA Ops:
  0.6 3.1 %slice.14 = s32[32,128,128]{2,1,0:T(8,128)} slice(s32[32,256,128]{2,1,0:T(8,128)} %bitcast.81), slice={[0:32], [0:128], [0:128]} | slice | bytes 4194304 | tf_op jit(solution)/shard_map/slice | solution.py:232
  3.8 11.9 %all-to-all-start.1 = ((s32[32,128,128]{2,1,0:T(8,128)}), s32[32,128,128]{2,1,0:T(8,128)S(1)}, u32[]{:S(2)}, u32[]{:S(2)}) async-start(s32[32,128,128]{2,1,0:T(8,128)} %slice.14), calls=%async_computation.1 | async-start | bytes 4194304 | tf_op jit(solution)/shard_map/all_to_all | solution.py:232
  15.7 2.6 %dynamic-slice_bitcast_fusion = (s32[8,128,128]{2,1,0:T(8,128)}, s32[8,128,128]{2,1,0:T(8,128)}, s32[8,128,128]{2,1,0:T(8,128)}) fusion(s32[8,4,256,128]{3,2,1,0:T(8,128)} %bitcast.82, s32[]{:T(128)S(6)} %select_n.209, s32[]{:T(128)S(6)} %select_n.206, s32[]{:T(128)S(6)} %select_n.203), kind=kLoop, calls=%fused_computation.16 | loop fusion | bytes 3145740 | tf_op jit(solution)/shard_map/reshape | solution.py:175
  19.5 2.4 %collective-permute-start.1 = (s32[8,128,128]{2,1,0:T(8,128)}, s32[8,128,128]{2,1,0:T(8,128)}, u32[]{:S(2)}, u32[]{:S(2)}) collective-permute-start(s32[8,128,128]{2,1,0:T(8,128)} %get-tuple-element.17), channel_id=1, source_target_pairs={{0,2},{1,3},{2,0},{3,1},{4,6},{5,7},{6,4},{7,5},{8,10},{9,11},{10,... | collective-permute-start | bytes 1572872 | tf_op jit(solution)/shard_map/ppermute | solution.py:180
  23.2 9.2 %reduce-window.6 = s32[32,32,128]{2,1,0:T(8,128)S(1)} reduce-window(s32[32,32,128]{2,1,0:T(8,128)S(1)} %fusion.4, s32[]{:T(128)} %constant.164.clone.1), window={size=1x1x128 pad=0_0x0_0x127_0}, to_apply=%region_3.4 | reduce-window | flops 16646144 | bytes 1048580 | tf_op jit(solution)/shard_map/reduce-window
  36.7 5.6 %synthesis.1 = f32[8,32,2,8,128]{4,3,2,1,0:T(8,128)} custom-call(s32[1]{0:T(128)} %bitcast.first_ref, f32[2,512,512]{2,1,0:T(8,128)} %white_ref.3, bf16[2,512,512]{2,1,0:T(8,128)(2,1)} %amplitude_ref.3, bf16[6,256,256]{2,1,0:T(8,128)(2,1)} %constant.173.clone.tables_ref), custom_call_target="tpu_custom_call" | custom-call | flops 1610612736 | bytes 8388608 | tf_op jit(solution)/shard_map/synthesis/pallas_call | solution.py:256
  42.3 4.2 %collective-permute-done.2 = s32[8,128,128]{2,1,0:T(8,128)} collective-permute-done((s32[8,128,128]{2,1,0:T(8,128)}, s32[8,128,128]{2,1,0:T(8,128)}, u32[]{:S(2)}, u32[]{:S(2)}) %collective-permute-start.2) | collective-permute-done | bytes 524320 | tf_op jit(solution)/shard_map/ppermute | solution.py:180
  46.6 17.9 %collective-permute-done.1 = s32[8,128,128]{2,1,0:T(8,128)} collective-permute-done((s32[8,128,128]{2,1,0:T(8,128)}, s32[8,128,128]{2,1,0:T(8,128)}, u32[]{:S(2)}, u32[]{:S(2)}) %collective-permute-start.1) | collective-permute-done | bytes 524320 | tf_op jit(solution)/shard_map/ppermute | solution.py:180
  65.8 1.4 collective-permute-start.5
  67.3 1.8 collective-permute-start.4
  70.2 3.0 %collective-permute-done.4 = s32[2,128,128]{2,1,0:T(8,128)S(1)} collective-permute-done((s32[2,128,128]{2,1,0:T(8,128)S(1)}, s32[2,128,128]{2,1,0:T(8,128)S(1)}, u32[]{:S(2)}, u32[]{:S(2)}) %collective-permute-start.4) | collective-permute-done | bytes 131104 | tf_op jit(solution)/shard_map/ppermute | solution.py:190
  73.1 3.4 %collective-permute-done.3 = s32[2,128,128]{2,1,0:T(8,128)S(1)} collective-permute-done((s32[2,128,128]{2,1,0:T(8,128)S(1)}, s32[2,128,128]{2,1,0:T(8,128)S(1)}, u32[]{:S(2)}, u32[]{:S(2)}) %collective-permute-start.3) | collective-permute-done | bytes 131104 | tf_op jit(solution)/shard_map/ppermute | solution.py:190
  76.6 4.9 %collective-permute-start.6 = (s32[128,128]{1,0:T(8,128)S(1)}, s32[128,128]{1,0:T(8,128)S(1)}, u32[]{:S(2)}, u32[]{:S(2)}) collective-permute-start(s32[128,128]{1,0:T(8,128)S(1)} %dynamic-slice_bitcast_fusion.6), channel_id=1, source_target_pairs={{0,16},{1,17},{2,18},{3,19},{4,20},{5,21},{6,22},{7,23},{8,24},{9,... | collective-permute-start | bytes 196616 | tf_op jit(solution)/shard_map/ppermute | solution.py:197
  81.5 2.3 collective-permute-done.6
  85.2 17.7 %all-to-all-start = ((f32[256,16,128]{2,1,0:T(8,128)}), f32[256,16,128]{2,1,0:T(8,128)}, u32[]{:S(2)}, u32[]{:S(2)}) async-start(f32[256,16,128]{2,1,0:T(8,128)} %bitcast.16), calls=%async_computation | async-start | bytes 4194304 | tf_op jit(solution)/shard_map/all_to_all | solution.py:270
  112.8 1.7 pad_add_fusion
  114.6 14.2 %gather_fusion = s32[4096,128]{1,0:T(8,128)} fusion(s32[4224,128]{1,0:T(8,128)S(1)} %pad_add_fusion, s32[4096]{0:T(1024)S(1)} %broadcast_clamp_fusion), kind=kCustom, calls=%fused_computation | custom fusion | bytes 4210688 | tf_op jit(solution)/shard_map/gather | solution.py:275
  128.8 1.7 convert_element_type.26
  130.5 1.8 copy.24
  132.3 23.3 %all-to-all-done = f32[256,16,128]{2,1,0:T(8,128)} async-done(((f32[256,16,128]{2,1,0:T(8,128)}), f32[256,16,128]{2,1,0:T(8,128)}, u32[]{:S(2)}, u32[]{:S(2)}) %all-to-all-start) | async-done | bytes 2097184 | tf_op jit(solution)/shard_map/all_to_all | solution.py:270
  155.6 7.1 %shell_gradient.1 = f32[4096,128]{1,0:T(8,128)} custom-call(f32[4096,128]{1,0:T(8,128)} %bitcast.17.field_ref, f32[512,1024]{1,0:T(8,128)} %bitcast.77, f32[4,1024]{1,0:T(4,128)} %get-tuple-element.13.bias_ref, f32[4,1024]{1,0:T(4,128)} %get-tuple-element.12.density_ref, bf16[6,256,256]{2,1,0:T(8,128)(2,1)} %constant.173.clone.tables_ref), custom_call_target="tpu_custom_call" | custom-call | flops 1610612736 | bytes 8388608 | tf_op jit(solution)/shard_map/shell_gradient/pallas_call | solution.py:279
  162.8 5.9 %all-to-all-start.2 = ((f32[256,16,128]{2,1,0:T(8,128)}), f32[256,16,128]{2,1,0:T(8,128)S(1)}, u32[]{:S(2)}, u32[]{:S(2)}) async-start(f32[256,16,128]{2,1,0:T(8,128)} %bitcast.76), calls=%async_computation.2 | async-start | bytes 4194304 | tf_op jit(solution)/shard_map/all_to_all | solution.py:287
  170.6 51.7 %all-to-all-done.2 = f32[256,16,128]{2,1,0:T(8,128)S(1)} async-done(((f32[256,16,128]{2,1,0:T(8,128)}), f32[256,16,128]{2,1,0:T(8,128)S(1)}, u32[]{:S(2)}, u32[]{:S(2)}) %all-to-all-start.2) | async-done | bytes 2097184 | tf_op jit(solution)/shard_map/all_to_all | solution.py:287
  223.7 7.6 %analysis.1 = (f32[2,512,512]{2,1,0:T(8,128)}, f32[2,512,512]{2,1,0:T(8,128)}) custom-call(s32[1]{0:T(128)} %bitcast.first_ref, f32[2]{0:T(128)} %pad_maximum_fusion.step_ref, f32[8,32,2,8,128]{4,3,2,1,0:T(8,128)} %bitcast.80, f32[2,512,512]{2,1,0:T(8,128)} %white_ref.3, bf16[2,512,512]{2,1,0:T(8,128)(2,1)} %amplitude_ref.3, bf16[2,512,512]{2,1,0:T(8,128)(2,1)} %kick_ref.1, ...), custom_call_target="tpu_custom_call" | custom-call | flops 1610612736 | bytes 12582912 | tf_op jit(solution)/shard_map/analysis/pallas_call | solution.py:293
  (45 shorter events, 20.2 us)
Async XLA Ops:
  3.8 80.1 %all-to-all-start.1 = ((s32[32,128,128]{2,1,0:T(8,128)}), s32[32,128,128]{2,1,0:T(8,128)S(1)}, u32[]{:S(2)}, u32[]{:S(2)}) async-start(s32[32,128,128]{2,1,0:T(8,128)} %slice.14), calls=%async_computation.1 | async-start | bytes 4194304 | tf_op jit(solution)/shard_map/all_to_all | solution.py:232
  15.6 7.5 %copy-start.2 = (s32[1,1,4096]{2,1,0:T(1,128)S(1)}, s32[1,1,4096]{2,1,0:T(1,128)}, u32[]{:S(2)}) copy-start(s32[1,1,4096]{2,1,0:T(1,128)} %param.12) | copy-start | bytes 49156
  18.3 28.3 %collective-permute-start.2 = (s32[8,128,128]{2,1,0:T(8,128)}, s32[8,128,128]{2,1,0:T(8,128)}, u32[]{:S(2)}, u32[]{:S(2)}) collective-permute-start(s32[8,128,128]{2,1,0:T(8,128)} %get-tuple-element.16), channel_id=1, source_target_pairs={{0,1},{1,2},{2,3},{3,0},{4,5},{5,6},{6,7},{7,4},{8,9},{9,10},{10,1... | collective-permute-start | bytes 1572872 | tf_op jit(solution)/shard_map/ppermute | solution.py:180
  19.5 45.0 %collective-permute-start.1 = (s32[8,128,128]{2,1,0:T(8,128)}, s32[8,128,128]{2,1,0:T(8,128)}, u32[]{:S(2)}, u32[]{:S(2)}) collective-permute-start(s32[8,128,128]{2,1,0:T(8,128)} %get-tuple-element.17), channel_id=1, source_target_pairs={{0,2},{1,3},{2,0},{3,1},{4,6},{5,7},{6,4},{7,5},{8,10},{9,11},{10,... | collective-permute-start | bytes 1572872 | tf_op jit(solution)/shard_map/ppermute | solution.py:180
  21.9 42.6 %collective-permute-start = (s32[8,128,128]{2,1,0:T(8,128)}, s32[8,128,128]{2,1,0:T(8,128)}, u32[]{:S(2)}, u32[]{:S(2)}) collective-permute-start(s32[8,128,128]{2,1,0:T(8,128)} %get-tuple-element.18), channel_id=1, source_target_pairs={{0,3},{1,0},{2,1},{3,2},{4,7},{5,4},{6,5},{7,6},{8,11},{9,8},{10,9... | collective-permute-start | bytes 1572872 | tf_op jit(solution)/shard_map/ppermute | solution.py:180
  65.8 4.3 %collective-permute-start.5 = (s32[2,128,128]{2,1,0:T(8,128)S(1)}, s32[2,128,128]{2,1,0:T(8,128)S(1)}, u32[]{:S(2)}, u32[]{:S(2)}) collective-permute-start(s32[2,128,128]{2,1,0:T(8,128)S(1)} %get-tuple-element.21), channel_id=1, source_target_pairs={{0,4},{1,5},{2,6},{3,7},{4,0},{5,1},{6,2},{7,3},{8,12},{9,13},{10,... | collective-permute-start | bytes 393224 | tf_op jit(solution)/shard_map/ppermute | solution.py:190
  67.3 5.9 %collective-permute-start.4 = (s32[2,128,128]{2,1,0:T(8,128)S(1)}, s32[2,128,128]{2,1,0:T(8,128)S(1)}, u32[]{:S(2)}, u32[]{:S(2)}) collective-permute-start(s32[2,128,128]{2,1,0:T(8,128)S(1)} %get-tuple-element.22), channel_id=1, source_target_pairs={{0,8},{1,9},{2,10},{3,11},{4,12},{5,13},{6,14},{7,15},{8,0},{9,1},... | collective-permute-start | bytes 393224 | tf_op jit(solution)/shard_map/ppermute | solution.py:190
  69.1 7.4 %collective-permute-start.3 = (s32[2,128,128]{2,1,0:T(8,128)S(1)}, s32[2,128,128]{2,1,0:T(8,128)S(1)}, u32[]{:S(2)}, u32[]{:S(2)}) collective-permute-start(s32[2,128,128]{2,1,0:T(8,128)S(1)} %get-tuple-element.23), channel_id=1, source_target_pairs={{0,12},{1,13},{2,14},{3,15},{4,8},{5,9},{6,10},{7,11},{8,4},{9,5},... | collective-permute-start | bytes 393224 | tf_op jit(solution)/shard_map/ppermute | solution.py:190
  76.6 7.2 %collective-permute-start.6 = (s32[128,128]{1,0:T(8,128)S(1)}, s32[128,128]{1,0:T(8,128)S(1)}, u32[]{:S(2)}, u32[]{:S(2)}) collective-permute-start(s32[128,128]{1,0:T(8,128)S(1)} %dynamic-slice_bitcast_fusion.6), channel_id=1, source_target_pairs={{0,16},{1,17},{2,18},{3,19},{4,20},{5,21},{6,22},{7,23},{8,24},{9,... | collective-permute-start | bytes 196616 | tf_op jit(solution)/shard_map/ppermute | solution.py:197
  83.8 1.3 copy-start
  85.2 70.5 %all-to-all-start = ((f32[256,16,128]{2,1,0:T(8,128)}), f32[256,16,128]{2,1,0:T(8,128)}, u32[]{:S(2)}, u32[]{:S(2)}) async-start(f32[256,16,128]{2,1,0:T(8,128)} %bitcast.16), calls=%async_computation | async-start | bytes 4194304 | tf_op jit(solution)/shard_map/all_to_all | solution.py:270
  162.8 5.9 %copy-start.3 = (s32[64]{0:T(128)S(1)}, s32[64]{0:T(128)}, u32[]{:S(2)}) copy-start(s32[64]{0:T(128)} %param.16) | copy-start | bytes 772
  162.8 59.5 %all-to-all-start.2 = ((f32[256,16,128]{2,1,0:T(8,128)}), f32[256,16,128]{2,1,0:T(8,128)S(1)}, u32[]{:S(2)}, u32[]{:S(2)}) async-start(f32[256,16,128]{2,1,0:T(8,128)} %bitcast.76), calls=%async_computation.2 | async-start | bytes 4194304 | tf_op jit(solution)/shard_map/all_to_all | solution.py:287
  222.3 1.4 copy-start.1

commit v5 on v4

--- a/solution.py
+++ b/solution.py
@@ -11,6 +11,7 @@
 BLOCK = 128
 HALF = BLOCK // 2
 WIDTH = 4
+GROUP = 64
 VMEM_BYTES = 56 * 1024 * 1024
 
 
@@ -95,8 +96,8 @@
         out_ref[2 * pair + 1, :, 0] = jnp.where(mask, right, left).reshape(groups, -1, BLOCK)
 
 
-def shell_kernel(field_ref, galaxy_ref, bias_ref, density_ref, tables_ref, out_ref):
-    even_table, odd_table, odd_transposed = table_pairs(tables_ref)
+def expected_kernel(field_ref, bias_ref, density_ref, tables_ref, out_ref):
+    even_table, _, odd_transposed = table_pairs(tables_ref)
     half_z = tables_ref.shape[1]
     rows_y = field_ref.shape[0] // (2 * half_z)
     for step in range(rows_y // 2):
@@ -112,12 +113,41 @@
         ]
         contrast = unfold(product(even_table, split(fields[0])), product(odd_transposed, split(fields[1])), 0)
         span = slice(2 * step * BLOCK, 2 * (step + 1) * BLOCK)
-        grads = []
         for quarter in range(2 * half_z // BLOCK):
             depth = slice(quarter * BLOCK, (quarter + 1) * BLOCK)
             bias = bias_ref[quarter : quarter + 1, span]
             density = density_ref[quarter : quarter + 1, span]
-            grads.append(bias * (galaxy_ref[depth, span] - density * jnp.exp(bias * contrast[depth])))
+            out_ref[depth, span] = bias * (density * jnp.exp(bias * contrast[depth]))
+
+
+def gradient_kernel(
+    slot_ref, counts_ref, bias_ref, expected_any, tables_ref, out_ref, rows_ref, expected_ref, sem
+):
+    load = pltpu.make_async_copy(expected_any, expected_ref, sem)
+    load.start()
+
+    def gather(group, carry):
+        base = pl.multiple_of(group * GROUP, GROUP)
+        for k in range(GROUP):
+            rows_ref[pl.ds(base + k, 1), :] = counts_ref[pl.ds(slot_ref[base + k], 1), :]
+        return carry
+
+    lax.fori_loop(0, rows_ref.shape[0] // GROUP, gather, 0)
+    load.wait()
+    even_table, odd_table, _ = table_pairs(tables_ref)
+    half_z = tables_ref.shape[1]
+    rows_y = out_ref.shape[0] // (2 * half_z)
+    columns = expected_ref.shape[1]
+    for step in range(rows_y // 2):
+        span = slice(2 * step * BLOCK, 2 * (step + 1) * BLOCK)
+        grads = []
+        for quarter in range(2 * half_z // BLOCK):
+            depth = slice(quarter * BLOCK, (quarter + 1) * BLOCK)
+            starts = [quarter * columns + (2 * step + k) * BLOCK for k in range(2)]
+            galaxy = jnp.concatenate(
+                [rows_ref[start : start + BLOCK, :].astype(jnp.float32).T for start in starts], axis=1
+            )
+            grads.append(bias_ref[quarter : quarter + 1, span] * galaxy - expected_ref[depth, span])
         total, change = fold(jnp.concatenate(grads, axis=0), 0)
         for parity, back in enumerate([product(even_table, split(total)), product(odd_table, split(change))]):
             for k in range(2):
@@ -160,43 +190,16 @@
     return jnp.float32(0.02) * jnp.exp(jnp.float32(2.0) * (accept_rate - jnp.float32(0.574)))
 
 
-def heavy_ranks(counts, keep, heavy, col_index, sent):
-    size, capacity, block = counts.shape
-    height = size // WIDTH
-    parts = counts.reshape(height, WIDTH, capacity, block)
-    at_z, at_x = col_index // WIDTH, col_index % WIDTH
-    heavy_z, heavy_x = heavy // WIDTH, heavy % WIDTH
-
-    def pick(array, axis, index):
-        return lax.dynamic_index_in_dim(array, index, axis, keepdims=False)
-
-    def column(index):
-        part = lax.dynamic_slice(parts, (0, index, keep, 0), (height, 1, capacity - keep, block))
-        return part.reshape(height, capacity - keep, block)
-
-    mine = column(at_x)
+def spread_ranks(counts, keep, heavy, col_index):
+    size, capacity, _ = counts.shape
+    width = (capacity - keep) // WIDTH
+    away = (col_index - heavy) % WIDTH
+    part = lambda k: counts[:, keep + k * width : keep + (k + 1) * width]
+    mine = part(0)
     for shift in range(1, WIDTH):
         pairs = [(i, i // WIDTH * WIDTH + (i + shift) % WIDTH) for i in range(size)]
-        arrived = lax.ppermute(column((at_x + shift) % WIDTH), "py", pairs)
-        mine = jnp.where((at_x - heavy_x) % WIDTH == shift, arrived, mine)
-    mine, sent = lax.optimization_barrier((mine, sent))
-    low = 4
-    mine = mine.reshape(height // low, low, capacity - keep, block)
-    here = at_z % low
-    away = here ^ (heavy_z % low)
-    best = pick(mine, 1, here)
-    for flip in range(1, low):
-        pairs = [(i, i ^ (flip * WIDTH)) for i in range(size)]
-        arrived = lax.ppermute(pick(mine, 1, here ^ flip), "py", pairs)
-        best = jnp.where(away == flip, arrived, best)
-    here = at_z // low
-    away = (here - heavy_z // low) % (height // low)
-    mine = pick(best, 0, here)
-    for shift in range(1, height // low):
-        pairs = [(i, (i + shift * low * WIDTH) % size) for i in range(size)]
-        arrived = lax.ppermute(pick(best, 0, (here + shift) % (height // low)), "py", pairs)
-        mine = jnp.where(away == shift, arrived, mine)
-    return lax.optimization_barrier((mine, sent))
+        mine = jnp.where(away == shift, lax.ppermute(part(shift), "py", pairs), mine)
+    return mine
 
 
 def solution(mesh):
@@ -226,10 +229,14 @@
         onehot_int = onehot.astype(jnp.int32)
         rank_index = jnp.sum(jnp.cumsum(onehot_int, axis=0) * onehot_int, axis=1) - 1
         heavy = jnp.argmax(jnp.sum(onehot_int, axis=0)).astype(jnp.int32)
+        width = (capacity - keep) // WIDTH
+        place = rank_index - keep
+        holder = owner_list // WIDTH * WIDTH + (owner_list + place // width) % WIDTH
         slot_index = jnp.where(
-            rank_index < keep, owner_list * keep + rank_index, rows_py * keep + rank_index - keep
+            place < 0,
+            owner_list * (keep + width) + rank_index,
+            holder * (keep + width) + keep + place % width,
         )
-        counts = lax.all_to_all(galaxy_in[:, :keep], "py", split_axis=0, concat_axis=0, tiled=True)
         bias_row = lax.dynamic_index_in_dim(shell_bias, row_index, 0, keepdims=False)
         density_row = lax.dynamic_index_in_dim(shell_density, row_index, 0, keepdims=False)
 
@@ -266,23 +273,39 @@
         )(first, white_noise, mode_amplitude, tables)
 
         chunk = depth * rows_y
-        extra, sent = heavy_ranks(galaxy_in, keep, heavy, col_index, sent)
         field = lax.all_to_all(
             sent.reshape(devices, chunk, BLOCK), ("px", "py"), split_axis=0, concat_axis=0, tiled=True
         )
 
-        held = jnp.concatenate([counts.reshape(-1, BLOCK), extra], axis=0)
-        picked = held.at[slot_grid.reshape(-1)].get(mode="promise_in_bounds")
-        galaxy = picked.reshape(quarters, -1, BLOCK).transpose(0, 2, 1).reshape(size_z, -1).astype(jnp.float32)
+        outgoing = jnp.concatenate([galaxy_in[:, :keep], spread_ranks(galaxy_in, keep, heavy, col_index)], axis=1)
+        outgoing, field = lax.optimization_barrier((outgoing, field))
+        counts = lax.all_to_all(outgoing, "py", split_axis=0, concat_axis=0, tiled=True)
 
         cells = (size_z * rows_y, BLOCK)
+        columns = span_x * span_y
+        expected = pl.pallas_call(
+            expected_kernel,
+            out_shape=jax.ShapeDtypeStruct((size_z, columns), jnp.float32),
+            compiler_params=params,
+            cost_estimate=pl.CostEstimate(
+                flops=flops // 2, bytes_accessed=4 * 2**20, transcendentals=size_z * columns
+            ),
+            name="expected_counts",
+        )(field.reshape(cells), bias_grid, density_grid, tables)
+        inside = pl.BlockSpec(memory_space=pltpu.VMEM)
         back = pl.pallas_call(
-            shell_kernel,
+            gradient_kernel,
+            in_specs=[scalar, inside, inside, pl.BlockSpec(memory_space=pl.ANY), inside],
             out_shape=jax.ShapeDtypeStruct(cells, jnp.float32),
+            scratch_shapes=[
+                pltpu.VMEM((quarters * columns, BLOCK), counts.dtype),
+                pltpu.VMEM(expected.shape, jnp.float32),
+                pltpu.SemaphoreType.DMA,
+            ],
             compiler_params=params,
-            cost_estimate=pl.CostEstimate(flops=flops, bytes_accessed=8 * 2**20, transcendentals=size_z * 1024),
+            cost_estimate=pl.CostEstimate(flops=flops // 2, bytes_accessed=8 * 2**20, transcendentals=0),
             name="shell_gradient",
-        )(field.reshape(cells), galaxy, bias_grid, density_grid, tables)
+        )(slot_grid.reshape(-1), counts.reshape(-1, BLOCK), bias_grid, expected, tables)
 
         returned = lax.all_to_all(
             back.reshape(devices, chunk, BLOCK), ("px", "py"), split_axis=0, concat_axis=0, tiled=True

time: 232 us -> 227 us (0.978)
  starting transfers between devices: 48.8 us -> 37.9 us
  local copies, waits for them, and re-layouts: 32.6 us -> 24.3 us
  waiting for transfers between devices: 106 us -> 112 us
  Pallas kernels: 20.4 us -> 26.2 us
  other arithmetic: 19.3 us -> 24.1 us
    all_to_all x1, waiting for transfers between devices: 0.01 us -> 32.2 us  [body(): lax.all_to_all(outgoing, 'py', split_axis=0, concat_axis=0, tiled=True)]
    all_to_all x1, waiting for transfers between devices: 23.3 us -> 2.2 us  [body(): lax.all_to_all(sent.reshape(devices, chunk, BLOCK), ('px', 'py'), split_a...]
    gather x1 -> x0, local copies, waits for them, and re-layouts: 14.2 us -> none  [body(): picked = held.at[slot_grid.reshape(-1)].get(mode='promise_in_bounds')]
    ppermute x7 -> x3, starting transfers between devices: 13.4 us -> 4.96 us  [spread_ranks(): lax.ppermute(part(shift), 'py', pairs)]
    transpose x2, other arithmetic: 0.99 us -> 7.54 us  [by_column(): return grid.transpose(3, 1, 2, 0).reshape(quarters, -1)]
    all_to_all x1, starting transfers between devices: 11.9 us -> 5.94 us  [body(): lax.all_to_all(outgoing, 'py', split_axis=0, concat_axis=0, tiled=True)]
    pallas_call x1 -> x2, Pallas kernels: 7.13 us -> 13 us  [the longest x1 8.35 us: body(): pl.pallas_call(gradient_kernel, in_specs=[scalar, inside, inside, pl.Bloc...]
    all_to_all x1, starting transfers between devices: 5.89 us -> 11.3 us  [body(): lax.all_to_all(back.reshape(devices, chunk, BLOCK), ('px', 'py'), split_a...]
  transfers between devices with their start and end apart: 10 -> 6, of which waited for: 7 -> 5; matrix products, arithmetic and copies ran while one was open for 20% -> 20% of each run, Pallas kernels for 2% -> 2%
where the time goes in v5:
time: 227 us; the launch traced here: 226 us
  waiting for transfers between devices  112 us (49%)
  starting transfers between devices  37.9 us (17%)
  Pallas kernels  26.2 us (12%)
  local copies, waits for them, and re-layouts  24.3 us (11%)
  other arithmetic  24.1 us (11%)
    all_to_all x1, waiting for transfers between devices, body(): lax.all_to_all(back.reshape(devices, chunk, BLOCK), ('px', 'py'), split_a...  51.7 us
    all_to_all x1, waiting for transfers between devices, body(): lax.all_to_all(outgoing, 'py', split_axis=0, concat_axis=0, tiled=True)  32.2 us
    ppermute x3, waiting for transfers between devices, spread_ranks(): lax.ppermute(part(shift), 'py', pairs)  25.5 us
    all_to_all x1, starting transfers between devices, body(): lax.all_to_all(sent.reshape(devices, chunk, BLOCK), ('px', 'py'), split_a...  15.7 us
    all_to_all x1, starting transfers between devices, body(): lax.all_to_all(back.reshape(devices, chunk, BLOCK), ('px', 'py'), split_a...  11.3 us
    another operation x3, other arithmetic  9.62 us
    pallas_call x1, Pallas kernels, body(): pl.pallas_call(gradient_kernel, in_specs=[scalar, inside, inside, pl.Bloc...  8.35 us
    pallas_call x1, Pallas kernels, body(): pl.pallas_call(analysis_kernel, grid=(depth,), in_specs=[scalar, scalar,...  7.58 us
  transfers between devices with their start and end apart: 6, of which 5 were waited for; matrix products, arithmetic and copies ran while one was open for 20% of the time, Pallas kernels for 2%

profile of v5, /device:TPU:1, one launch (start us, length us, event | category | flops | bytes accessed | tf_op | source)
XLA Modules:
  0.0 226.2 jit_solution(1931184948978212410)
XLA Ops:
  0.6 5.6 %synthesis.1 = f32[8,32,2,8,128]{4,3,2,1,0:T(8,128)} custom-call(s32[1]{0:T(128)} %bitcast.first_ref, f32[2,512,512]{2,1,0:T(8,128)} %white_ref.3, bf16[2,512,512]{2,1,0:T(8,128)(2,1)} %amplitude_ref.3, bf16[6,256,256]{2,1,0:T(8,128)(2,1)} %constant.120.clone.tables_ref), custom_call_target="tpu_custom_call" | custom-call | flops 1610612736 | bytes 8388608 | tf_op jit(solution)/shard_map/synthesis/pallas_call | solution.py:263
  6.3 15.7 %all-to-all-start = ((f32[256,16,128]{2,1,0:T(8,128)}), f32[256,16,128]{2,1,0:T(8,128)S(1)}, u32[]{:S(2)}, u32[]{:S(2)}) async-start(f32[256,16,128]{2,1,0:T(8,128)} %bitcast.34), calls=%async_computation | async-start | bytes 4194304 | tf_op jit(solution)/shard_map/all_to_all | solution.py:276
  22.0 2.6 %fusion.10 = (s32[32,32,128]{2,1,0:T(8,128)}, s32[32,32,128]{2,1,0:T(8,128)}, s32[32,32,128]{2,1,0:T(8,128)}) fusion(s32[32,256,128]{2,1,0:T(8,128)} %bitcast.38), kind=kLoop, calls=%fused_computation.42 | loop fusion | bytes 3145728 | tf_op jit(solution)/shard_map/slice | solution.py:197
  24.5 1.4 collective-permute-start.2
  25.9 2.4 %collective-permute-start.1 = (s32[32,32,128]{2,1,0:T(8,128)}, s32[32,32,128]{2,1,0:T(8,128)}, u32[]{:S(2)}, u32[]{:S(2)}) collective-permute-start(s32[32,32,128]{2,1,0:T(8,128)} %get-tuple-element.13), channel_id=1, source_target_pairs={{0,2},{1,3},{2,0},{3,1},{4,6},{5,7},{6,4},{7,5},{8,10},{9,11},{10,... | collective-permute-start | bytes 1572872 | tf_op jit(solution)/shard_map/ppermute | solution.py:201
  29.6 9.2 %reduce-window.6 = s32[32,32,128]{2,1,0:T(8,128)S(1)} reduce-window(s32[32,32,128]{2,1,0:T(8,128)S(1)} %fusion.9, s32[]{:T(128)} %constant.108.clone.1), window={size=1x1x128 pad=0_0x0_0x127_0}, to_apply=%region_1.2 | reduce-window | flops 16646144 | bytes 1048580 | tf_op jit(solution)/shard_map/reduce-window
  41.6 3.1 %slice.30 = s32[32,128,128]{2,1,0:T(8,128)} slice(s32[32,256,128]{2,1,0:T(8,128)} %bitcast.39), slice={[0:32], [0:128], [0:128]} | slice | bytes 4194304 | tf_op jit(solution)/shard_map/slice | solution.py:280
  45.5 24.7 %collective-permute-done.1 = s32[32,32,128]{2,1,0:T(8,128)} collective-permute-done((s32[32,32,128]{2,1,0:T(8,128)}, s32[32,32,128]{2,1,0:T(8,128)}, u32[]{:S(2)}, u32[]{:S(2)}) %collective-permute-start.1) | collective-permute-done | bytes 524320 | tf_op jit(solution)/shard_map/ppermute | solution.py:201
  70.2 1.4 fusion.8
  71.7 1.7 pad_add_fusion
  73.4 2.2 all-to-all-done
  76.9 5.9 %all-to-all-start.1 = ((s32[32,160,128]{2,1,0:T(8,128)}), s32[32,160,128]{2,1,0:T(8,128)S(1)}, u32[]{:S(2)}, u32[]{:S(2)}) async-start(s32[32,160,128]{2,1,0:T(8,128)} %pad_add_fusion), calls=%async_computation.1 | async-start | bytes 5242880 | tf_op jit(solution)/shard_map/all_to_all | solution.py:282
  84.9 2.2 rev.7
  87.1 1.6 sub.32
  88.7 1.6 sub.34
  90.4 6.2 %select_bitcast_fusion = (s32[4,8,2,64]{0,2,1,3:T(2,128)}, s32[64,8,2,4]{3,2,1,0:T(2,128)}) fusion(s32[64,8,2,4]{3,2,1,0:T(2,128)S(1)} %reshape.52, s32[64,8,2,4]{3,2,1,0:T(2,128)} %rev.7, pred[]{:T(512)S(6)} %eq.62, s32[64,8,2,4]{3,2,1,0:T(2,128)} %sub.32, s32[64,8,2,4]{3,2,1,0:T(2,128)} %sub.34), kind=kLoop, calls=%fused_computation.28 | loop fusion | flops 225280 | bytes 98305 | tf_op jit(solution)/shard_map/transpose | solution.py:246
  98.0 3.6 %rev.6 = s32[64,8,2,4]{3,2,1,0:T(2,128)} reverse(s32[64,8,2,4]{3,2,1,0:T(2,128)} %get-tuple-element.16), dimensions={2} | reverse | bytes 32768 | tf_op jit(solution)/shard_map/rev | solution.py:245
  105.6 4.7 %expected_counts.1.expected_any = f32[512,1024]{1,0:T(8,128)} custom-call(f32[4096,128]{1,0:T(8,128)} %bitcast.35, f32[4,1024]{1,0:T(4,128)} %get-tuple-element.9.bias_ref, f32[4,1024]{1,0:T(4,128)} %get-tuple-element.8.density_ref, bf16[6,256,256]{2,1,0:T(8,128)(2,1)} %constant.120.clone.tables_ref), custom_call_target="tpu_custom_call" | custom-call | flops 805306368 | bytes 4194304 | tf_op jit(solution)/shard_map/expected_counts/pallas_call | solution.py:286
  110.2 32.2 %all-to-all-done.1 = s32[32,160,128]{2,1,0:T(8,128)S(1)} async-done(((s32[32,160,128]{2,1,0:T(8,128)}), s32[32,160,128]{2,1,0:T(8,128)S(1)}, u32[]{:S(2)}, u32[]{:S(2)}) %all-to-all-start.1) | async-done | bytes 2621472 | tf_op jit(solution)/shard_map/all_to_all | solution.py:282
  142.4 1.5 copy-done
  143.9 8.4 %shell_gradient.1 = f32[4096,128]{1,0:T(8,128)} custom-call(s32[4096]{0:T(1024)} %reshape_reshape.4.slot_ref, s32[5120,128]{1,0:T(8,128)} %bitcast.33, f32[4,1024]{1,0:T(4,128)} %get-tuple-element.9.bias_ref, f32[512,1024]{1,0:T(8,128)} %expected_counts.1.expected_any, bf16[6,256,256]{2,1,0:T(8,128)(2,1)} %constant.120.clone.tables_ref), custom_call_target="tpu_custom_call" | custom-call | flops 805306368 | bytes 8388608 | tf_op jit(solution)/shard_map/shell_gradient/pallas_call | solution.py:296
  152.3 11.3 %all-to-all-start.2 = ((f32[256,16,128]{2,1,0:T(8,128)}), f32[256,16,128]{2,1,0:T(8,128)S(1)}, u32[]{:S(2)}, u32[]{:S(2)}) async-start(f32[256,16,128]{2,1,0:T(8,128)} %bitcast.37), calls=%async_computation.2 | async-start | bytes 4194304 | tf_op jit(solution)/shard_map/all_to_all | solution.py:310
  165.5 51.7 %all-to-all-done.2 = f32[256,16,128]{2,1,0:T(8,128)S(1)} async-done(((f32[256,16,128]{2,1,0:T(8,128)}), f32[256,16,128]{2,1,0:T(8,128)S(1)}, u32[]{:S(2)}, u32[]{:S(2)}) %all-to-all-start.2) | async-done | bytes 2097184 | tf_op jit(solution)/shard_map/all_to_all | solution.py:310
  218.6 7.6 %analysis.1 = (f32[2,512,512]{2,1,0:T(8,128)}, f32[2,512,512]{2,1,0:T(8,128)}) custom-call(s32[1]{0:T(128)} %bitcast.first_ref, f32[2]{0:T(128)} %pad_maximum_fusion.step_ref, f32[8,32,2,8,128]{4,3,2,1,0:T(8,128)} %bitcast.36, f32[2,512,512]{2,1,0:T(8,128)} %white_ref.3, bf16[2,512,512]{2,1,0:T(8,128)(2,1)} %amplitude_ref.3, bf16[2,512,512]{2,1,0:T(8,128)(2,1)} %kick_ref.1, ...), custom_call_target="tpu_custom_call" | custom-call | flops 1610612736 | bytes 12582912 | tf_op jit(solution)/shard_map/analysis/pallas_call | solution.py:316
  (33 shorter events, 15.5 us)
Async XLA Ops:
  6.3 69.3 %all-to-all-start = ((f32[256,16,128]{2,1,0:T(8,128)}), f32[256,16,128]{2,1,0:T(8,128)S(1)}, u32[]{:S(2)}, u32[]{:S(2)}) async-start(f32[256,16,128]{2,1,0:T(8,128)} %bitcast.34), calls=%async_computation | async-start | bytes 4194304 | tf_op jit(solution)/shard_map/all_to_all | solution.py:276
  22.0 7.5 %copy-start.4 = (s32[1,1,4096]{2,1,0:T(1,128)S(1)}, s32[1,1,4096]{2,1,0:T(1,128)}, u32[]{:S(2)}) copy-start(s32[1,1,4096]{2,1,0:T(1,128)} %param.12) | copy-start | bytes 49156
  24.5 21.0 %collective-permute-start.2 = (s32[32,32,128]{2,1,0:T(8,128)}, s32[32,32,128]{2,1,0:T(8,128)}, u32[]{:S(2)}, u32[]{:S(2)}) collective-permute-start(s32[32,32,128]{2,1,0:T(8,128)} %get-tuple-element.12), channel_id=1, source_target_pairs={{0,1},{1,2},{2,3},{3,0},{4,5},{5,6},{6,7},{7,4},{8,9},{9,10},{10,1... | collective-permute-start | bytes 1572872 | tf_op jit(solution)/shard_map/ppermute | solution.py:201
  25.9 44.3 %collective-permute-start.1 = (s32[32,32,128]{2,1,0:T(8,128)}, s32[32,32,128]{2,1,0:T(8,128)}, u32[]{:S(2)}, u32[]{:S(2)}) collective-permute-start(s32[32,32,128]{2,1,0:T(8,128)} %get-tuple-element.13), channel_id=1, source_target_pairs={{0,2},{1,3},{2,0},{3,1},{4,6},{5,7},{6,4},{7,5},{8,10},{9,11},{10,... | collective-permute-start | bytes 1572872 | tf_op jit(solution)/shard_map/ppermute | solution.py:201
  28.3 41.9 %collective-permute-start = (s32[32,32,128]{2,1,0:T(8,128)}, s32[32,32,128]{2,1,0:T(8,128)}, u32[]{:S(2)}, u32[]{:S(2)}) collective-permute-start(s32[32,32,128]{2,1,0:T(8,128)} %get-tuple-element.14), channel_id=1, source_target_pairs={{0,3},{1,0},{2,1},{3,2},{4,7},{5,4},{6,5},{7,6},{8,11},{9,8},{10,9... | collective-permute-start | bytes 1572872 | tf_op jit(solution)/shard_map/ppermute | solution.py:201
  44.8 26.9 %copy-start.2 = (s32[32,128,128]{2,1,0:T(8,128)S(1)}, s32[32,128,128]{2,1,0:T(8,128)}, u32[]{:S(2)}) copy-start(s32[32,128,128]{2,1,0:T(8,128)} %slice.30) | copy-start | bytes 6291460
  75.6 1.3 copy-start.1
  76.9 65.5 %all-to-all-start.1 = ((s32[32,160,128]{2,1,0:T(8,128)}), s32[32,160,128]{2,1,0:T(8,128)S(1)}, u32[]{:S(2)}, u32[]{:S(2)}) async-start(s32[32,160,128]{2,1,0:T(8,128)} %pad_add_fusion), calls=%async_computation.1 | async-start | bytes 5242880 | tf_op jit(solution)/shard_map/all_to_all | solution.py:282
  142.4 1.5 copy-start
  152.3 11.3 %copy-start.5 = (s32[64]{0:T(128)S(1)}, s32[64]{0:T(128)}, u32[]{:S(2)}) copy-start(s32[64]{0:T(128)} %param.16) | copy-start | bytes 772
  152.3 64.9 %all-to-all-start.2 = ((f32[256,16,128]{2,1,0:T(8,128)}), f32[256,16,128]{2,1,0:T(8,128)S(1)}, u32[]{:S(2)}, u32[]{:S(2)}) async-start(f32[256,16,128]{2,1,0:T(8,128)} %bitcast.37), calls=%async_computation.2 | async-start | bytes 4194304 | tf_op jit(solution)/shard_map/all_to_all | solution.py:310
  217.2 1.4 copy-start.3

commit v6 on v5

--- a/solution.py
+++ b/solution.py
@@ -11,7 +11,7 @@
 BLOCK = 128
 HALF = BLOCK // 2
 WIDTH = 4
-GROUP = 64
+GROUP = 128
 VMEM_BYTES = 56 * 1024 * 1024
 
 
@@ -286,7 +286,7 @@
         expected = pl.pallas_call(
             expected_kernel,
             out_shape=jax.ShapeDtypeStruct((size_z, columns), jnp.float32),
-            compiler_params=params,
+            compiler_params=pltpu.CompilerParams(vmem_limit_bytes=48 * 2**20),
             cost_estimate=pl.CostEstimate(
                 flops=flops // 2, bytes_accessed=4 * 2**20, transcendentals=size_z * columns
             ),
@@ -302,7 +302,7 @@
                 pltpu.VMEM(expected.shape, jnp.float32),
                 pltpu.SemaphoreType.DMA,
             ],
-            compiler_params=params,
+            compiler_params=pltpu.CompilerParams(vmem_limit_bytes=56 * 2**20),
             cost_estimate=pl.CostEstimate(flops=flops // 2, bytes_accessed=8 * 2**20, transcendentals=0),
             name="shell_gradient",
         )(slot_grid.reshape(-1), counts.reshape(-1, BLOCK), bias_grid, expected, tables)
@@ -320,7 +320,7 @@
             out_specs=(plane, plane),
             out_shape=(out_plane, out_plane),
             scratch_shapes=[tiled],
-            compiler_params=params,
+            compiler_params=pltpu.CompilerParams(vmem_limit_bytes=50 * 2**20),
             cost_estimate=pl.CostEstimate(flops=flops, bytes_accessed=12 * 2**20, transcendentals=0),
             name="analysis",
         )(first, steps, returned.reshape(packed_shape), white_noise, mode_amplitude, kick_noise, tables)

time: 227 us -> 221 us (0.974)
  Pallas kernels: 26.2 us -> 21.8 us
  local copies, waits for them, and re-layouts: 24.3 us -> 21 us
    pallas_call x1, Pallas kernels: 4.65 us -> 1.54 us  [body(): pl.pallas_call(expected_kernel, out_shape=jax.ShapeDtypeStruct((size_z, c...]
    unnamed x13 -> x19, local copies, waits for them, and re-layouts: 4.7 us -> 1.87 us
  transfers between devices with their start and end apart: 6 -> 6, of which waited for: 5 -> 5; matrix products, arithmetic and copies ran while one was open for 20% -> 20% of each run, Pallas kernels for 2% -> 1%
where the time goes in v6:
time: 221 us
  waiting for transfers between devices  113 us (51%)
  starting transfers between devices  39 us (18%)
  other arithmetic  23.7 us (11%)
  Pallas kernels  21.8 us (10%)
  local copies, waits for them, and re-layouts  21 us (10%)
    all_to_all x1, waiting for transfers between devices, body(): lax.all_to_all(back.reshape(devices, chunk, BLOCK), ('px', 'py'), split_a...  51.3 us
    all_to_all x1, waiting for transfers between devices, body(): lax.all_to_all(outgoing, 'py', split_axis=0, concat_axis=0, tiled=True)  34.3 us
    ppermute x3, waiting for transfers between devices, spread_ranks(): lax.ppermute(part(shift), 'py', pairs)  25.5 us
    all_to_all x1, starting transfers between devices, body(): lax.all_to_all(sent.reshape(devices, chunk, BLOCK), ('px', 'py'), split_a...  15.7 us
    all_to_all x1, starting transfers between devices, body(): lax.all_to_all(back.reshape(devices, chunk, BLOCK), ('px', 'py'), split_a...  12.3 us
    another operation x3, other arithmetic  9.62 us
    transpose x2, other arithmetic, by_column(): return grid.transpose(3, 1, 2, 0).reshape(quarters, -1)  8.24 us
    pallas_call x1, Pallas kernels, body(): pl.pallas_call(gradient_kernel, in_specs=[scalar, inside, inside, pl.Bloc...  8.22 us
  transfers between devices with their start and end apart: 6, of which 5 were waited for; matrix products, arithmetic and copies ran while one was open for 20% of the time, Pallas kernels for 1%

profile of v6, /device:TPU:1, one launch (start us, length us, event | category | flops | bytes accessed | tf_op | source)
XLA Modules:
  0.0 221.0 jit_solution(1861003176276626319)
XLA Ops:
  0.6 5.6 %synthesis.1 = f32[8,32,2,8,128]{4,3,2,1,0:T(8,128)} custom-call(s32[1]{0:T(128)} %bitcast.first_ref, f32[2,512,512]{2,1,0:T(8,128)} %white_ref.3, bf16[2,512,512]{2,1,0:T(8,128)(2,1)} %amplitude_ref.3, bf16[6,256,256]{2,1,0:T(8,128)(2,1)} %constant.120.clone.tables_ref), custom_call_target="tpu_custom_call" | custom-call | flops 1610612736 | bytes 8388608 | tf_op jit(solution)/shard_map/synthesis/pallas_call | solution.py:263
  6.3 15.7 %all-to-all-start = ((f32[256,16,128]{2,1,0:T(8,128)}), f32[256,16,128]{2,1,0:T(8,128)S(1)}, u32[]{:S(2)}, u32[]{:S(2)}) async-start(f32[256,16,128]{2,1,0:T(8,128)} %bitcast.34), calls=%async_computation | async-start | bytes 4194304 | tf_op jit(solution)/shard_map/all_to_all | solution.py:276
  22.0 2.6 %fusion.10 = (s32[32,32,128]{2,1,0:T(8,128)}, s32[32,32,128]{2,1,0:T(8,128)}, s32[32,32,128]{2,1,0:T(8,128)}) fusion(s32[32,256,128]{2,1,0:T(8,128)} %bitcast.36), kind=kLoop, calls=%fused_computation.42 | loop fusion | bytes 3145728 | tf_op jit(solution)/shard_map/slice | solution.py:197
  24.5 1.4 collective-permute-start.2
  25.9 2.4 %collective-permute-start.1 = (s32[32,32,128]{2,1,0:T(8,128)}, s32[32,32,128]{2,1,0:T(8,128)}, u32[]{:S(2)}, u32[]{:S(2)}) collective-permute-start(s32[32,32,128]{2,1,0:T(8,128)} %get-tuple-element.13), channel_id=1, source_target_pairs={{0,2},{1,3},{2,0},{3,1},{4,6},{5,7},{6,4},{7,5},{8,10},{9,11},{10,... | collective-permute-start | bytes 1572872 | tf_op jit(solution)/shard_map/ppermute | solution.py:201
  29.6 9.2 %reduce-window.6 = s32[32,32,128]{2,1,0:T(8,128)S(1)} reduce-window(s32[32,32,128]{2,1,0:T(8,128)S(1)} %fusion.9, s32[]{:T(128)} %constant.108.clone.1), window={size=1x1x128 pad=0_0x0_0x127_0}, to_apply=%region_1.2 | reduce-window | flops 16646144 | bytes 1048580 | tf_op jit(solution)/shard_map/reduce-window
  41.6 3.1 %slice.30 = s32[32,128,128]{2,1,0:T(8,128)} slice(s32[32,256,128]{2,1,0:T(8,128)} %bitcast.37), slice={[0:32], [0:128], [0:128]} | slice | bytes 4194304 | tf_op jit(solution)/shard_map/slice | solution.py:280
  45.5 24.7 %collective-permute-done.1 = s32[32,32,128]{2,1,0:T(8,128)} collective-permute-done((s32[32,32,128]{2,1,0:T(8,128)}, s32[32,32,128]{2,1,0:T(8,128)}, u32[]{:S(2)}, u32[]{:S(2)}) %collective-permute-start.1) | collective-permute-done | bytes 524320 | tf_op jit(solution)/shard_map/ppermute | solution.py:201
  70.2 1.4 fusion.8
  71.7 1.8 pad_add_fusion
  73.4 2.2 all-to-all-done
  75.6 6.1 %all-to-all-start.1 = ((s32[32,160,128]{2,1,0:T(8,128)}), s32[32,160,128]{2,1,0:T(8,128)}, u32[]{:S(2)}, u32[]{:S(2)}) async-start(s32[32,160,128]{2,1,0:T(8,128)} %pad_add_fusion), calls=%async_computation.1 | async-start | bytes 5242880 | tf_op jit(solution)/shard_map/all_to_all | solution.py:282
  83.7 2.2 %rev.7 = s32[64,8,2,4]{3,2,1,0:T(2,128)} reverse(s32[64,8,2,4]{3,2,1,0:T(2,128)S(1)} %reshape.52), dimensions={2} | reverse | bytes 32768 | tf_op jit(solution)/shard_map/rev | solution.py:245
  85.9 1.6 sub.32
  87.6 1.6 sub.34
  89.2 6.1 %select_bitcast_fusion = (s32[4,8,2,64]{0,2,1,3:T(2,128)}, s32[64,8,2,4]{3,2,1,0:T(2,128)S(1)}) fusion(s32[64,8,2,4]{3,2,1,0:T(2,128)S(1)} %reshape.52, s32[64,8,2,4]{3,2,1,0:T(2,128)} %rev.7, pred[]{:T(512)S(6)} %eq.62, s32[64,8,2,4]{3,2,1,0:T(2,128)} %sub.32, s32[64,8,2,4]{3,2,1,0:T(2,128)} %sub.34), kind=kLoop, calls=%fused_computation.28 | loop fusion | flops 225280 | bytes 98305 | tf_op jit(solution)/shard_map/transpose | solution.py:246
  96.8 2.2 rev.6
  99.0 2.1 select_bitcast_fusion.1
  104.0 1.5 expected_counts.1.expected_any
  106.9 34.3 %all-to-all-done.1 = s32[32,160,128]{2,1,0:T(8,128)} async-done(((s32[32,160,128]{2,1,0:T(8,128)}), s32[32,160,128]{2,1,0:T(8,128)}, u32[]{:S(2)}, u32[]{:S(2)}) %all-to-all-start.1) | async-done | bytes 2621472 | tf_op jit(solution)/shard_map/all_to_all | solution.py:282
  141.2 8.2 %shell_gradient.1 = f32[4096,128]{1,0:T(8,128)} custom-call(s32[4096]{0:T(1024)} %reshape_reshape.4.slot_ref, s32[5120,128]{1,0:T(8,128)} %bitcast.9.counts_ref, f32[4,1024]{1,0:T(4,128)} %copy-done.5, f32[512,1024]{1,0:T(8,128)} %copy-done.2, bf16[6,256,256]{2,1,0:T(8,128)(2,1)} %constant.120.clone.tables_ref), custom_call_target="tpu_custom_call" | custom-call | flops 805306368 | bytes 8388608 | tf_op jit(solution)/shard_map/shell_gradient/pallas_call | solution.py:296
  149.5 12.3 %all-to-all-start.2 = ((f32[256,16,128]{2,1,0:T(8,128)}), f32[256,16,128]{2,1,0:T(8,128)}, u32[]{:S(2)}, u32[]{:S(2)}) async-start(f32[256,16,128]{2,1,0:T(8,128)} %bitcast.35), calls=%async_computation.2 | async-start | bytes 4194304 | tf_op jit(solution)/shard_map/all_to_all | solution.py:310
  163.2 51.3 %all-to-all-done.2 = f32[256,16,128]{2,1,0:T(8,128)} async-done(((f32[256,16,128]{2,1,0:T(8,128)}), f32[256,16,128]{2,1,0:T(8,128)}, u32[]{:S(2)}, u32[]{:S(2)}) %all-to-all-start.2) | async-done | bytes 2097184 | tf_op jit(solution)/shard_map/all_to_all | solution.py:310
  214.6 6.4 %analysis.1 = (f32[2,512,512]{2,1,0:T(8,128)}, f32[2,512,512]{2,1,0:T(8,128)}) custom-call(s32[1]{0:T(128)} %bitcast.first_ref, f32[2]{0:T(128)S(1)} %pad_maximum_fusion.step_ref, f32[8,32,2,8,128]{4,3,2,1,0:T(8,128)} %bitcast.15.field_ref, f32[2,512,512]{2,1,0:T(8,128)} %white_ref.3, bf16[2,512,512]{2,1,0:T(8,128)(2,1)S(1)} %copy-done.3, ...), custom_call_target="tpu_custom_call" | custom-call | flops 1610612736 | bytes 12582912 | tf_op jit(solution)/shard_map/analysis/pallas_call | solution.py:316
  (39 shorter events, 12.6 us)
Async XLA Ops:
  6.3 69.3 %all-to-all-start = ((f32[256,16,128]{2,1,0:T(8,128)}), f32[256,16,128]{2,1,0:T(8,128)S(1)}, u32[]{:S(2)}, u32[]{:S(2)}) async-start(f32[256,16,128]{2,1,0:T(8,128)} %bitcast.34), calls=%async_computation | async-start | bytes 4194304 | tf_op jit(solution)/shard_map/all_to_all | solution.py:276
  22.0 7.5 %copy-start.7 = (s32[1,1,4096]{2,1,0:T(1,128)S(1)}, s32[1,1,4096]{2,1,0:T(1,128)}, u32[]{:S(2)}) copy-start(s32[1,1,4096]{2,1,0:T(1,128)} %param.12) | copy-start | bytes 49156
  24.5 21.0 %collective-permute-start.2 = (s32[32,32,128]{2,1,0:T(8,128)}, s32[32,32,128]{2,1,0:T(8,128)}, u32[]{:S(2)}, u32[]{:S(2)}) collective-permute-start(s32[32,32,128]{2,1,0:T(8,128)} %get-tuple-element.12), channel_id=1, source_target_pairs={{0,1},{1,2},{2,3},{3,0},{4,5},{5,6},{6,7},{7,4},{8,9},{9,10},{10,1... | collective-permute-start | bytes 1572872 | tf_op jit(solution)/shard_map/ppermute | solution.py:201
  25.9 44.3 %collective-permute-start.1 = (s32[32,32,128]{2,1,0:T(8,128)}, s32[32,32,128]{2,1,0:T(8,128)}, u32[]{:S(2)}, u32[]{:S(2)}) collective-permute-start(s32[32,32,128]{2,1,0:T(8,128)} %get-tuple-element.13), channel_id=1, source_target_pairs={{0,2},{1,3},{2,0},{3,1},{4,6},{5,7},{6,4},{7,5},{8,10},{9,11},{10,... | collective-permute-start | bytes 1572872 | tf_op jit(solution)/shard_map/ppermute | solution.py:201
  28.3 41.9 %collective-permute-start = (s32[32,32,128]{2,1,0:T(8,128)}, s32[32,32,128]{2,1,0:T(8,128)}, u32[]{:S(2)}, u32[]{:S(2)}) collective-permute-start(s32[32,32,128]{2,1,0:T(8,128)} %get-tuple-element.14), channel_id=1, source_target_pairs={{0,3},{1,0},{2,1},{3,2},{4,7},{5,4},{6,5},{7,6},{8,11},{9,8},{10,9... | collective-permute-start | bytes 1572872 | tf_op jit(solution)/shard_map/ppermute | solution.py:201
  44.8 26.9 %copy-start.6 = (s32[32,128,128]{2,1,0:T(8,128)S(1)}, s32[32,128,128]{2,1,0:T(8,128)}, u32[]{:S(2)}) copy-start(s32[32,128,128]{2,1,0:T(8,128)} %slice.30) | copy-start | bytes 6291460
  75.6 65.6 %all-to-all-start.1 = ((s32[32,160,128]{2,1,0:T(8,128)}), s32[32,160,128]{2,1,0:T(8,128)}, u32[]{:S(2)}, u32[]{:S(2)}) async-start(s32[32,160,128]{2,1,0:T(8,128)} %pad_add_fusion), calls=%async_computation.1 | async-start | bytes 5242880 | tf_op jit(solution)/shard_map/all_to_all | solution.py:282
  95.3 8.7 %copy-start = (bf16[6,256,256]{2,1,0:T(8,128)(2,1)S(1)}, bf16[6,256,256]{2,1,0:T(8,128)(2,1)}, u32[]{:S(2)}) copy-start(bf16[6,256,256]{2,1,0:T(8,128)(2,1)} %constant.120.clone.tables_ref) | copy-start | bytes 2359300
  104.0 1.6 copy-start.5
  105.6 1.3 copy-start.2
  149.5 12.3 %copy-start.8 = (s32[64]{0:T(128)S(1)}, s32[64]{0:T(128)}, u32[]{:S(2)}) copy-start(s32[64]{0:T(128)} %param.16) | copy-start | bytes 772
  149.5 65.1 %copy-start.1 = (bf16[6,256,256]{2,1,0:T(8,128)(2,1)S(1)}, bf16[6,256,256]{2,1,0:T(8,128)(2,1)}, u32[]{:S(2)}) copy-start(bf16[6,256,256]{2,1,0:T(8,128)(2,1)} %constant.120.clone.tables_ref) | copy-start | bytes 2359300
  149.5 65.1 %copy-start.3 = (bf16[2,512,512]{2,1,0:T(8,128)(2,1)S(1)}, bf16[2,512,512]{2,1,0:T(8,128)(2,1)}, u32[]{:S(2)}) copy-start(bf16[2,512,512]{2,1,0:T(8,128)(2,1)} %amplitude_ref.3) | copy-start | bytes 3145732
  149.5 65.1 %copy-start.4 = (bf16[2,512,512]{2,1,0:T(8,128)(2,1)S(1)}, bf16[2,512,512]{2,1,0:T(8,128)(2,1)}, u32[]{:S(2)}) copy-start(bf16[2,512,512]{2,1,0:T(8,128)(2,1)} %kick_ref.1) | copy-start | bytes 3145732
  149.5 65.0 %all-to-all-start.2 = ((f32[256,16,128]{2,1,0:T(8,128)}), f32[256,16,128]{2,1,0:T(8,128)}, u32[]{:S(2)}, u32[]{:S(2)}) async-start(f32[256,16,128]{2,1,0:T(8,128)} %bitcast.35), calls=%async_computation.2 | async-start | bytes 4194304 | tf_op jit(solution)/shard_map/all_to_all | solution.py:310

commit v7 on v6

--- a/solution.py
+++ b/solution.py
@@ -194,7 +194,7 @@
     size, capacity, _ = counts.shape
     width = (capacity - keep) // WIDTH
     away = (col_index - heavy) % WIDTH
-    part = lambda k: counts[:, keep + k * width : keep + (k + 1) * width]
+    part = lambda k: counts[::-1, keep + k * width : keep + (k + 1) * width]
     mine = part(0)
     for shift in range(1, WIDTH):
         pairs = [(i, i // WIDTH * WIDTH + (i + shift) % WIDTH) for i in range(size)]
@@ -234,8 +234,8 @@
         holder = owner_list // WIDTH * WIDTH + (owner_list + place // width) % WIDTH
         slot_index = jnp.where(
             place < 0,
-            owner_list * (keep + width) + rank_index,
-            holder * (keep + width) + keep + place % width,
+            (rows_py - 1 - owner_list) * (keep + width) + rank_index,
+            (rows_py - 1 - holder) * (keep + width) + keep + place % width,
         )
         bias_row = lax.dynamic_index_in_dim(shell_bias, row_index, 0, keepdims=False)
         density_row = lax.dynamic_index_in_dim(shell_density, row_index, 0, keepdims=False)
@@ -277,9 +277,16 @@
             sent.reshape(devices, chunk, BLOCK), ("px", "py"), split_axis=0, concat_axis=0, tiled=True
         )
 
-        outgoing = jnp.concatenate([galaxy_in[:, :keep], spread_ranks(galaxy_in, keep, heavy, col_index)], axis=1)
+        outgoing = jnp.concatenate([galaxy_in[::-1, :keep], spread_ranks(galaxy_in, keep, heavy, col_index)], axis=1)
         outgoing, field = lax.optimization_barrier((outgoing, field))
-        counts = lax.all_to_all(outgoing, "py", split_axis=0, concat_axis=0, tiled=True)
+        counts = lax.all_to_all(
+            outgoing,
+            "py",
+            split_axis=0,
+            concat_axis=0,
+            tiled=True,
+            axis_index_groups=[list(range(rows_py - 1, -1, -1))],
+        )
 
         cells = (size_z * rows_y, BLOCK)
         columns = span_x * span_y

time: 221 us -> 224 us (1.014)
  waiting for transfers between devices: 113 us -> 105 us
  local copies, waits for them, and re-layouts: 21 us -> 28 us
  starting transfers between devices: 39 us -> 42.1 us
    rev x0 -> x4, local copies, waits for them, and re-layouts: none -> 6.77 us  [the longest x3 3.58 us: spread_ranks(): part = lambda k: counts[::-1, keep + k * width:keep + (k + 1) * width]]
    all_to_all x1, waiting for transfers between devices: 34.3 us -> 31.1 us  [body(): lax.all_to_all(outgoing, 'py', split_axis=0, concat_axis=0, tiled=True, a...]
    all_to_all x1, starting transfers between devices: 6.08 us -> 9.15 us  [body(): lax.all_to_all(outgoing, 'py', split_axis=0, concat_axis=0, tiled=True, a...]
    ppermute x3, waiting for transfers between devices: 25.5 us -> 22.8 us  [spread_ranks(): lax.ppermute(part(shift), 'py', pairs)]
  transfers between devices with their start and end apart: 6 -> 6, of which waited for: 5 -> 4; matrix products, arithmetic and copies ran while one was open for 20% -> 23% of each run, Pallas kernels for 1% -> 1%
where the time goes in v7:
time: 224 us; the launch traced here: 223 us
  waiting for transfers between devices  105 us (47%)
  starting transfers between devices  42.1 us (19%)
  local copies, waits for them, and re-layouts  28 us (12%)
  other arithmetic  23.7 us (11%)
  Pallas kernels  21.8 us (10%)
  between operations  2.24 us (1%)
    all_to_all x1, waiting for transfers between devices, body(): lax.all_to_all(back.reshape(devices, chunk, BLOCK), ('px', 'py'), split_a...  51.3 us
    all_to_all x1, waiting for transfers between devices, body(): lax.all_to_all(outgoing, 'py', split_axis=0, concat_axis=0, tiled=True, a...  31.1 us
    ppermute x3, waiting for transfers between devices, spread_ranks(): lax.ppermute(part(shift), 'py', pairs)  22.8 us
    all_to_all x1, starting transfers between devices, body(): lax.all_to_all(sent.reshape(devices, chunk, BLOCK), ('px', 'py'), split_a...  15.7 us
    all_to_all x1, starting transfers between devices, body(): lax.all_to_all(back.reshape(devices, chunk, BLOCK), ('px', 'py'), split_a...  13.5 us
    another operation x3, other arithmetic  9.62 us
    all_to_all x1, starting transfers between devices, body(): lax.all_to_all(outgoing, 'py', split_axis=0, concat_axis=0, tiled=True, a...  9.15 us
    transpose x2, other arithmetic, by_column(): return grid.transpose(3, 1, 2, 0).reshape(quarters, -1)  8.37 us
  transfers between devices with their start and end apart: 6, of which 4 were waited for; matrix products, arithmetic and copies ran while one was open for 23% of the time, Pallas kernels for 1%

profile of v7, /device:TPU:1, one launch (start us, length us, event | category | flops | bytes accessed | tf_op | source)
XLA Modules:
  0.0 223.0 jit_solution(18427610978694888474)
XLA Ops:
  0.6 5.7 %synthesis.1 = f32[8,32,2,8,128]{4,3,2,1,0:T(8,128)} custom-call(s32[1]{0:T(128)} %bitcast.first_ref, f32[2,512,512]{2,1,0:T(8,128)} %white_ref.3, bf16[2,512,512]{2,1,0:T(8,128)(2,1)} %amplitude_ref.3, bf16[6,256,256]{2,1,0:T(8,128)(2,1)} %constant.121.clone.tables_ref), custom_call_target="tpu_custom_call" | custom-call | flops 1610612736 | bytes 8388608 | tf_op jit(solution)/shard_map/synthesis/pallas_call | solution.py:263
  6.3 15.7 %all-to-all-start = ((f32[256,16,128]{2,1,0:T(8,128)}), f32[256,16,128]{2,1,0:T(8,128)S(1)}, u32[]{:S(2)}, u32[]{:S(2)}) async-start(f32[256,16,128]{2,1,0:T(8,128)} %bitcast.34), calls=%async_computation | async-start | bytes 4194304 | tf_op jit(solution)/shard_map/all_to_all | solution.py:276
  22.0 2.7 %fusion.8 = (s32[32,32,128]{2,1,0:T(8,128)}, s32[32,32,128]{2,1,0:T(8,128)S(1)}, s32[32,32,128]{2,1,0:T(8,128)S(1)}, s32[32,32,128]{2,1,0:T(8,128)}) fusion(s32[32,256,128]{2,1,0:T(8,128)} %bitcast.36), kind=kLoop, calls=%fused_computation.40 | loop fusion | bytes 4194304 | tf_op jit(solution)/shard_map/slice | solution.py:197
  24.7 1.9 rev.23
  26.6 2.6 %collective-permute-start = (s32[32,32,128]{2,1,0:T(8,128)}, s32[32,32,128]{2,1,0:T(8,128)}, u32[]{:S(2)}, u32[]{:S(2)}) collective-permute-start(s32[32,32,128]{2,1,0:T(8,128)} %rev.23), channel_id=1, source_target_pairs={{0,3},{1,0},{2,1},{3,2},{4,7},{5,4},{6,5},{7,6},{8,11},{9,8},{10,9... | collective-permute-start | bytes 1572872 | tf_op jit(solution)/shard_map/ppermute | solution.py:201
  32.1 9.2 %reduce-window.6 = s32[32,32,128]{2,1,0:T(8,128)S(1)} reduce-window(s32[32,32,128]{2,1,0:T(8,128)S(1)} %fusion.7, s32[]{:T(128)} %constant.109.clone.1), window={size=1x1x128 pad=0_0x0_0x127_0}, to_apply=%region_1.2 | reduce-window | flops 16646144 | bytes 1048580 | tf_op jit(solution)/shard_map/reduce-window
  44.3 3.1 %slice.30 = s32[32,128,128]{2,1,0:T(8,128)} slice(s32[32,256,128]{2,1,0:T(8,128)} %bitcast.37), slice={[0:32], [0:128], [0:128]} | slice | bytes 4194304 | tf_op jit(solution)/shard_map/slice | solution.py:280
  47.4 3.2 %rev.22 = s32[32,128,128]{2,1,0:T(8,128)} reverse(s32[32,128,128]{2,1,0:T(8,128)} %slice.30), dimensions={0} | reverse | bytes 4194304 | tf_op jit(solution)/shard_map/rev | solution.py:280
  50.6 4.3 %collective-permute-done = s32[32,32,128]{2,1,0:T(8,128)} collective-permute-done((s32[32,32,128]{2,1,0:T(8,128)}, s32[32,32,128]{2,1,0:T(8,128)}, u32[]{:S(2)}, u32[]{:S(2)}) %collective-permute-start) | collective-permute-done | bytes 524320 | tf_op jit(solution)/shard_map/ppermute | solution.py:201
  55.0 18.5 %collective-permute-done.2 = s32[32,32,128]{2,1,0:T(8,128)} collective-permute-done((s32[32,32,128]{2,1,0:T(8,128)}, s32[32,32,128]{2,1,0:T(8,128)}, u32[]{:S(2)}, u32[]{:S(2)}) %collective-permute-start.2) | collective-permute-done | bytes 524320 | tf_op jit(solution)/shard_map/ppermute | solution.py:201
  74.7 1.7 pad_add_fusion
  76.5 9.2 %all-to-all-start.1 = ((s32[32,160,128]{2,1,0:T(8,128)}), s32[32,160,128]{2,1,0:T(8,128)}, u32[]{:S(2)}, u32[]{:S(2)}) async-start(s32[32,160,128]{2,1,0:T(8,128)} %pad_add_fusion), calls=%async_computation.1 | async-start | bytes 5242880 | tf_op jit(solution)/shard_map/all_to_all | solution.py:282
  87.7 2.2 rev.27
  89.9 1.6 sub.40
  91.5 1.6 sub.43
  93.1 6.3 %select_bitcast_fusion = (s32[4,8,2,64]{0,2,1,3:T(2,128)}, s32[64,8,2,4]{3,2,1,0:T(2,128)S(1)}) fusion(s32[64,8,2,4]{3,2,1,0:T(2,128)S(1)} %reshape.52, s32[64,8,2,4]{3,2,1,0:T(2,128)} %rev.27, pred[]{:T(512)S(6)} %eq.62, s32[64,8,2,4]{3,2,1,0:T(2,128)} %sub.40, s32[64,8,2,4]{3,2,1,0:T(2,128)} %sub.43), kind=kLoop, calls=%fused_computation.25 | loop fusion | flops 233472 | bytes 98305 | tf_op jit(solution)/shard_map/transpose | solution.py:246
  100.9 2.2 rev.21
  103.1 2.1 select_bitcast_fusion.1
  108.1 1.5 expected_counts.1.expected_any
  111.0 31.1 %all-to-all-done.1 = s32[32,160,128]{2,1,0:T(8,128)} async-done(((s32[32,160,128]{2,1,0:T(8,128)}), s32[32,160,128]{2,1,0:T(8,128)}, u32[]{:S(2)}, u32[]{:S(2)}) %all-to-all-start.1) | async-done | bytes 2621472 | tf_op jit(solution)/shard_map/all_to_all | solution.py:282
  142.0 8.2 %shell_gradient.1 = f32[4096,128]{1,0:T(8,128)} custom-call(s32[4096]{0:T(1024)} %reshape_reshape.4.slot_ref, s32[5120,128]{1,0:T(8,128)} %bitcast.9.counts_ref, f32[4,1024]{1,0:T(4,128)} %copy-done.5, f32[512,1024]{1,0:T(8,128)} %copy-done.2, bf16[6,256,256]{2,1,0:T(8,128)(2,1)} %constant.121.clone.tables_ref), custom_call_target="tpu_custom_call" | custom-call | flops 805306368 | bytes 8388608 | tf_op jit(solution)/shard_map/shell_gradient/pallas_call | solution.py:303
  150.3 13.5 %all-to-all-start.2 = ((f32[256,16,128]{2,1,0:T(8,128)}), f32[256,16,128]{2,1,0:T(8,128)}, u32[]{:S(2)}, u32[]{:S(2)}) async-start(f32[256,16,128]{2,1,0:T(8,128)} %bitcast.35), calls=%async_computation.2 | async-start | bytes 4194304 | tf_op jit(solution)/shard_map/all_to_all | solution.py:317
  165.3 51.3 %all-to-all-done.2 = f32[256,16,128]{2,1,0:T(8,128)} async-done(((f32[256,16,128]{2,1,0:T(8,128)}), f32[256,16,128]{2,1,0:T(8,128)}, u32[]{:S(2)}, u32[]{:S(2)}) %all-to-all-start.2) | async-done | bytes 2097184 | tf_op jit(solution)/shard_map/all_to_all | solution.py:317
  216.6 6.4 %analysis.1 = (f32[2,512,512]{2,1,0:T(8,128)}, f32[2,512,512]{2,1,0:T(8,128)}) custom-call(s32[1]{0:T(128)} %bitcast.first_ref, f32[2]{0:T(128)S(1)} %pad_maximum_fusion.step_ref, f32[8,32,2,8,128]{4,3,2,1,0:T(8,128)} %bitcast.15.field_ref, f32[2,512,512]{2,1,0:T(8,128)} %white_ref.3, bf16[2,512,512]{2,1,0:T(8,128)(2,1)S(1)} %copy-done.3, ...), custom_call_target="tpu_custom_call" | custom-call | flops 1610612736 | bytes 12582912 | tf_op jit(solution)/shard_map/analysis/pallas_call | solution.py:323
  (45 shorter events, 14.9 us)
Async XLA Ops:
  6.3 70.2 %all-to-all-start = ((f32[256,16,128]{2,1,0:T(8,128)}), f32[256,16,128]{2,1,0:T(8,128)S(1)}, u32[]{:S(2)}, u32[]{:S(2)}) async-start(f32[256,16,128]{2,1,0:T(8,128)} %bitcast.34), calls=%async_computation | async-start | bytes 4194304 | tf_op jit(solution)/shard_map/all_to_all | solution.py:276
  24.7 7.3 %copy-start.8 = (s32[1,1,4096]{2,1,0:T(1,128)S(1)}, s32[1,1,4096]{2,1,0:T(1,128)}, u32[]{:S(2)}) copy-start(s32[1,1,4096]{2,1,0:T(1,128)} %param.12) | copy-start | bytes 49156
  26.6 28.3 %collective-permute-start = (s32[32,32,128]{2,1,0:T(8,128)}, s32[32,32,128]{2,1,0:T(8,128)}, u32[]{:S(2)}, u32[]{:S(2)}) collective-permute-start(s32[32,32,128]{2,1,0:T(8,128)} %rev.23), channel_id=1, source_target_pairs={{0,3},{1,0},{2,1},{3,2},{4,7},{5,4},{6,5},{7,6},{8,11},{9,8},{10,9... | collective-permute-start | bytes 1572872 | tf_op jit(solution)/shard_map/ppermute | solution.py:201
  30.1 24.9 %collective-permute-start.1 = (s32[32,32,128]{2,1,0:T(8,128)}, s32[32,32,128]{2,1,0:T(8,128)}, u32[]{:S(2)}, u32[]{:S(2)}) collective-permute-start(s32[32,32,128]{2,1,0:T(8,128)} %rev.24), channel_id=1, source_target_pairs={{0,2},{1,3},{2,0},{3,1},{4,6},{5,7},{6,4},{7,5},{8,10},{9,11},{10,... | collective-permute-start | bytes 1572872 | tf_op jit(solution)/shard_map/ppermute | solution.py:201
  31.5 42.0 %collective-permute-start.2 = (s32[32,32,128]{2,1,0:T(8,128)}, s32[32,32,128]{2,1,0:T(8,128)}, u32[]{:S(2)}, u32[]{:S(2)}) collective-permute-start(s32[32,32,128]{2,1,0:T(8,128)} %rev.25), channel_id=1, source_target_pairs={{0,1},{1,2},{2,3},{3,0},{4,5},{5,6},{6,7},{7,4},{8,9},{9,10},{10,1... | collective-permute-start | bytes 1572872 | tf_op jit(solution)/shard_map/ppermute | solution.py:201
  47.4 26.0 %copy-start.7 = (s32[32,32,128]{2,1,0:T(8,128)S(1)}, s32[32,32,128]{2,1,0:T(8,128)}, u32[]{:S(2)}) copy-start(s32[32,32,128]{2,1,0:T(8,128)} %get-tuple-element.12) | copy-start | bytes 1572868
  50.6 24.1 %copy-start.6 = (s32[32,128,128]{2,1,0:T(8,128)S(1)}, s32[32,128,128]{2,1,0:T(8,128)}, u32[]{:S(2)}) copy-start(s32[32,128,128]{2,1,0:T(8,128)} %rev.22) | copy-start | bytes 6291460
  76.5 65.6 %all-to-all-start.1 = ((s32[32,160,128]{2,1,0:T(8,128)}), s32[32,160,128]{2,1,0:T(8,128)}, u32[]{:S(2)}, u32[]{:S(2)}) async-start(s32[32,160,128]{2,1,0:T(8,128)} %pad_add_fusion), calls=%async_computation.1 | async-start | bytes 5242880 | tf_op jit(solution)/shard_map/all_to_all | solution.py:282
  99.4 8.7 %copy-start = (bf16[6,256,256]{2,1,0:T(8,128)(2,1)S(1)}, bf16[6,256,256]{2,1,0:T(8,128)(2,1)}, u32[]{:S(2)}) copy-start(bf16[6,256,256]{2,1,0:T(8,128)(2,1)} %constant.121.clone.tables_ref) | copy-start | bytes 2359300
  108.1 1.6 copy-start.5
  109.7 1.3 copy-start.2
  150.3 13.6 %copy-start.9 = (s32[64]{0:T(128)S(1)}, s32[64]{0:T(128)}, u32[]{:S(2)}) copy-start(s32[64]{0:T(128)} %param.16) | copy-start | bytes 772
  150.3 66.3 %copy-start.1 = (bf16[6,256,256]{2,1,0:T(8,128)(2,1)S(1)}, bf16[6,256,256]{2,1,0:T(8,128)(2,1)}, u32[]{:S(2)}) copy-start(bf16[6,256,256]{2,1,0:T(8,128)(2,1)} %constant.121.clone.tables_ref) | copy-start | bytes 2359300
  150.3 66.3 %copy-start.3 = (bf16[2,512,512]{2,1,0:T(8,128)(2,1)S(1)}, bf16[2,512,512]{2,1,0:T(8,128)(2,1)}, u32[]{:S(2)}) copy-start(bf16[2,512,512]{2,1,0:T(8,128)(2,1)} %amplitude_ref.3) | copy-start | bytes 3145732
  150.3 66.3 %copy-start.4 = (bf16[2,512,512]{2,1,0:T(8,128)(2,1)S(1)}, bf16[2,512,512]{2,1,0:T(8,128)(2,1)}, u32[]{:S(2)}) copy-start(bf16[2,512,512]{2,1,0:T(8,128)(2,1)} %kick_ref.1) | copy-start | bytes 3145732
  150.3 66.3 %all-to-all-start.2 = ((f32[256,16,128]{2,1,0:T(8,128)}), f32[256,16,128]{2,1,0:T(8,128)}, u32[]{:S(2)}, u32[]{:S(2)}) async-start(f32[256,16,128]{2,1,0:T(8,128)} %bitcast.35), calls=%async_computation.2 | async-start | bytes 4194304 | tf_op jit(solution)/shard_map/all_to_all | solution.py:317

commit v8 on v6

--- a/solution.py
+++ b/solution.py
@@ -11,6 +11,7 @@
 BLOCK = 128
 HALF = BLOCK // 2
 WIDTH = 4
+ROWS = 8
 GROUP = 128
 VMEM_BYTES = 56 * 1024 * 1024
 
@@ -51,9 +52,12 @@
 
 
 def live_amplitude(first, amplitude):
-    rows = lax.broadcasted_iota(jnp.int32, amplitude.shape, 0)
-    cols = lax.broadcasted_iota(jnp.int32, amplitude.shape, 1)
-    return jnp.where(rows + cols + first == 0, 0.0, amplitude.astype(jnp.float32))
+    amplitude = amplitude.astype(jnp.float32)
+    top = amplitude[:ROWS]
+    rows = lax.broadcasted_iota(jnp.int32, top.shape, 0)
+    cols = lax.broadcasted_iota(jnp.int32, top.shape, 1)
+    top = jnp.where(rows + cols + first == 0, 0.0, top)
+    return jnp.concatenate([top, amplitude[ROWS:]], axis=0)
 
 
 def table_pairs(tables_ref):
@@ -156,30 +160,49 @@
 
 
 def analysis_kernel(
-    first_ref, step_ref, field_ref, white_ref, amplitude_ref, kick_ref, tables_ref, grad_ref, next_ref, back_ref
+    first_ref, step_ref, field_any, white_any, amplitude_ref, kick_ref, tables_ref,
+    grad_any, next_any, field_ref, white_ref, grad_ref, next_ref, back_ref, load_sems, sems,
 ):
+    loads = [
+        [
+            pltpu.make_async_copy(field_any.at[:, :, plane], field_ref.at[plane], load_sems.at[plane, 0]),
+            pltpu.make_async_copy(white_any.at[plane], white_ref.at[plane], load_sems.at[plane, 1]),
+        ]
+        for plane in range(white_ref.shape[0])
+    ]
+    for copy in sum(loads, []):
+        copy.start()
     even_table, odd_table, _ = table_pairs(tables_ref)
     tiles, size, _ = back_ref.shape
-    lower, upper = [], []
-    for pair in range(field_ref.shape[0] // 2):
-        left = field_ref[2 * pair, :, 0].reshape(-1, BLOCK)
-        right = field_ref[2 * pair + 1, :, 0].reshape(-1, BLOCK)
-        mask = first_half(left.shape)
-        lower.append(jnp.where(mask, left, right))
-        upper.append(swap_halves(jnp.where(mask, right, left)))
-    transposed = ((1,), (1,))
-    folded = [fold(jnp.concatenate(part, axis=1), 1) for part in (lower, upper)]
-    for parity, table in enumerate([even_table, odd_table]):
-        passed = [split(product(table, split(part[parity]), transposed)) for part in folded]
-        back = unfold(product(passed[0], even_table), product(passed[1], odd_table), 1)
-        for tile in range(tiles):
-            rows = pl.ds(parity, size // 2, stride=2)
-            back_ref[tile, rows, :] = back[:, tile * BLOCK : (tile + 1) * BLOCK]
-    back = jnp.concatenate([back_ref[tile] for tile in range(tiles)], axis=1)
-    white = white_ref[0]
-    gradient = live_amplitude(first_ref[0] + pl.program_id(0), amplitude_ref[0]) * back - white
-    grad_ref[0] = gradient
-    next_ref[0] = white + step_ref[0] * gradient + step_ref[1] * kick_ref[0].astype(jnp.float32)
+    stores = []
+    for plane in range(white_ref.shape[0]):
+        loads[plane][0].wait()
+        lower, upper = [], []
+        for pair in range(field_ref.shape[1] // 2):
+            left = field_ref[plane, 2 * pair].reshape(-1, BLOCK)
+            right = field_ref[plane, 2 * pair + 1].reshape(-1, BLOCK)
+            mask = first_half(left.shape)
+            lower.append(jnp.where(mask, left, right))
+            upper.append(swap_halves(jnp.where(mask, right, left)))
+        transposed = ((1,), (1,))
+        folded = [fold(jnp.concatenate(part, axis=1), 1) for part in (lower, upper)]
+        for parity, table in enumerate([even_table, odd_table]):
+            passed = [split(product(table, split(part[parity]), transposed)) for part in folded]
+            back = unfold(product(passed[0], even_table), product(passed[1], odd_table), 1)
+            for tile in range(tiles):
+                rows = pl.ds(parity, size // 2, stride=2)
+                back_ref[tile, rows, :] = back[:, tile * BLOCK : (tile + 1) * BLOCK]
+        back = jnp.concatenate([back_ref[tile] for tile in range(tiles)], axis=1)
+        loads[plane][1].wait()
+        white = white_ref[plane]
+        gradient = live_amplitude(first_ref[0] + plane, amplitude_ref[plane]) * back - white
+        grad_ref[plane] = gradient
+        next_ref[plane] = white + step_ref[0] * gradient + step_ref[1] * kick_ref[plane].astype(jnp.float32)
+        for n, (source, target) in enumerate([(grad_ref, grad_any), (next_ref, next_any)]):
+            stores.append(pltpu.make_async_copy(source.at[plane], target.at[plane], sems.at[plane, n]))
+            stores[-1].start()
+    for copy in stores:
+        copy.wait()
 
 
 def adapted_step(accepted):
@@ -293,6 +316,7 @@
             name="expected_counts",
         )(field.reshape(cells), bias_grid, density_grid, tables)
         inside = pl.BlockSpec(memory_space=pltpu.VMEM)
+        anywhere = pl.BlockSpec(memory_space=pl.ANY)
         back = pl.pallas_call(
             gradient_kernel,
             in_specs=[scalar, inside, inside, pl.BlockSpec(memory_space=pl.ANY), inside],
@@ -315,11 +339,18 @@
         out_plane = jax.ShapeDtypeStruct(white_noise.shape, jnp.float32)
         return pl.pallas_call(
             analysis_kernel,
-            grid=(depth,),
-            in_specs=[scalar, scalar, packed, plane, plane, plane, whole(tables)],
-            out_specs=(plane, plane),
+            in_specs=[scalar, scalar, anywhere, anywhere, inside, inside, inside],
+            out_specs=(anywhere, anywhere),
             out_shape=(out_plane, out_plane),
-            scratch_shapes=[tiled],
+            scratch_shapes=[
+                pltpu.VMEM((depth, rows_px, rows_py, rows_y, BLOCK), jnp.float32),
+                pltpu.VMEM(white_noise.shape, jnp.float32),
+                pltpu.VMEM(white_noise.shape, jnp.float32),
+                pltpu.VMEM(white_noise.shape, jnp.float32),
+                tiled,
+                pltpu.SemaphoreType.DMA((depth, 2)),
+                pltpu.SemaphoreType.DMA((depth, 2)),
+            ],
             compiler_params=pltpu.CompilerParams(vmem_limit_bytes=50 * 2**20),
             cost_estimate=pl.CostEstimate(flops=flops, bytes_accessed=12 * 2**20, transcendentals=0),
             name="analysis",

time: 221 us -> 221 us (level)
  no operation moved by 1% of the time
where the time goes in v8:
time: 221 us
  waiting for transfers between devices  113 us (51%)
  starting transfers between devices  39 us (18%)
  other arithmetic  23.7 us (11%)
  Pallas kernels  21.4 us (10%)
  local copies, waits for them, and re-layouts  21 us (10%)
  between operations  2.33 us (1%)
    all_to_all x1, waiting for transfers between devices, body(): lax.all_to_all(back.reshape(devices, chunk, BLOCK), ('px', 'py'), split_a...  51.3 us
    all_to_all x1, waiting for transfers between devices, body(): lax.all_to_all(outgoing, 'py', split_axis=0, concat_axis=0, tiled=True)  34.3 us
    ppermute x3, waiting for transfers between devices, spread_ranks(): lax.ppermute(part(shift), 'py', pairs)  25.5 us
    all_to_all x1, starting transfers between devices, body(): lax.all_to_all(sent.reshape(devices, chunk, BLOCK), ('px', 'py'), split_a...  15.7 us
    all_to_all x1, starting transfers between devices, body(): lax.all_to_all(back.reshape(devices, chunk, BLOCK), ('px', 'py'), split_a...  12.3 us
    another operation x3, other arithmetic  9.62 us
    transpose x2, other arithmetic, by_column(): return grid.transpose(3, 1, 2, 0).reshape(quarters, -1)  8.24 us
    pallas_call x1, Pallas kernels, body(): pl.pallas_call(gradient_kernel, in_specs=[scalar, inside, inside, pl.Bloc...  8.22 us
  transfers between devices with their start and end apart: 6, of which 5 were waited for; matrix products, arithmetic and copies ran while one was open for 20% of the time, Pallas kernels for 1%

profile of v8, /device:TPU:1, one launch (start us, length us, event | category | flops | bytes accessed | tf_op | source)
XLA Modules:
  0.0 220.8 jit_solution(3624888971656404272)
XLA Ops:
  0.6 5.3 %synthesis.1 = f32[8,32,2,8,128]{4,3,2,1,0:T(8,128)} custom-call(s32[1]{0:T(128)} %bitcast.first_ref, f32[2,512,512]{2,1,0:T(8,128)} %white_any.1, bf16[2,512,512]{2,1,0:T(8,128)(2,1)} %amplitude_ref.3, bf16[6,256,256]{2,1,0:T(8,128)(2,1)} %constant.120.clone.tables_ref), custom_call_target="tpu_custom_call" | custom-call | flops 1610612736 | bytes 8388608 | tf_op jit(solution)/shard_map/synthesis/pallas_call | solution.py:286
  5.9 15.7 %all-to-all-start = ((f32[256,16,128]{2,1,0:T(8,128)}), f32[256,16,128]{2,1,0:T(8,128)S(1)}, u32[]{:S(2)}, u32[]{:S(2)}) async-start(f32[256,16,128]{2,1,0:T(8,128)} %bitcast.34), calls=%async_computation | async-start | bytes 4194304 | tf_op jit(solution)/shard_map/all_to_all | solution.py:299
  21.6 2.6 %fusion.10 = (s32[32,32,128]{2,1,0:T(8,128)}, s32[32,32,128]{2,1,0:T(8,128)}, s32[32,32,128]{2,1,0:T(8,128)}) fusion(s32[32,256,128]{2,1,0:T(8,128)} %bitcast.36), kind=kLoop, calls=%fused_computation.42 | loop fusion | bytes 3145728 | tf_op jit(solution)/shard_map/slice | solution.py:220
  24.1 1.4 collective-permute-start.2
  25.5 2.4 %collective-permute-start.1 = (s32[32,32,128]{2,1,0:T(8,128)}, s32[32,32,128]{2,1,0:T(8,128)}, u32[]{:S(2)}, u32[]{:S(2)}) collective-permute-start(s32[32,32,128]{2,1,0:T(8,128)} %get-tuple-element.13), channel_id=1, source_target_pairs={{0,2},{1,3},{2,0},{3,1},{4,6},{5,7},{6,4},{7,5},{8,10},{9,11},{10,... | collective-permute-start | bytes 1572872 | tf_op jit(solution)/shard_map/ppermute | solution.py:224
  29.2 9.2 %reduce-window.6 = s32[32,32,128]{2,1,0:T(8,128)S(1)} reduce-window(s32[32,32,128]{2,1,0:T(8,128)S(1)} %fusion.9, s32[]{:T(128)} %constant.108.clone.1), window={size=1x1x128 pad=0_0x0_0x127_0}, to_apply=%region_1.2 | reduce-window | flops 16646144 | bytes 1048580 | tf_op jit(solution)/shard_map/reduce-window
  41.2 3.1 %slice.30 = s32[32,128,128]{2,1,0:T(8,128)} slice(s32[32,256,128]{2,1,0:T(8,128)} %bitcast.37), slice={[0:32], [0:128], [0:128]} | slice | bytes 4194304 | tf_op jit(solution)/shard_map/slice | solution.py:303
  45.1 24.7 %collective-permute-done.1 = s32[32,32,128]{2,1,0:T(8,128)} collective-permute-done((s32[32,32,128]{2,1,0:T(8,128)}, s32[32,32,128]{2,1,0:T(8,128)}, u32[]{:S(2)}, u32[]{:S(2)}) %collective-permute-start.1) | collective-permute-done | bytes 524320 | tf_op jit(solution)/shard_map/ppermute | solution.py:224
  69.8 1.4 fusion.8
  71.3 1.8 pad_add_fusion
  73.0 2.2 all-to-all-done
  75.2 6.1 %all-to-all-start.1 = ((s32[32,160,128]{2,1,0:T(8,128)}), s32[32,160,128]{2,1,0:T(8,128)}, u32[]{:S(2)}, u32[]{:S(2)}) async-start(s32[32,160,128]{2,1,0:T(8,128)} %pad_add_fusion), calls=%async_computation.1 | async-start | bytes 5242880 | tf_op jit(solution)/shard_map/all_to_all | solution.py:305
  83.3 2.2 %rev.7 = s32[64,8,2,4]{3,2,1,0:T(2,128)} reverse(s32[64,8,2,4]{3,2,1,0:T(2,128)S(1)} %reshape.52), dimensions={2} | reverse | bytes 32768 | tf_op jit(solution)/shard_map/rev | solution.py:268
  85.6 1.6 sub.32
  87.2 1.6 sub.34
  88.8 6.1 %select_bitcast_fusion = (s32[4,8,2,64]{0,2,1,3:T(2,128)}, s32[64,8,2,4]{3,2,1,0:T(2,128)S(1)}) fusion(s32[64,8,2,4]{3,2,1,0:T(2,128)S(1)} %reshape.52, s32[64,8,2,4]{3,2,1,0:T(2,128)} %rev.7, pred[]{:T(512)S(6)} %eq.62, s32[64,8,2,4]{3,2,1,0:T(2,128)} %sub.32, s32[64,8,2,4]{3,2,1,0:T(2,128)} %sub.34), kind=kLoop, calls=%fused_computation.28 | loop fusion | flops 225280 | bytes 98305 | tf_op jit(solution)/shard_map/transpose | solution.py:269
  96.4 2.2 rev.6
  98.6 2.1 select_bitcast_fusion.1
  103.7 1.5 expected_counts.1.expected_any
  106.5 34.3 %all-to-all-done.1 = s32[32,160,128]{2,1,0:T(8,128)} async-done(((s32[32,160,128]{2,1,0:T(8,128)}), s32[32,160,128]{2,1,0:T(8,128)}, u32[]{:S(2)}, u32[]{:S(2)}) %all-to-all-start.1) | async-done | bytes 2621472 | tf_op jit(solution)/shard_map/all_to_all | solution.py:305
  140.9 8.2 %shell_gradient.1 = f32[4096,128]{1,0:T(8,128)} custom-call(s32[4096]{0:T(1024)} %reshape_reshape.4.slot_ref, s32[5120,128]{1,0:T(8,128)} %bitcast.9.counts_ref, f32[4,1024]{1,0:T(4,128)} %copy-done.5, f32[512,1024]{1,0:T(8,128)} %copy-done.2, bf16[6,256,256]{2,1,0:T(8,128)(2,1)} %constant.120.clone.tables_ref), custom_call_target="tpu_custom_call" | custom-call | flops 805306368 | bytes 8388608 | tf_op jit(solution)/shard_map/shell_gradient/pallas_call | solution.py:320
  149.1 12.3 %all-to-all-start.2 = ((f32[256,16,128]{2,1,0:T(8,128)}), f32[256,16,128]{2,1,0:T(8,128)}, u32[]{:S(2)}, u32[]{:S(2)}) async-start(f32[256,16,128]{2,1,0:T(8,128)} %bitcast.35), calls=%async_computation.2 | async-start | bytes 4194304 | tf_op jit(solution)/shard_map/all_to_all | solution.py:334
  162.9 51.3 %all-to-all-done.2 = f32[256,16,128]{2,1,0:T(8,128)} async-done(((f32[256,16,128]{2,1,0:T(8,128)}), f32[256,16,128]{2,1,0:T(8,128)}, u32[]{:S(2)}, u32[]{:S(2)}) %all-to-all-start.2) | async-done | bytes 2097184 | tf_op jit(solution)/shard_map/all_to_all | solution.py:334
  214.2 6.4 %analysis.1 = (f32[2,512,512]{2,1,0:T(8,128)}, f32[2,512,512]{2,1,0:T(8,128)}) custom-call(s32[1]{0:T(128)} %bitcast.first_ref, f32[2]{0:T(128)S(1)} %pad_maximum_fusion.step_ref, f32[8,32,2,8,128]{4,3,2,1,0:T(8,128)} %bitcast.15.field_any, f32[2,512,512]{2,1,0:T(8,128)} %white_any.1, bf16[2,512,512]{2,1,0:T(8,128)(2,1)S(1)} %copy-done.3, ...), custom_call_target="tpu_custom_call" | custom-call | flops 1610612736 | bytes 12582912 | tf_op jit(solution)/shard_map/analysis/pallas_call | solution.py:340
  (39 shorter events, 12.6 us)
Async XLA Ops:
  5.9 69.3 %all-to-all-start = ((f32[256,16,128]{2,1,0:T(8,128)}), f32[256,16,128]{2,1,0:T(8,128)S(1)}, u32[]{:S(2)}, u32[]{:S(2)}) async-start(f32[256,16,128]{2,1,0:T(8,128)} %bitcast.34), calls=%async_computation | async-start | bytes 4194304 | tf_op jit(solution)/shard_map/all_to_all | solution.py:299
  21.6 7.5 %copy-start.7 = (s32[1,1,4096]{2,1,0:T(1,128)S(1)}, s32[1,1,4096]{2,1,0:T(1,128)}, u32[]{:S(2)}) copy-start(s32[1,1,4096]{2,1,0:T(1,128)} %param.12) | copy-start | bytes 49156
  24.1 21.0 %collective-permute-start.2 = (s32[32,32,128]{2,1,0:T(8,128)}, s32[32,32,128]{2,1,0:T(8,128)}, u32[]{:S(2)}, u32[]{:S(2)}) collective-permute-start(s32[32,32,128]{2,1,0:T(8,128)} %get-tuple-element.12), channel_id=1, source_target_pairs={{0,1},{1,2},{2,3},{3,0},{4,5},{5,6},{6,7},{7,4},{8,9},{9,10},{10,1... | collective-permute-start | bytes 1572872 | tf_op jit(solution)/shard_map/ppermute | solution.py:224
  25.5 44.3 %collective-permute-start.1 = (s32[32,32,128]{2,1,0:T(8,128)}, s32[32,32,128]{2,1,0:T(8,128)}, u32[]{:S(2)}, u32[]{:S(2)}) collective-permute-start(s32[32,32,128]{2,1,0:T(8,128)} %get-tuple-element.13), channel_id=1, source_target_pairs={{0,2},{1,3},{2,0},{3,1},{4,6},{5,7},{6,4},{7,5},{8,10},{9,11},{10,... | collective-permute-start | bytes 1572872 | tf_op jit(solution)/shard_map/ppermute | solution.py:224
  27.9 41.9 %collective-permute-start = (s32[32,32,128]{2,1,0:T(8,128)}, s32[32,32,128]{2,1,0:T(8,128)}, u32[]{:S(2)}, u32[]{:S(2)}) collective-permute-start(s32[32,32,128]{2,1,0:T(8,128)} %get-tuple-element.14), channel_id=1, source_target_pairs={{0,3},{1,0},{2,1},{3,2},{4,7},{5,4},{6,5},{7,6},{8,11},{9,8},{10,9... | collective-permute-start | bytes 1572872 | tf_op jit(solution)/shard_map/ppermute | solution.py:224
  44.4 26.9 %copy-start.6 = (s32[32,128,128]{2,1,0:T(8,128)S(1)}, s32[32,128,128]{2,1,0:T(8,128)}, u32[]{:S(2)}) copy-start(s32[32,128,128]{2,1,0:T(8,128)} %slice.30) | copy-start | bytes 6291460
  75.2 65.6 %all-to-all-start.1 = ((s32[32,160,128]{2,1,0:T(8,128)}), s32[32,160,128]{2,1,0:T(8,128)}, u32[]{:S(2)}, u32[]{:S(2)}) async-start(s32[32,160,128]{2,1,0:T(8,128)} %pad_add_fusion), calls=%async_computation.1 | async-start | bytes 5242880 | tf_op jit(solution)/shard_map/all_to_all | solution.py:305
  94.9 8.7 %copy-start = (bf16[6,256,256]{2,1,0:T(8,128)(2,1)S(1)}, bf16[6,256,256]{2,1,0:T(8,128)(2,1)}, u32[]{:S(2)}) copy-start(bf16[6,256,256]{2,1,0:T(8,128)(2,1)} %constant.120.clone.tables_ref) | copy-start | bytes 2359300
  103.6 1.6 copy-start.5
  105.2 1.3 copy-start.2
  149.1 12.4 %copy-start.8 = (s32[64]{0:T(128)S(1)}, s32[64]{0:T(128)}, u32[]{:S(2)}) copy-start(s32[64]{0:T(128)} %param.16) | copy-start | bytes 772
  149.1 65.1 %copy-start.1 = (bf16[6,256,256]{2,1,0:T(8,128)(2,1)S(1)}, bf16[6,256,256]{2,1,0:T(8,128)(2,1)}, u32[]{:S(2)}) copy-start(bf16[6,256,256]{2,1,0:T(8,128)(2,1)} %constant.120.clone.tables_ref) | copy-start | bytes 2359300
  149.1 65.1 %copy-start.3 = (bf16[2,512,512]{2,1,0:T(8,128)(2,1)S(1)}, bf16[2,512,512]{2,1,0:T(8,128)(2,1)}, u32[]{:S(2)}) copy-start(bf16[2,512,512]{2,1,0:T(8,128)(2,1)} %amplitude_ref.3) | copy-start | bytes 3145732
  149.1 65.1 %copy-start.4 = (bf16[2,512,512]{2,1,0:T(8,128)(2,1)S(1)}, bf16[2,512,512]{2,1,0:T(8,128)(2,1)}, u32[]{:S(2)}) copy-start(bf16[2,512,512]{2,1,0:T(8,128)(2,1)} %kick_ref.1) | copy-start | bytes 3145732
  149.1 65.0 %all-to-all-start.2 = ((f32[256,16,128]{2,1,0:T(8,128)}), f32[256,16,128]{2,1,0:T(8,128)}, u32[]{:S(2)}, u32[]{:S(2)}) async-start(f32[256,16,128]{2,1,0:T(8,128)} %bitcast.35), calls=%async_computation.2 | async-start | bytes 4194304 | tf_op jit(solution)/shard_map/all_to_all | solution.py:334

commit v9 on v7

--- a/solution.py
+++ b/solution.py
@@ -11,6 +11,7 @@
 BLOCK = 128
 HALF = BLOCK // 2
 WIDTH = 4
+ROWS = 8
 GROUP = 128
 VMEM_BYTES = 56 * 1024 * 1024
 
@@ -51,9 +52,12 @@
 
 
 def live_amplitude(first, amplitude):
-    rows = lax.broadcasted_iota(jnp.int32, amplitude.shape, 0)
-    cols = lax.broadcasted_iota(jnp.int32, amplitude.shape, 1)
-    return jnp.where(rows + cols + first == 0, 0.0, amplitude.astype(jnp.float32))
+    amplitude = amplitude.astype(jnp.float32)
+    top = amplitude[:ROWS]
+    rows = lax.broadcasted_iota(jnp.int32, top.shape, 0)
+    cols = lax.broadcasted_iota(jnp.int32, top.shape, 1)
+    top = jnp.where(rows + cols + first == 0, 0.0, top)
+    return jnp.concatenate([top, amplitude[ROWS:]], axis=0)
 
 
 def table_pairs(tables_ref):
@@ -194,7 +198,7 @@
     size, capacity, _ = counts.shape
     width = (capacity - keep) // WIDTH
     away = (col_index - heavy) % WIDTH
-    part = lambda k: counts[::-1, keep + k * width : keep + (k + 1) * width]
+    part = lambda k: counts[:, keep + k * width : keep + (k + 1) * width]
     mine = part(0)
     for shift in range(1, WIDTH):
         pairs = [(i, i // WIDTH * WIDTH + (i + shift) % WIDTH) for i in range(size)]
@@ -277,7 +281,8 @@
             sent.reshape(devices, chunk, BLOCK), ("px", "py"), split_axis=0, concat_axis=0, tiled=True
         )
 
-        outgoing = jnp.concatenate([galaxy_in[::-1, :keep], spread_ranks(galaxy_in, keep, heavy, col_index)], axis=1)
+        spread = spread_ranks(galaxy_in, keep, heavy, col_index)
+        outgoing = jnp.concatenate([galaxy_in[::-1, :keep], spread[::-1]], axis=1)
         outgoing, field = lax.optimization_barrier((outgoing, field))
         counts = lax.all_to_all(
             outgoing,

time: 224 us -> 222 us (level)
  local copies, waits for them, and re-layouts: 28 us -> 24.2 us
    rev x4 -> x2, local copies, waits for them, and re-layouts: 6.77 us -> 3.17 us  [body(): outgoing = jnp.concatenate([galaxy_in[::-1, :keep], spread[::-1]], axis=1)]
  transfers between devices with their start and end apart: 6 -> 6, of which waited for: 4 -> 4; matrix products, arithmetic and copies ran while one was open for 23% -> 22% of each run, Pallas kernels for 1% -> 1%
where the time goes in v9:
time: 222 us
  waiting for transfers between devices  105 us (47%)
  starting transfers between devices  44 us (20%)
  other arithmetic  25.5 us (11%)
  local copies, waits for them, and re-layouts  24.2 us (11%)
  Pallas kernels  21.2 us (10%)
  between operations  2.25 us (1%)
    all_to_all x1, waiting for transfers between devices, body(): lax.all_to_all(back.reshape(devices, chunk, BLOCK), ('px', 'py'), split_a...  51.3 us
    all_to_all x1, waiting for transfers between devices, body(): lax.all_to_all(outgoing, 'py', split_axis=0, concat_axis=0, tiled=True, a...  30.7 us
    ppermute x3, waiting for transfers between devices, spread_ranks(): lax.ppermute(part(shift), 'py', pairs)  22.2 us
    all_to_all x1, starting transfers between devices, body(): lax.all_to_all(sent.reshape(devices, chunk, BLOCK), ('px', 'py'), split_a...  15.7 us
    all_to_all x1, starting transfers between devices, body(): lax.all_to_all(back.reshape(devices, chunk, BLOCK), ('px', 'py'), split_a...  14.4 us
    another operation x3, other arithmetic  9.62 us
    all_to_all x1, starting transfers between devices, body(): lax.all_to_all(outgoing, 'py', split_axis=0, concat_axis=0, tiled=True, a...  8.99 us
    transpose x2, other arithmetic, by_column(): return grid.transpose(3, 1, 2, 0).reshape(quarters, -1)  8.37 us
  transfers between devices with their start and end apart: 6, of which 4 were waited for; matrix products, arithmetic and copies ran while one was open for 22% of the time, Pallas kernels for 1%

profile of v9, /device:TPU:1, one launch (start us, length us, event | category | flops | bytes accessed | tf_op | source)
XLA Modules:
  0.0 221.8 jit_solution(3611486406986049369)
XLA Ops:
  0.6 5.3 %synthesis.1 = f32[8,32,2,8,128]{4,3,2,1,0:T(8,128)} custom-call(s32[1]{0:T(128)} %bitcast.first_ref, f32[2,512,512]{2,1,0:T(8,128)} %white_ref.3, bf16[2,512,512]{2,1,0:T(8,128)(2,1)} %amplitude_ref.3, bf16[6,256,256]{2,1,0:T(8,128)(2,1)} %constant.121.clone.tables_ref), custom_call_target="tpu_custom_call" | custom-call | flops 1610612736 | bytes 8388608 | tf_op jit(solution)/shard_map/synthesis/pallas_call | solution.py:267
  5.9 15.7 %all-to-all-start = ((f32[256,16,128]{2,1,0:T(8,128)}), f32[256,16,128]{2,1,0:T(8,128)S(1)}, u32[]{:S(2)}, u32[]{:S(2)}) async-start(f32[256,16,128]{2,1,0:T(8,128)} %bitcast.34), calls=%async_computation | async-start | bytes 4194304 | tf_op jit(solution)/shard_map/all_to_all | solution.py:280
  21.6 2.6 %fusion.10 = (s32[32,32,128]{2,1,0:T(8,128)}, s32[32,32,128]{2,1,0:T(8,128)}, s32[32,32,128]{2,1,0:T(8,128)}) fusion(s32[32,256,128]{2,1,0:T(8,128)} %bitcast.36), kind=kLoop, calls=%fused_computation.42 | loop fusion | bytes 3145728 | tf_op jit(solution)/shard_map/slice | solution.py:201
  24.2 1.4 collective-permute-start.2
  25.6 2.4 %collective-permute-start.1 = (s32[32,32,128]{2,1,0:T(8,128)}, s32[32,32,128]{2,1,0:T(8,128)}, u32[]{:S(2)}, u32[]{:S(2)}) collective-permute-start(s32[32,32,128]{2,1,0:T(8,128)} %get-tuple-element.13), channel_id=1, source_target_pairs={{0,2},{1,3},{2,0},{3,1},{4,6},{5,7},{6,4},{7,5},{8,10},{9,11},{10,... | collective-permute-start | bytes 1572872 | tf_op jit(solution)/shard_map/ppermute | solution.py:205
  29.2 9.2 %reduce-window.6 = s32[32,32,128]{2,1,0:T(8,128)S(1)} reduce-window(s32[32,32,128]{2,1,0:T(8,128)S(1)} %fusion.9, s32[]{:T(128)} %constant.109.clone.1), window={size=1x1x128 pad=0_0x0_0x127_0}, to_apply=%region_1.2 | reduce-window | flops 16646144 | bytes 1048580 | tf_op jit(solution)/shard_map/reduce-window
  41.4 3.1 %slice.30 = s32[32,128,128]{2,1,0:T(8,128)} slice(s32[32,256,128]{2,1,0:T(8,128)} %bitcast.37), slice={[0:32], [0:128], [0:128]} | slice | bytes 4194304 | tf_op jit(solution)/shard_map/slice | solution.py:285
  44.5 3.1 %rev.13 = s32[32,128,128]{2,1,0:T(8,128)} reverse(s32[32,128,128]{2,1,0:T(8,128)} %slice.30), dimensions={0} | reverse | bytes 4194304 | tf_op jit(solution)/shard_map/rev | solution.py:285
  47.7 22.2 %collective-permute-done.1 = s32[32,32,128]{2,1,0:T(8,128)} collective-permute-done((s32[32,32,128]{2,1,0:T(8,128)}, s32[32,32,128]{2,1,0:T(8,128)}, u32[]{:S(2)}, u32[]{:S(2)}) %collective-permute-start.1) | collective-permute-done | bytes 524320 | tf_op jit(solution)/shard_map/ppermute | solution.py:205
  69.9 1.4 fusion.8
  71.3 3.3 %pad_add_fusion = s32[32,160,128]{2,1,0:T(8,128)} fusion(s32[32,32,128]{2,1,0:T(8,128)S(1)} %rev.14, s32[32,128,128]{2,1,0:T(8,128)} %rev.13), kind=kLoop, calls=%fused_computation | loop fusion | flops 655360 | bytes 5242880 | tf_op jit(solution)/shard_map/concatenate | solution.py:285
  75.2 9.0 %all-to-all-start.1 = ((s32[32,160,128]{2,1,0:T(8,128)}), s32[32,160,128]{2,1,0:T(8,128)}, u32[]{:S(2)}, u32[]{:S(2)}) async-start(s32[32,160,128]{2,1,0:T(8,128)} %pad_add_fusion), calls=%async_computation.1 | async-start | bytes 5242880 | tf_op jit(solution)/shard_map/all_to_all | solution.py:287
  86.3 2.2 rev.15
  88.5 1.6 sub.40
  90.1 1.6 sub.43
  91.8 6.3 %select_bitcast_fusion = (s32[4,8,2,64]{0,2,1,3:T(2,128)}, s32[64,8,2,4]{3,2,1,0:T(2,128)S(1)}) fusion(s32[64,8,2,4]{3,2,1,0:T(2,128)S(1)} %reshape.52, s32[64,8,2,4]{3,2,1,0:T(2,128)} %rev.15, pred[]{:T(512)S(6)} %eq.62, s32[64,8,2,4]{3,2,1,0:T(2,128)} %sub.40, s32[64,8,2,4]{3,2,1,0:T(2,128)} %sub.43), kind=kLoop, calls=%fused_computation.28 | loop fusion | flops 233472 | bytes 98305 | tf_op jit(solution)/shard_map/transpose | solution.py:250
  99.5 2.2 rev.12
  101.7 2.1 select_bitcast_fusion.1
  106.7 1.5 expected_counts.1.expected_any
  109.6 30.7 %all-to-all-done.1 = s32[32,160,128]{2,1,0:T(8,128)} async-done(((s32[32,160,128]{2,1,0:T(8,128)}), s32[32,160,128]{2,1,0:T(8,128)}, u32[]{:S(2)}, u32[]{:S(2)}) %all-to-all-start.1) | async-done | bytes 2621472 | tf_op jit(solution)/shard_map/all_to_all | solution.py:287
  140.3 8.2 %shell_gradient.1 = f32[4096,128]{1,0:T(8,128)} custom-call(s32[4096]{0:T(1024)} %reshape_reshape.4.slot_ref, s32[5120,128]{1,0:T(8,128)} %bitcast.9.counts_ref, f32[4,1024]{1,0:T(4,128)} %copy-done.5, f32[512,1024]{1,0:T(8,128)} %copy-done.2, bf16[6,256,256]{2,1,0:T(8,128)(2,1)} %constant.121.clone.tables_ref), custom_call_target="tpu_custom_call" | custom-call | flops 805306368 | bytes 8388608 | tf_op jit(solution)/shard_map/shell_gradient/pallas_call | solution.py:308
  148.5 14.4 %all-to-all-start.2 = ((f32[256,16,128]{2,1,0:T(8,128)}), f32[256,16,128]{2,1,0:T(8,128)}, u32[]{:S(2)}, u32[]{:S(2)}) async-start(f32[256,16,128]{2,1,0:T(8,128)} %bitcast.35), calls=%async_computation.2 | async-start | bytes 4194304 | tf_op jit(solution)/shard_map/all_to_all | solution.py:322
  164.4 51.3 %all-to-all-done.2 = f32[256,16,128]{2,1,0:T(8,128)} async-done(((f32[256,16,128]{2,1,0:T(8,128)}), f32[256,16,128]{2,1,0:T(8,128)}, u32[]{:S(2)}, u32[]{:S(2)}) %all-to-all-start.2) | async-done | bytes 2097184 | tf_op jit(solution)/shard_map/all_to_all | solution.py:322
  215.7 6.1 %analysis.1 = (f32[2,512,512]{2,1,0:T(8,128)}, f32[2,512,512]{2,1,0:T(8,128)}) custom-call(s32[1]{0:T(128)} %bitcast.first_ref, f32[2]{0:T(128)S(1)} %pad_maximum_fusion.step_ref, f32[8,32,2,8,128]{4,3,2,1,0:T(8,128)} %bitcast.15.field_ref, f32[2,512,512]{2,1,0:T(8,128)} %white_ref.3, bf16[2,512,512]{2,1,0:T(8,128)(2,1)S(1)} %copy-done.3, ...), custom_call_target="tpu_custom_call" | custom-call | flops 1610612736 | bytes 12582912 | tf_op jit(solution)/shard_map/analysis/pallas_call | solution.py:328
  (39 shorter events, 12.5 us)
Async XLA Ops:
  5.9 69.3 %all-to-all-start = ((f32[256,16,128]{2,1,0:T(8,128)}), f32[256,16,128]{2,1,0:T(8,128)S(1)}, u32[]{:S(2)}, u32[]{:S(2)}) async-start(f32[256,16,128]{2,1,0:T(8,128)} %bitcast.34), calls=%async_computation | async-start | bytes 4194304 | tf_op jit(solution)/shard_map/all_to_all | solution.py:280
  21.6 7.5 %copy-start.6 = (s32[1,1,4096]{2,1,0:T(1,128)S(1)}, s32[1,1,4096]{2,1,0:T(1,128)}, u32[]{:S(2)}) copy-start(s32[1,1,4096]{2,1,0:T(1,128)} %param.12) | copy-start | bytes 49156
  24.2 23.5 %collective-permute-start.2 = (s32[32,32,128]{2,1,0:T(8,128)}, s32[32,32,128]{2,1,0:T(8,128)}, u32[]{:S(2)}, u32[]{:S(2)}) collective-permute-start(s32[32,32,128]{2,1,0:T(8,128)} %get-tuple-element.12), channel_id=1, source_target_pairs={{0,1},{1,2},{2,3},{3,0},{4,5},{5,6},{6,7},{7,4},{8,9},{9,10},{10,1... | collective-permute-start | bytes 1572872 | tf_op jit(solution)/shard_map/ppermute | solution.py:205
  25.6 44.3 %collective-permute-start.1 = (s32[32,32,128]{2,1,0:T(8,128)}, s32[32,32,128]{2,1,0:T(8,128)}, u32[]{:S(2)}, u32[]{:S(2)}) collective-permute-start(s32[32,32,128]{2,1,0:T(8,128)} %get-tuple-element.13), channel_id=1, source_target_pairs={{0,2},{1,3},{2,0},{3,1},{4,6},{5,7},{6,4},{7,5},{8,10},{9,11},{10,... | collective-permute-start | bytes 1572872 | tf_op jit(solution)/shard_map/ppermute | solution.py:205
  28.0 41.9 %collective-permute-start = (s32[32,32,128]{2,1,0:T(8,128)}, s32[32,32,128]{2,1,0:T(8,128)}, u32[]{:S(2)}, u32[]{:S(2)}) collective-permute-start(s32[32,32,128]{2,1,0:T(8,128)} %get-tuple-element.14), channel_id=1, source_target_pairs={{0,3},{1,0},{2,1},{3,2},{4,7},{5,4},{6,5},{7,6},{8,11},{9,8},{10,9... | collective-permute-start | bytes 1572872 | tf_op jit(solution)/shard_map/ppermute | solution.py:205
  75.2 65.0 %all-to-all-start.1 = ((s32[32,160,128]{2,1,0:T(8,128)}), s32[32,160,128]{2,1,0:T(8,128)}, u32[]{:S(2)}, u32[]{:S(2)}) async-start(s32[32,160,128]{2,1,0:T(8,128)} %pad_add_fusion), calls=%async_computation.1 | async-start | bytes 5242880 | tf_op jit(solution)/shard_map/all_to_all | solution.py:287
  98.0 8.7 %copy-start = (bf16[6,256,256]{2,1,0:T(8,128)(2,1)S(1)}, bf16[6,256,256]{2,1,0:T(8,128)(2,1)}, u32[]{:S(2)}) copy-start(bf16[6,256,256]{2,1,0:T(8,128)(2,1)} %constant.121.clone.tables_ref) | copy-start | bytes 2359300
  106.7 1.6 copy-start.5
  108.3 1.3 copy-start.2
  148.5 14.4 %copy-start.7 = (s32[64]{0:T(128)S(1)}, s32[64]{0:T(128)}, u32[]{:S(2)}) copy-start(s32[64]{0:T(128)} %param.16) | copy-start | bytes 772
  148.5 67.2 %copy-start.1 = (bf16[6,256,256]{2,1,0:T(8,128)(2,1)S(1)}, bf16[6,256,256]{2,1,0:T(8,128)(2,1)}, u32[]{:S(2)}) copy-start(bf16[6,256,256]{2,1,0:T(8,128)(2,1)} %constant.121.clone.tables_ref) | copy-start | bytes 2359300
  148.5 67.2 %copy-start.3 = (bf16[2,512,512]{2,1,0:T(8,128)(2,1)S(1)}, bf16[2,512,512]{2,1,0:T(8,128)(2,1)}, u32[]{:S(2)}) copy-start(bf16[2,512,512]{2,1,0:T(8,128)(2,1)} %amplitude_ref.3) | copy-start | bytes 3145732
  148.5 67.1 %copy-start.4 = (bf16[2,512,512]{2,1,0:T(8,128)(2,1)S(1)}, bf16[2,512,512]{2,1,0:T(8,128)(2,1)}, u32[]{:S(2)}) copy-start(bf16[2,512,512]{2,1,0:T(8,128)(2,1)} %kick_ref.1) | copy-start | bytes 3145732
  148.5 67.1 %all-to-all-start.2 = ((f32[256,16,128]{2,1,0:T(8,128)}), f32[256,16,128]{2,1,0:T(8,128)}, u32[]{:S(2)}, u32[]{:S(2)}) async-start(f32[256,16,128]{2,1,0:T(8,128)} %bitcast.35), calls=%async_computation.2 | async-start | bytes 4194304 | tf_op jit(solution)/shard_map/all_to_all | solution.py:322

commit v10 on v6

--- a/solution.py
+++ b/solution.py
@@ -11,6 +11,7 @@
 BLOCK = 128
 HALF = BLOCK // 2
 WIDTH = 4
+ROWS = 8
 GROUP = 128
 VMEM_BYTES = 56 * 1024 * 1024
 
@@ -51,9 +52,12 @@
 
 
 def live_amplitude(first, amplitude):
-    rows = lax.broadcasted_iota(jnp.int32, amplitude.shape, 0)
-    cols = lax.broadcasted_iota(jnp.int32, amplitude.shape, 1)
-    return jnp.where(rows + cols + first == 0, 0.0, amplitude.astype(jnp.float32))
+    amplitude = amplitude.astype(jnp.float32)
+    top = amplitude[:ROWS]
+    rows = lax.broadcasted_iota(jnp.int32, top.shape, 0)
+    cols = lax.broadcasted_iota(jnp.int32, top.shape, 1)
+    top = jnp.where(rows + cols + first == 0, 0.0, top)
+    return jnp.concatenate([top, amplitude[ROWS:]], axis=0)
 
 
 def table_pairs(tables_ref):
@@ -302,7 +306,7 @@
                 pltpu.VMEM(expected.shape, jnp.float32),
                 pltpu.SemaphoreType.DMA,
             ],
-            compiler_params=pltpu.CompilerParams(vmem_limit_bytes=56 * 2**20),
+            compiler_params=pltpu.CompilerParams(vmem_limit_bytes=53 * 2**20),
             cost_estimate=pl.CostEstimate(flops=flops // 2, bytes_accessed=8 * 2**20, transcendentals=0),
             name="shell_gradient",
         )(slot_grid.reshape(-1), counts.reshape(-1, BLOCK), bias_grid, expected, tables)

time: 221 us -> 221 us (level)
  transfers between devices with their start and end apart: 6 -> 6, of which waited for: 5 -> 5; matrix products, arithmetic and copies ran while one was open for 20% -> 19% of each run, Pallas kernels for 1% -> 1%
where the time goes in v10:
time: 221 us; the launch traced here: 220 us
  waiting for transfers between devices  114 us (52%)
  starting transfers between devices  38.8 us (18%)
  other arithmetic  23.7 us (11%)
  Pallas kernels  20.9 us (9%)
  local copies, waits for them, and re-layouts  20.4 us (9%)
    all_to_all x1, waiting for transfers between devices, body(): lax.all_to_all(back.reshape(devices, chunk, BLOCK), ('px', 'py'), split_a...  51.3 us
    all_to_all x1, waiting for transfers between devices, body(): lax.all_to_all(outgoing, 'py', split_axis=0, concat_axis=0, tiled=True)  34.9 us
    ppermute x3, waiting for transfers between devices, spread_ranks(): lax.ppermute(part(shift), 'py', pairs)  25.5 us
    all_to_all x1, starting transfers between devices, body(): lax.all_to_all(sent.reshape(devices, chunk, BLOCK), ('px', 'py'), split_a...  15.7 us
    all_to_all x1, starting transfers between devices, body(): lax.all_to_all(back.reshape(devices, chunk, BLOCK), ('px', 'py'), split_a...  12.1 us
    another operation x3, other arithmetic  9.62 us
    transpose x2, other arithmetic, by_column(): return grid.transpose(3, 1, 2, 0).reshape(quarters, -1)  8.24 us
    pallas_call x1, Pallas kernels, body(): pl.pallas_call(gradient_kernel, in_specs=[scalar, inside, inside, pl.Bloc...  8.02 us
  transfers between devices with their start and end apart: 6, of which 5 were waited for; matrix products, arithmetic and copies ran while one was open for 19% of the time, Pallas kernels for 1%

profile of v10, /device:TPU:1, one launch (start us, length us, event | category | flops | bytes accessed | tf_op | source)
XLA Modules:
  0.0 219.9 jit_solution(10823814631304408900)
XLA Ops:
  0.6 5.3 %synthesis.1 = f32[8,32,2,8,128]{4,3,2,1,0:T(8,128)} custom-call(s32[1]{0:T(128)} %bitcast.first_ref, f32[2,512,512]{2,1,0:T(8,128)} %white_ref.3, bf16[2,512,512]{2,1,0:T(8,128)(2,1)} %amplitude_ref.3, bf16[6,256,256]{2,1,0:T(8,128)(2,1)} %constant.120.clone.tables_ref), custom_call_target="tpu_custom_call" | custom-call | flops 1610612736 | bytes 8388608 | tf_op jit(solution)/shard_map/synthesis/pallas_call | solution.py:267
  5.9 15.7 %all-to-all-start = ((f32[256,16,128]{2,1,0:T(8,128)}), f32[256,16,128]{2,1,0:T(8,128)S(1)}, u32[]{:S(2)}, u32[]{:S(2)}) async-start(f32[256,16,128]{2,1,0:T(8,128)} %bitcast.34), calls=%async_computation | async-start | bytes 4194304 | tf_op jit(solution)/shard_map/all_to_all | solution.py:280
  21.6 2.6 %fusion.10 = (s32[32,32,128]{2,1,0:T(8,128)}, s32[32,32,128]{2,1,0:T(8,128)}, s32[32,32,128]{2,1,0:T(8,128)}) fusion(s32[32,256,128]{2,1,0:T(8,128)} %bitcast.36), kind=kLoop, calls=%fused_computation.42 | loop fusion | bytes 3145728 | tf_op jit(solution)/shard_map/slice | solution.py:201
  24.1 1.4 collective-permute-start.2
  25.5 2.4 %collective-permute-start.1 = (s32[32,32,128]{2,1,0:T(8,128)}, s32[32,32,128]{2,1,0:T(8,128)}, u32[]{:S(2)}, u32[]{:S(2)}) collective-permute-start(s32[32,32,128]{2,1,0:T(8,128)} %get-tuple-element.13), channel_id=1, source_target_pairs={{0,2},{1,3},{2,0},{3,1},{4,6},{5,7},{6,4},{7,5},{8,10},{9,11},{10,... | collective-permute-start | bytes 1572872 | tf_op jit(solution)/shard_map/ppermute | solution.py:205
  29.2 9.2 %reduce-window.6 = s32[32,32,128]{2,1,0:T(8,128)S(1)} reduce-window(s32[32,32,128]{2,1,0:T(8,128)S(1)} %fusion.9, s32[]{:T(128)} %constant.108.clone.1), window={size=1x1x128 pad=0_0x0_0x127_0}, to_apply=%region_1.2 | reduce-window | flops 16646144 | bytes 1048580 | tf_op jit(solution)/shard_map/reduce-window
  41.2 3.1 %slice.30 = s32[32,128,128]{2,1,0:T(8,128)} slice(s32[32,256,128]{2,1,0:T(8,128)} %bitcast.37), slice={[0:32], [0:128], [0:128]} | slice | bytes 4194304 | tf_op jit(solution)/shard_map/slice | solution.py:284
  45.1 24.7 %collective-permute-done.1 = s32[32,32,128]{2,1,0:T(8,128)} collective-permute-done((s32[32,32,128]{2,1,0:T(8,128)}, s32[32,32,128]{2,1,0:T(8,128)}, u32[]{:S(2)}, u32[]{:S(2)}) %collective-permute-start.1) | collective-permute-done | bytes 524320 | tf_op jit(solution)/shard_map/ppermute | solution.py:205
  69.8 1.4 fusion.8
  71.3 1.8 pad_add_fusion
  73.0 2.2 all-to-all-done
  75.2 6.1 %all-to-all-start.1 = ((s32[32,160,128]{2,1,0:T(8,128)}), s32[32,160,128]{2,1,0:T(8,128)}, u32[]{:S(2)}, u32[]{:S(2)}) async-start(s32[32,160,128]{2,1,0:T(8,128)} %pad_add_fusion), calls=%async_computation.1 | async-start | bytes 5242880 | tf_op jit(solution)/shard_map/all_to_all | solution.py:286
  83.3 2.2 %rev.7 = s32[64,8,2,4]{3,2,1,0:T(2,128)} reverse(s32[64,8,2,4]{3,2,1,0:T(2,128)S(1)} %reshape.52), dimensions={2} | reverse | bytes 32768 | tf_op jit(solution)/shard_map/rev | solution.py:249
  85.6 1.6 sub.32
  87.2 1.6 sub.34
  88.8 6.1 %select_bitcast_fusion = (s32[4,8,2,64]{0,2,1,3:T(2,128)}, s32[64,8,2,4]{3,2,1,0:T(2,128)S(1)}) fusion(s32[64,8,2,4]{3,2,1,0:T(2,128)S(1)} %reshape.52, s32[64,8,2,4]{3,2,1,0:T(2,128)} %rev.7, pred[]{:T(512)S(6)} %eq.62, s32[64,8,2,4]{3,2,1,0:T(2,128)} %sub.32, s32[64,8,2,4]{3,2,1,0:T(2,128)} %sub.34), kind=kLoop, calls=%fused_computation.28 | loop fusion | flops 225280 | bytes 98305 | tf_op jit(solution)/shard_map/transpose | solution.py:250
  96.4 2.2 %rev.6 = s32[64,8,2,4]{3,2,1,0:T(2,128)} reverse(s32[64,8,2,4]{3,2,1,0:T(2,128)S(1)} %get-tuple-element.16), dimensions={2} | reverse | bytes 32768 | tf_op jit(solution)/shard_map/rev | solution.py:249
  98.6 2.1 select_bitcast_fusion.1
  103.1 1.5 expected_counts.1.expected_any
  105.9 34.9 %all-to-all-done.1 = s32[32,160,128]{2,1,0:T(8,128)} async-done(((s32[32,160,128]{2,1,0:T(8,128)}), s32[32,160,128]{2,1,0:T(8,128)}, u32[]{:S(2)}, u32[]{:S(2)}) %all-to-all-start.1) | async-done | bytes 2621472 | tf_op jit(solution)/shard_map/all_to_all | solution.py:286
  140.9 8.0 %shell_gradient.1 = f32[4096,128]{1,0:T(8,128)} custom-call(s32[4096]{0:T(1024)S(1)} %reshape_reshape.4.slot_ref, s32[5120,128]{1,0:T(8,128)} %bitcast.9.counts_ref, f32[4,1024]{1,0:T(4,128)S(1)} %get-tuple-element.9.bias_ref, f32[512,1024]{1,0:T(8,128)} %copy-done.1, bf16[6,256,256]{2,1,0:T(8,128)(2,1)S(1)} %copy-done), custom_call_target="tpu_custom_call" | custom-call | flops 805306368 | bytes 8388608 | tf_op jit(solution)/shard_map/shell_gradient/pallas_call | solution.py:300
  148.9 12.1 %all-to-all-start.2 = ((f32[256,16,128]{2,1,0:T(8,128)}), f32[256,16,128]{2,1,0:T(8,128)}, u32[]{:S(2)}, u32[]{:S(2)}) async-start(f32[256,16,128]{2,1,0:T(8,128)} %bitcast.35), calls=%async_computation.2 | async-start | bytes 4194304 | tf_op jit(solution)/shard_map/all_to_all | solution.py:314
  162.5 51.3 %all-to-all-done.2 = f32[256,16,128]{2,1,0:T(8,128)} async-done(((f32[256,16,128]{2,1,0:T(8,128)}), f32[256,16,128]{2,1,0:T(8,128)}, u32[]{:S(2)}, u32[]{:S(2)}) %all-to-all-start.2) | async-done | bytes 2097184 | tf_op jit(solution)/shard_map/all_to_all | solution.py:314
  213.8 6.1 %analysis.1 = (f32[2,512,512]{2,1,0:T(8,128)}, f32[2,512,512]{2,1,0:T(8,128)}) custom-call(s32[1]{0:T(128)} %bitcast.first_ref, f32[2]{0:T(128)S(1)} %pad_maximum_fusion.step_ref, f32[8,32,2,8,128]{4,3,2,1,0:T(8,128)} %bitcast.15.field_ref, f32[2,512,512]{2,1,0:T(8,128)} %white_ref.3, bf16[2,512,512]{2,1,0:T(8,128)(2,1)S(1)} %copy-done.2, ...), custom_call_target="tpu_custom_call" | custom-call | flops 1610612736 | bytes 12582912 | tf_op jit(solution)/shard_map/analysis/pallas_call | solution.py:320
  (35 shorter events, 12.0 us)
Async XLA Ops:
  5.9 69.3 %all-to-all-start = ((f32[256,16,128]{2,1,0:T(8,128)}), f32[256,16,128]{2,1,0:T(8,128)S(1)}, u32[]{:S(2)}, u32[]{:S(2)}) async-start(f32[256,16,128]{2,1,0:T(8,128)} %bitcast.34), calls=%async_computation | async-start | bytes 4194304 | tf_op jit(solution)/shard_map/all_to_all | solution.py:280
  21.6 7.5 %copy-start.5 = (s32[1,1,4096]{2,1,0:T(1,128)S(1)}, s32[1,1,4096]{2,1,0:T(1,128)}, u32[]{:S(2)}) copy-start(s32[1,1,4096]{2,1,0:T(1,128)} %param.12) | copy-start | bytes 49156
  24.1 21.0 %collective-permute-start.2 = (s32[32,32,128]{2,1,0:T(8,128)}, s32[32,32,128]{2,1,0:T(8,128)}, u32[]{:S(2)}, u32[]{:S(2)}) collective-permute-start(s32[32,32,128]{2,1,0:T(8,128)} %get-tuple-element.12), channel_id=1, source_target_pairs={{0,1},{1,2},{2,3},{3,0},{4,5},{5,6},{6,7},{7,4},{8,9},{9,10},{10,1... | collective-permute-start | bytes 1572872 | tf_op jit(solution)/shard_map/ppermute | solution.py:205
  25.5 44.3 %collective-permute-start.1 = (s32[32,32,128]{2,1,0:T(8,128)}, s32[32,32,128]{2,1,0:T(8,128)}, u32[]{:S(2)}, u32[]{:S(2)}) collective-permute-start(s32[32,32,128]{2,1,0:T(8,128)} %get-tuple-element.13), channel_id=1, source_target_pairs={{0,2},{1,3},{2,0},{3,1},{4,6},{5,7},{6,4},{7,5},{8,10},{9,11},{10,... | collective-permute-start | bytes 1572872 | tf_op jit(solution)/shard_map/ppermute | solution.py:205
  27.9 41.9 %collective-permute-start = (s32[32,32,128]{2,1,0:T(8,128)}, s32[32,32,128]{2,1,0:T(8,128)}, u32[]{:S(2)}, u32[]{:S(2)}) collective-permute-start(s32[32,32,128]{2,1,0:T(8,128)} %get-tuple-element.14), channel_id=1, source_target_pairs={{0,3},{1,0},{2,1},{3,2},{4,7},{5,4},{6,5},{7,6},{8,11},{9,8},{10,9... | collective-permute-start | bytes 1572872 | tf_op jit(solution)/shard_map/ppermute | solution.py:205
  44.4 26.9 %copy-start.4 = (s32[32,128,128]{2,1,0:T(8,128)S(1)}, s32[32,128,128]{2,1,0:T(8,128)}, u32[]{:S(2)}) copy-start(s32[32,128,128]{2,1,0:T(8,128)} %slice.30) | copy-start | bytes 6291460
  75.2 65.6 %all-to-all-start.1 = ((s32[32,160,128]{2,1,0:T(8,128)}), s32[32,160,128]{2,1,0:T(8,128)}, u32[]{:S(2)}, u32[]{:S(2)}) async-start(s32[32,160,128]{2,1,0:T(8,128)} %pad_add_fusion), calls=%async_computation.1 | async-start | bytes 5242880 | tf_op jit(solution)/shard_map/all_to_all | solution.py:286
  94.9 8.1 %copy-start = (bf16[6,256,256]{2,1,0:T(8,128)(2,1)S(1)}, bf16[6,256,256]{2,1,0:T(8,128)(2,1)}, u32[]{:S(2)}) copy-start(bf16[6,256,256]{2,1,0:T(8,128)(2,1)} %constant.120.clone.tables_ref) | copy-start | bytes 2359300
  104.6 1.3 copy-start.1
  148.9 12.2 %copy-start.6 = (s32[64]{0:T(128)S(1)}, s32[64]{0:T(128)}, u32[]{:S(2)}) copy-start(s32[64]{0:T(128)} %param.16) | copy-start | bytes 772
  148.9 64.9 %copy-start.2 = (bf16[2,512,512]{2,1,0:T(8,128)(2,1)S(1)}, bf16[2,512,512]{2,1,0:T(8,128)(2,1)}, u32[]{:S(2)}) copy-start(bf16[2,512,512]{2,1,0:T(8,128)(2,1)} %amplitude_ref.3) | copy-start | bytes 3145732
  148.9 64.9 %copy-start.3 = (bf16[2,512,512]{2,1,0:T(8,128)(2,1)S(1)}, bf16[2,512,512]{2,1,0:T(8,128)(2,1)}, u32[]{:S(2)}) copy-start(bf16[2,512,512]{2,1,0:T(8,128)(2,1)} %kick_ref.1) | copy-start | bytes 3145732
  148.9 64.9 %all-to-all-start.2 = ((f32[256,16,128]{2,1,0:T(8,128)}), f32[256,16,128]{2,1,0:T(8,128)}, u32[]{:S(2)}, u32[]{:S(2)}) async-start(f32[256,16,128]{2,1,0:T(8,128)} %bitcast.35), calls=%async_computation.2 | async-start | bytes 4194304 | tf_op jit(solution)/shard_map/all_to_all | solution.py:314
